TPU v7x, 512 devices: a whole 4x8x8 slice. The times are simulated.
512 devices in a mesh: tok: 64 (over y_hi, z, x), head: 8 (over y_lo, core).
Axes of the slice: x: 4, y: 8 (y_hi: 2, y_lo: 4; y = y_hi * 4 + y_lo), z: 8, core: 2. Of those that a mesh axis runs over, the one named last changes fastest.
Arguments:
- text_queries: bfloat16 [256, 8192], P('tok', 'head'), may hold values from -6 to 6
- text_grads: bfloat16 [256, 8192], P('tok', 'head'), may hold values from -6 to 6
- vision_keys: bfloat16 [32768, 1024], P('tok', 'head'), may hold values from -6 to 6
- video_value_rows: bfloat16 [32768, 1024], P('tok', 'head'), may hold values from -6 to 6
- vision: bfloat16 [32768, 4096], P('tok'), may hold values from -16 to 16
- lengths: int32 [8], replicated, may hold values from 16 to 48, as said below
- frame_range: int32 [8, 2], replicated, may hold values from 0 to 256, as said below
Outputs:
- query_grad: bfloat16 [256, 8192], P(None, 'head')
- key_weight_grad: float32 [4096, 1024], P('tok', 'head')
- value_weight_grad: float32 [4096, 1024], P('tok', 'head')
Inputs may be any that keep to these rules, and one draw needn't show every extreme that they name: Each segment holds at least one row; the lengths sum to 256. `frame_range`: each segment's range covers 256 // 4 frames or more, first entry below the second.
All inputs are finite; a program needn't handle non-finite values.
Results may differ from a plain program's by a relative error of at most 0.0073.
Values may be sent and summed in bfloat16 or wider, within the bound.
No kernel may reach another device: no remote copies, remote signals or barrier semaphores. Data moves between devices by JAX's collectives and lax.ppermute only.
A program may use at most 64 MiB of HBM per device.

v0:
```python
import jax
import jax.numpy as jnp
from jax import lax
from jax.sharding import Mesh
from jax.sharding import PartitionSpec as P

HEAD_WIDTH = 128
FRAME_DEV = 4
TOK = ("tok_0", "tok_1", "tok_2")


NEG_FILL = -1e30


def side_by_side(arrays, axis, dim, along):
    ends, at = ([], 0)
    for a in arrays[:-1]:
        at += a.shape[along]
        ends.append(at)
    both = jnp.concatenate(arrays, axis=along)
    return tuple(jnp.split(lax.all_gather(both, axis, axis=dim, tiled=True), ends, axis=along))


def all_in_one(x, axis):
    leaves = jax.tree.leaves(x)
    order = sorted(range(len(leaves)), key=lambda k: -leaves[k].size)
    width = (1, *leaves[order[0]].shape)[-1]
    lines = [
        jnp.pad(leaves[k].reshape(-1), (0, -leaves[k].size % width)).reshape(-1, width)
        for k in order
    ]
    both, at, found = (lax.all_gather(jnp.concatenate(lines), axis), 0, {})
    for k, line in zip(order, lines):
        section = both[:, at : at + len(line)].reshape(len(both), -1)
        found[k] = section[:, : leaves[k].size].reshape(-1, *leaves[k].shape)
        at += len(line)
    numbers = iter(range(len(leaves)))
    return jax.tree.map(lambda _: found[next(numbers)], x)


def joined_all(x, axes, combine):
    for axis in axes:
        pieces = all_in_one(x, axis)
        x = jax.tree.map(lambda part: part[0], pieces)
        for k in range(1, lax.axis_size(axis)):
            x = combine(x, jax.tree.map(lambda part: part[k], pieces))
    return x


def in_blocks(x, dim, peers):
    before, after = (x.shape[:dim], x.shape[dim + 1 :])
    return jnp.moveaxis(x.reshape(*before, peers, -1, *after), dim, 0)


def sum_at_owner(x, axis, dim):
    peers = lax.axis_size(axis)
    blocks = lax.all_to_all(in_blocks(x, dim, peers), axis, 0, 0, tiled=True)
    return jnp.sum(blocks, axis=0)


def padded_to(lines, peers):
    spare = -len(lines) % peers
    return jnp.pad(lines, [(0, spare)] + [(0, 0)] * (lines.ndim - 1))


def from_everyone(x, axis):
    peers = lax.axis_size(axis)
    return lax.all_to_all(jnp.broadcast_to(x[None], (peers, *x.shape)), axis, 0, 0, tiled=True)


def joined_along(blocks, dim):
    blocks = jnp.moveaxis(blocks, 0, dim)
    shape = blocks.shape
    return blocks.reshape(*shape[:dim], shape[dim] * shape[dim + 1], *shape[dim + 2 :])


def gathered_copies(x, axis, dim):
    blocks = from_everyone(x, axis)
    return joined_along(blocks, dim)


def nested_sum(x, axes):
    lines = x.reshape(-1, x.shape[-1])
    own = sum_at_owner(padded_to(lines, lax.axis_size(axes)), axes, 0)
    whole = gathered_copies(own, axes, 0)
    return whole[: len(lines)].reshape(x.shape)


def sum_by_axis(x, axes, dim):
    far, near = axes
    own = sum_at_owner(in_blocks(x, dim, lax.axis_size(far)), near, dim + 1)
    return jnp.sum(lax.all_to_all(own, far, 0, 0, tiled=True), axis=0)


def merge_stats(earlier, second):
    first_max, first_sum, first_dot = earlier
    second_max, second_sum, second_dot = second
    joint_max = jnp.maximum(first_max, second_max)
    first_scale = jnp.exp(first_max - joint_max)
    second_scale = jnp.exp(second_max - joint_max)
    return (
        joint_max,
        first_sum * first_scale + second_sum * second_scale,
        first_dot * first_scale + second_dot * second_scale,
    )


def shards(text_queries, text_grads, vision_keys, video_value_rows, vision, lengths, frame_range):
    text_q, text_g = side_by_side((text_queries, text_grads), TOK, 0, 1)
    text_len = text_q.shape[0]
    kv_rows = vision_keys.shape[0]
    kv_local = vision_keys.shape[1] // HEAD_WIDTH
    group_width = text_q.shape[1] // vision_keys.shape[1]
    score_scale = HEAD_WIDTH ** (-0.5)
    row_ids = jnp.arange(text_len, dtype=jnp.int32)
    segment_ends = jnp.cumsum(lengths)
    segment = jnp.sum((row_ids[:, None] >= segment_ends[None, :]).astype(jnp.int32), axis=1)
    segment_pick = (
        segment[:, None] == jnp.arange(lengths.shape[0], dtype=jnp.int32)[None, :]
    ).astype(jnp.int32)
    first_frame = jnp.sum(segment_pick * frame_range[None, :, 0], axis=1)
    end_frame = jnp.sum(segment_pick * frame_range[None, :, 1], axis=1)
    key_ids = lax.axis_index(TOK) * kv_rows + jnp.arange(kv_rows, dtype=jnp.int32)
    frames = key_ids // (kv_rows // FRAME_DEV)
    allowed = (frames[None, :] >= first_frame[:, None]) & (frames[None, :] < end_frame[:, None])
    query_member = text_q.reshape(text_len, kv_local, group_width, HEAD_WIDTH).transpose(2, 0, 1, 3)
    grad_member = text_g.reshape(text_len, kv_local, group_width, HEAD_WIDTH).transpose(2, 0, 1, 3)
    key_three = vision_keys.reshape(kv_rows, kv_local, HEAD_WIDTH)
    value_three = video_value_rows.reshape(kv_rows, kv_local, HEAD_WIDTH)

    def scores_of(query_one, grad_one):
        scores = (
            jnp.einsum("ihd,jhd->hij", query_one, key_three, preferred_element_type=jnp.float32)
            * score_scale
        )
        dprobs = jnp.einsum(
            "ihd,jhd->hij", grad_one, value_three, preferred_element_type=jnp.float32
        )
        return (scores, dprobs)

    def local_stats(carry, member):
        scores, dprobs = scores_of(member[0], member[1])
        local_max = jnp.max(jnp.where(allowed, scores, NEG_FILL), axis=2)
        local_exp = jnp.where(allowed, jnp.exp(scores - local_max[..., None]), 0.0)
        return (carry, (local_max, jnp.sum(local_exp, axis=2), jnp.sum(local_exp * dprobs, axis=2)))

    unused, (local_max, local_sum, local_dot) = lax.scan(
        local_stats, jnp.zeros((), jnp.float32), (query_member, grad_member)
    )
    row_max, row_sum, row_dot = joined_all((local_max, local_sum, local_dot), TOK, merge_stats)

    def member_grads(running, member):
        query_one, grad_one, max_one, sum_one, dot_one = member
        scores, dprobs = scores_of(query_one, grad_one)
        exp_terms = jnp.where(allowed, jnp.exp(scores - max_one[..., None]), 0.0)
        attn_probs = exp_terms / sum_one[..., None]
        row_delta = dot_one / sum_one
        dscore = (attn_probs * (dprobs - row_delta[..., None])).astype(jnp.bfloat16)
        value_sum = running[1] + jnp.einsum(
            "hij,ihd->jhd",
            attn_probs.astype(jnp.bfloat16),
            grad_one,
            preferred_element_type=jnp.float32,
        )
        key_sum = running[0] + jnp.einsum(
            "hij,ihd->jhd", dscore, query_one, preferred_element_type=jnp.float32
        )
        query_part = score_scale * jnp.einsum(
            "hij,jhd->ihd", dscore, key_three, preferred_element_type=jnp.float32
        )
        return ((key_sum, value_sum), query_part)

    zero_acc = jnp.zeros((kv_rows, kv_local, HEAD_WIDTH), jnp.float32)
    (key_sum, value_sum), query_parts = lax.scan(
        member_grads, (zero_acc, zero_acc), (query_member, grad_member, row_max, row_sum, row_dot)
    )
    key_grad = (score_scale * key_sum).astype(jnp.bfloat16)
    value_grad = value_sum.astype(jnp.bfloat16)
    query_part = query_parts.transpose(1, 2, 0, 3).reshape(text_len, -1)
    query_grad = nested_sum(query_part, TOK).astype(jnp.bfloat16)
    kv_data = jnp.concatenate(
        (key_grad.reshape(kv_rows, -1), value_grad.reshape(kv_rows, -1)), axis=1
    )
    half_width = kv_data.shape[1] // 2
    weight_grads = sum_by_axis(
        jnp.einsum("tf,tc->fc", vision, kv_data, preferred_element_type=jnp.float32),
        (("tok_0", "tok_1"), "tok_2"),
        0,
    )
    return (query_grad, weight_grads[:, :half_width], weight_grads[:, half_width:])


def solution(mesh):
    finer = Mesh(
        mesh.devices.reshape(2, 8, 4, mesh.shape["head"]), ("tok_0", "tok_1", "tok_2", "head")
    )
    return jax.shard_map(
        shards,
        mesh=finer,
        in_specs=(
            P(TOK, "head"),
            P(TOK, "head"),
            P(TOK, "head"),
            P(TOK, "head"),
            P(TOK, None),
            P(),
            P(),
        ),
        out_specs=(P(None, "head"), P(TOK, "head"), P(TOK, "head")),
        check_vma=False,
    )
```

profile of v0, /device:TPU:64, one launch (start us, length us, event | category | flops | bytes accessed | tf_op | source)
XLA Modules:
  0.0 352.2 jit_solution(468170734512573459)
XLA Ops:
  7.2 1.3 maximum_bitcast_fusion
  8.6 0.8 reduce-window.8
  9.6 0.8 slice_bitcast_fusion.43
  10.4 133.0 %all-gather.6.cloned.1.call-done = bf16[64,4,2048]{2,1,0:T(4,128)(2,1)} async-done(((bf16[1,4,2048]{2,1,0:T(4,128)(2,1)}), bf16[64,4,2048]{2,1,0:T(4,128)(2,1)}) %all-gather.6.cloned.1.call-update) | async-done | bytes 1048592 | tf_op jit(solution)/shard_map/all_gather | solution.py:21
  143.5 1.3 reshape.886
  145.1 0.3 copy.46
  145.6 0.3 copy.47
  145.9 9.0 %while.30 = (s32[]{:T(128)}, f32[8,1,256]{2,0,1:T(8,128)S(1)}, f32[8,1,256]{2,0,1:T(8,128)S(1)}, f32[8,1,256]{2,0,1:T(8,128)S(1)}, bf16[8,256,1,128]{3,1,2,0:T(8...) while((s32[]{:T(128)}, f32[8,1,256]{2,0,1:T(8,128)S(1)}, ...), condition=%wide.region_8.9_spmd.clone, body=%wide.region_4.8_spmd.clone.sunk | while | flops 69598464 | bytes 1989785 | solution.py:147
  145.9 0.3 select_reduce_fusion.4
  146.2 0.3 fusion.156
  146.6 0.3 fusion.155
  147.0 0.3 select_reduce_fusion.4
  147.4 0.3 fusion.156
  147.7 0.3 fusion.155
  148.1 0.3 select_reduce_fusion.4
  148.5 0.3 fusion.156
  148.8 0.3 fusion.155
  149.3 0.3 select_reduce_fusion.4
  149.6 0.3 fusion.156
  149.9 0.3 fusion.155
  150.4 0.3 select_reduce_fusion.4
  150.7 0.3 fusion.156
  151.1 0.3 fusion.155
  151.5 0.3 select_reduce_fusion.4
  151.8 0.3 fusion.156
  152.2 0.3 fusion.155
  152.6 0.3 select_reduce_fusion.4
  153.0 0.3 fusion.156
  153.3 0.3 fusion.155
  153.7 0.3 select_reduce_fusion.4
  154.1 0.3 fusion.156
  154.4 0.3 fusion.155
  154.9 8.4 %all-gather = f32[48,256]{1,0:T(8,128)S(1)} all-gather(f32[24,256]{1,0:T(8,128)S(1)} %pad_maximum_fusion), channel_id=2, replica_groups=mesh['tok_0'=2,'tok_1'=8,'tok_2'=4,'head'=8] {'tok_0'}, dimensions={0}, use_global_device_ids=true | all-gather | bytes 73728 | tf_op jit(solution)/shard_map/all_gather | solution.py:32
  163.3 24.8 %all-gather.1 = f32[192,256]{1,0:T(8,128)S(1)} all-gather(f32[24,256]{1,0:T(8,128)S(1)} %pad_maximum_fusion.1), channel_id=3, replica_groups=mesh['tok_0'=2,'tok_1'=8,'tok_2'=4,'head'=8] {'tok_1'}, dimensions={0}, use_global_device_ids=true | all-gather | bytes 221184 | tf_op jit(solution)/shard_map/all_gather | solution.py:32
  188.2 12.2 %all-gather.2 = f32[96,256]{1,0:T(8,128)S(1)} all-gather(f32[24,256]{1,0:T(8,128)S(1)} %pad_maximum_fusion.2), channel_id=4, replica_groups=mesh['tok_0'=2,'tok_1'=8,'tok_2'=4,'head'=8] {'tok_2'}, dimensions={0}, use_global_device_ids=true | all-gather | bytes 122880 | tf_op jit(solution)/shard_map/all_gather | solution.py:32
  200.5 10.8 %while.31 = (s32[]{:T(128)}, f32[512,1,128]{0,2,1:T(8,128)S(1)}, f32[512,1,128]{0,2,1:T(8,128)S(1)}, f32[8,256,1,128]{3,1,2,0:T(8,128)S(1)}, bf16[8,256,1,128]{3...) while((s32[]{:T(128)}, f32[512,1,128]{0,2,1:T(8,128)S(1)}, ...), condition=%wide.region_10.11_spmd.clone, body=%wide.region_9.10_spmd.clone.sunk | while | flops 169509120 | bytes 4210884 | solution.py:174
  200.6 0.3 fusion.167
  201.2 0.2 fusion.170
  201.9 0.3 fusion.167
  202.5 0.2 fusion.170
  203.3 0.3 fusion.167
  204.6 0.3 fusion.167
  206.0 0.3 fusion.167
  207.3 0.3 fusion.167
  208.7 0.3 fusion.167
  209.2 0.2 fusion.170
  210.0 0.3 fusion.167
  211.3 0.6 copy.52
  211.9 1.4 reshape.879
  213.3 7.8 %all-to-all-start = ((f32[64,4,1024]{2,1,0:T(4,128)}), f32[64,4,1024]{2,1,0:T(4,128)S(1)}, u32[]{:S(2)}, u32[]{:S(2)}) async-start(f32[64,4,1024]{2,1,0:T(4,128)} %reshape.879), calls=%async_computation | async-start | bytes 2097152 | tf_op jit(solution)/shard_map/all_to_all | solution.py:57
  221.2 5.4 %convolution_bitcast_fusion.2 = f32[4096,256]{0,1:T(8,128)} fusion(bf16[512,4096]{1,0:T(8,128)(2,1)} %param.15, bf16[512,128]{0,1:T(8,128)(2,1)S(1)} %get-tuple-element.369, bf16[512,128]{0,1:T(8,128)(2,1)S(1)} %get-tuple-element.368), kind=kOutput, calls=%fused_computation.51 | convolution fusion | flops 1074266112 | bytes 8650752 | tf_op jit(solution)/shard_map/tf,tc->fc/dot_general | solution.py:186
  226.6 5.6 %copy.53 = f32[4096,256]{1,0:T(8,128)} copy(f32[4096,256]{0,1:T(8,128)} %convolution_bitcast_fusion.2) | data formatting | bytes 8388608 | tf_op jit(solution)/shard_map/tf,tc->fc/dot_general | solution.py:186
  232.2 4.6 %copy.54 = f32[4,16,64,256]{3,2,1,0:T(8,128)} copy(f32[4,16,64,256]{3,2,0,1:T(8,128)} %bitcast.603) | data formatting | bytes 8388608 | tf_op jit(solution)/shard_map/transpose | solution.py:52
  236.8 3.0 all-to-all-done
  239.8 4.8 %all-to-all-start.2 = ((f32[4,16,64,256]{3,2,1,0:T(8,128)}), f32[4,16,64,256]{3,2,1,0:T(8,128)}, u32[]{:S(2)}, u32[]{:S(2)}) async-start(f32[4,16,64,256]{3,2,1,0:T(8,128)} %copy.54), calls=%async_computation.2 | async-start | bytes 8388608 | tf_op jit(solution)/shard_map/all_to_all | solution.py:57
  244.8 35.5 %all-to-all-done.2 = f32[4,16,64,256]{3,2,1,0:T(8,128)} async-done(((f32[4,16,64,256]{3,2,1,0:T(8,128)}), f32[4,16,64,256]{3,2,1,0:T(8,128)}, u32[]{:S(2)}, u32[]{:S(2)}) %all-to-all-start.2) | async-done | bytes 4194336 | tf_op jit(solution)/shard_map/all_to_all | solution.py:57
  280.3 0.9 broadcast_in_dim.54
  281.2 11.3 %all-to-all-start.1 = ((bf16[64,4,1024]{2,1,0:T(4,128)(2,1)}), bf16[64,4,1024]{2,1,0:T(4,128)(2,1)S(1)}, u32[]{:S(2)}, u32[]{:S(2)}) async-start(bf16[64,4,1024]{2,1,0:T(4,128)(2,1)} %broadcast_in_dim.54), calls=%async_computation.1 | async-start | bytes 1048576 | tf_op jit(solution)/shard_map/all_to_all | solution.py:68
  292.5 3.6 %reduce_sum.76 = f32[16,64,256]{2,1,0:T(8,128)} reduce(f32[4,16,64,256]{3,2,1,0:T(8,128)} %all-to-all-done.2, f32[]{:T(128)} %constant.75.clone.1), dimensions={0}, to_apply=%region_12.13 | reduce | flops 786432 | bytes 5242884 | tf_op jit(solution)/shard_map/reduce_sum | solution.py:58
  296.1 13.4 %all-to-all-done.1 = bf16[64,4,1024]{2,1,0:T(4,128)(2,1)S(1)} async-done(((bf16[64,4,1024]{2,1,0:T(4,128)(2,1)}), bf16[64,4,1024]{2,1,0:T(4,128)(2,1)S(1)}, u32[]{:S(2)}, u32[]{:S(2)}) %all-to-all-start.1) | async-done | bytes 524320 | tf_op jit(solution)/shard_map/all_to_all | solution.py:68
  309.5 15.8 %all-to-all-start.3 = ((f32[16,64,256]{2,1,0:T(8,128)}), f32[16,64,256]{2,1,0:T(8,128)S(1)}, u32[]{:S(2)}, u32[]{:S(2)}) async-start(f32[16,64,256]{2,1,0:T(8,128)} %reduce_sum.76), calls=%async_computation.3 | async-start | bytes 2097152 | tf_op jit(solution)/shard_map/all_to_all | solution.py:92
  325.3 0.9 convert_element_type.26
  326.2 18.5 %all-to-all-done.3 = f32[16,64,256]{2,1,0:T(8,128)S(1)} async-done(((f32[16,64,256]{2,1,0:T(8,128)}), f32[16,64,256]{2,1,0:T(8,128)S(1)}, u32[]{:S(2)}, u32[]{:S(2)}) %all-to-all-start.3) | async-done | bytes 1048608 | tf_op jit(solution)/shard_map/all_to_all | solution.py:92
  344.8 0.6 fusion.130
  (109 shorter events, 9.0 us)
Async XLA Ops:
  7.2 136.3 %all-gather.6.cloned.1.call-start = ((), (), s32[]{:S(2)}) async-start(), calls=%async_computation.4 | async-start | bytes 1064960 | tf_op jit(solution)/shard_map/all_gather | solution.py:21
  10.4 135.5 %copy-start = (bf16[512,128]{1,0:T(8,128)(2,1)S(1)}, bf16[512,128]{1,0:T(8,128)(2,1)}, u32[]{:S(2)}) copy-start(bf16[512,128]{1,0:T(8,128)(2,1)} %param.13) | copy-start | bytes 393220
  10.4 135.5 %copy-start.1 = (bf16[512,128]{1,0:T(8,128)(2,1)S(1)}, bf16[512,128]{1,0:T(8,128)(2,1)}, u32[]{:S(2)}) copy-start(bf16[512,128]{1,0:T(8,128)(2,1)} %param.14) | copy-start | bytes 393220
  145.9 54.6 %copy-start.2 = (f32[8,256,1,128]{3,1,2,0:T(8,128)S(1)}, f32[8,256,1,128]{3,1,2,0:T(8,128)}, u32[]{:S(2)}) copy-start(f32[8,256,1,128]{3,1,2,0:T(8,128)} %custom-call.5) | copy-start | bytes 3145732
  213.3 26.4 %all-to-all-start = ((f32[64,4,1024]{2,1,0:T(4,128)}), f32[64,4,1024]{2,1,0:T(4,128)S(1)}, u32[]{:S(2)}, u32[]{:S(2)}) async-start(f32[64,4,1024]{2,1,0:T(4,128)} %reshape.879), calls=%async_computation | async-start | bytes 2097152 | tf_op jit(solution)/shard_map/all_to_all | solution.py:57
  239.8 40.5 %all-to-all-start.2 = ((f32[4,16,64,256]{3,2,1,0:T(8,128)}), f32[4,16,64,256]{3,2,1,0:T(8,128)}, u32[]{:S(2)}, u32[]{:S(2)}) async-start(f32[4,16,64,256]{3,2,1,0:T(8,128)} %copy.54), calls=%async_computation.2 | async-start | bytes 8388608 | tf_op jit(solution)/shard_map/all_to_all | solution.py:57
  281.2 28.3 %all-to-all-start.1 = ((bf16[64,4,1024]{2,1,0:T(4,128)(2,1)}), bf16[64,4,1024]{2,1,0:T(4,128)(2,1)S(1)}, u32[]{:S(2)}, u32[]{:S(2)}) async-start(bf16[64,4,1024]{2,1,0:T(4,128)(2,1)} %broadcast_in_dim.54), calls=%async_computation.1 | async-start | bytes 1048576 | tf_op jit(solution)/shard_map/all_to_all | solution.py:68
  309.5 35.2 %all-to-all-start.3 = ((f32[16,64,256]{2,1,0:T(8,128)}), f32[16,64,256]{2,1,0:T(8,128)S(1)}, u32[]{:S(2)}, u32[]{:S(2)}) async-start(f32[16,64,256]{2,1,0:T(8,128)} %reduce_sum.76), calls=%async_computation.3 | async-start | bytes 2097152 | tf_op jit(solution)/shard_map/all_to_all | solution.py:92
Sparse Core Ops, SparseCore 0:
  13.1 130.3 all-gather.5
where the time goes:
time: 353 us; the launch traced here: 352 us
  waiting for transfers between devices  203 us (58%)
  blocking collectives  45.5 us (13%)
  starting transfers between devices  39.8 us (11%)
  matrix products  20.8 us (6%)
  local copies, waits for them, and re-layouts  19 us (5%)
  between operations  14.3 us (4%)
  other arithmetic  8.75 us (2%)
    all_gather x1, waiting for transfers between devices, side_by_side(): lax.all_gather(both, axis, axis=dim, tiled=True)  133 us
    all_gather x3, blocking collectives, all_in_one(): both, at, found = (lax.all_gather(jnp.concatenate(lines), axis), 0, {})  45.5 us
    all_to_all x2, waiting for transfers between devices, sum_at_owner(): blocks = lax.all_to_all(in_blocks(x, dim, peers), axis, 0, 0, tiled=True)  38.5 us
    all_to_all x1, waiting for transfers between devices, sum_by_axis(): return jnp.sum(lax.all_to_all(own, far, 0, 0, tiled=True), axis=0)  18.5 us
    all_to_all x1, starting transfers between devices, sum_by_axis(): return jnp.sum(lax.all_to_all(own, far, 0, 0, tiled=True), axis=0)  15.8 us
    all_to_all x1, waiting for transfers between devices, from_everyone(): lax.all_to_all(jnp.broadcast_to(x[None], (peers, *x.shape)), axis, 0, 0,...  13.4 us
    all_to_all x2, starting transfers between devices, sum_at_owner(): blocks = lax.all_to_all(in_blocks(x, dim, peers), axis, 0, 0, tiled=True)  12.6 us
    all_to_all x1, starting transfers between devices, from_everyone(): lax.all_to_all(jnp.broadcast_to(x[None], (peers, *x.shape)), axis, 0, 0,...  11.3 us
  transfers between devices with their start and end apart: 5, of which 5 were waited for; matrix products, arithmetic and copies ran while one was open for 6% of the time, Pallas kernels for 0%

commit v1 on v0

v1 whole, which is shorter than its diff:
```python
import jax
import jax.numpy as jnp
from jax import lax
from jax.experimental import pallas as pl
from jax.experimental.pallas import tpu as pltpu
from jax.sharding import Mesh
from jax.sharding import PartitionSpec as P

HEAD_WIDTH = 128
FRAME_DEV = 4
TOK = ("tok_0", "tok_1", "tok_2")
CHUNK = 256
SCALE = HEAD_WIDTH**-0.5
LOG2E = 1.4426950408889634
OFF = 1e30
LOW = -1e29
F32 = jnp.float32
BF16 = jnp.bfloat16
NT = (((1,), (1,)), ((), ()))
NN = (((1,), (0,)), ((), ()))
PARAMS = pltpu.CompilerParams(vmem_limit_bytes=48 * 2**20)


def from_everyone(x, axis):
    peers = lax.axis_size(axis)
    return lax.all_to_all(jnp.broadcast_to(x[None], (peers, *x.shape)), axis, 0, 0, tiled=True)


def dot(a, b, dims):
    return lax.dot_general(a, b, dims, preferred_element_type=F32)


def chunk_of(text_ref, c, which):
    per = CHUNK // text_ref.shape[2]
    return text_ref[c * per : (c + 1) * per, which].reshape(CHUNK, HEAD_WIDTH)


def stats_kernel(text_ref, k_ref, v_ref, off_ref, out_ref):
    chunks = out_ref.shape[0] // 3
    frames = off_ref.shape[1]
    rows = k_ref.shape[0] // frames
    for c in range(chunks):
        scores = dot(k_ref[...], chunk_of(text_ref, c, 0), NT) * (SCALE * LOG2E)
        dprobs = dot(v_ref[...], chunk_of(text_ref, c, 1), NT)
        top = jnp.full((1, CHUNK), LOW, F32)
        for f in range(frames):
            high = jnp.max(scores[f * rows : (f + 1) * rows], axis=0, keepdims=True)
            top = jnp.maximum(top, high - off_ref[c, f : f + 1, :])
        total = jnp.zeros((1, CHUNK), F32)
        weighted = jnp.zeros((1, CHUNK), F32)
        for f in range(frames):
            here = slice(f * rows, (f + 1) * rows)
            terms = jnp.exp2(scores[here] - (top + off_ref[c, f : f + 1, :]))
            total += jnp.sum(terms, axis=0, keepdims=True)
            weighted += jnp.sum(terms * dprobs[here], axis=0, keepdims=True)
        out_ref[c : c + 1, :] = top
        out_ref[chunks + c : chunks + c + 1, :] = total
        out_ref[2 * chunks + c : 2 * chunks + c + 1, :] = weighted


def joined(stats_ref):
    peers, lines = stats_ref.shape[0], stats_ref.shape[1] // 3
    top = stats_ref[0, :lines]
    for k in range(1, peers):
        top = jnp.maximum(top, stats_ref[k, :lines])
    total = jnp.zeros_like(top)
    weighted = jnp.zeros_like(top)
    for k in range(peers):
        factor = jnp.exp2(stats_ref[k, :lines] - top)
        total += stats_ref[k, lines : 2 * lines] * factor
        weighted += stats_ref[k, 2 * lines :] * factor
    return top, total, weighted


def join_kernel(stats_ref, out_ref):
    lines = out_ref.shape[0] // 3
    for k, part in enumerate(joined(stats_ref)):
        out_ref[k * lines : (k + 1) * lines] = part


def grads_kernel(text_ref, k_ref, v_ref, off_ref, stats_ref, kv_ref, dq_ref, p_scr, ds_scr):
    top, total, weighted = joined(stats_ref)
    shift = top + jnp.log2(total)
    delta = weighted / total
    frames = off_ref.shape[1]
    rows = k_ref.shape[0] // frames
    per = CHUNK // dq_ref.shape[1]
    k_all = k_ref[...]
    k_t = k_all.T
    key_sum = jnp.zeros(k_ref.shape, F32)
    value_sum = jnp.zeros(v_ref.shape, F32)
    for c in range(top.shape[0]):
        q_c = chunk_of(text_ref, c, 0)
        g_c = chunk_of(text_ref, c, 1)
        scores = dot(k_all, q_c, NT) * (SCALE * LOG2E)
        dprobs = dot(v_ref[...], g_c, NT)
        for f in range(frames):
            here = slice(f * rows, (f + 1) * rows)
            probs = jnp.exp2(scores[here] - (shift[c : c + 1] + off_ref[c, f : f + 1, :]))
            p_scr[here] = probs.astype(BF16)
            ds_scr[here] = (probs * (dprobs[here] - delta[c : c + 1])).astype(BF16)
        p_c = p_scr[...]
        ds_c = ds_scr[...]
        value_sum += dot(p_c, g_c, NN)
        key_sum += dot(ds_c, q_c, NN)
        dq = (dot(k_t, ds_c, NN) * SCALE).T
        dq_ref[c * per : (c + 1) * per] = dq.reshape(per, dq_ref.shape[1], HEAD_WIDTH)
    kv_ref[:, :HEAD_WIDTH] = (key_sum * SCALE).astype(BF16)
    kv_ref[:, HEAD_WIDTH:] = value_sum.astype(BF16)


def weight_kernel(vision_ref, kv_ref, out_ref):
    out_ref[...] = dot(vision_ref[...], kv_ref[...], NN).astype(BF16)


def offsets(lengths, frame_range, rows, first, frames):
    part_ids = jnp.arange(lengths.shape[0], dtype=jnp.int32)
    ends = jnp.sum(jnp.where(part_ids[None, :] <= part_ids[:, None], lengths[None, :], 0), axis=1)
    segment = jnp.sum((rows[:, None] >= ends[None, :]).astype(jnp.int32), axis=1)
    pick = (segment[:, None] == part_ids[None, :]).astype(jnp.int32)
    begin = jnp.sum(pick * frame_range[None, :, 0], axis=1)
    end = jnp.sum(pick * frame_range[None, :, 1], axis=1)
    at = first + jnp.arange(frames, dtype=jnp.int32)
    allowed = (at[:, None] >= begin[None, :]) & (at[:, None] < end[None, :])
    off = jnp.where(allowed, 0.0, OFF).astype(F32)
    return off.reshape(frames, -1, CHUNK).transpose(1, 0, 2)


def shards(text_queries, text_grads, vision_keys, video_value_rows, vision, lengths, frame_range):
    peers = lax.axis_size(TOK)
    own_rows = text_queries.shape[0]
    members = text_queries.shape[1] // HEAD_WIDTH
    lines = own_rows * members
    kv_rows = vision_keys.shape[0]
    features = vision.shape[1]
    far = lax.axis_size("tok_0") * lax.axis_size("tok_1")
    near = lax.axis_size("tok_2")

    own_text = jnp.stack(
        (text_queries.reshape(lines, HEAD_WIDTH), text_grads.reshape(lines, HEAD_WIDTH))
    )
    text = from_everyone(own_text, TOK)
    text = text.reshape(peers, 2, lines, HEAD_WIDTH)

    row_of = jnp.arange(peers * lines, dtype=jnp.int32) // members
    off = offsets(lengths, frame_range, row_of, lax.axis_index(TOK) * FRAME_DEV, FRAME_DEV)
    vision_t = (
        vision.reshape(kv_rows, far, near, features // peers)
        .transpose(2, 1, 3, 0)
        .reshape(features, kv_rows)
    )

    chunks = peers * lines // CHUNK
    whole = pl.BlockSpec(memory_space=pltpu.VMEM)
    stats = pl.pallas_call(
        stats_kernel,
        out_shape=jax.ShapeDtypeStruct((3 * chunks, CHUNK), F32),
        in_specs=[whole] * 4,
        out_specs=whole,
        compiler_params=PARAMS,
    )(text, vision_keys, video_value_rows, off)

    stats = from_everyone(stats, ("tok_0", "tok_2"))
    stats = pl.pallas_call(
        join_kernel,
        out_shape=jax.ShapeDtypeStruct((3 * chunks, CHUNK), F32),
        in_specs=[whole],
        out_specs=whole,
        compiler_params=PARAMS,
    )(stats.reshape(-1, 3 * chunks, CHUNK))
    stats = from_everyone(stats, "tok_1").reshape(-1, 3 * chunks, CHUNK)

    kv_data, dq = pl.pallas_call(
        grads_kernel,
        out_shape=(
            jax.ShapeDtypeStruct((kv_rows, 2 * HEAD_WIDTH), BF16),
            jax.ShapeDtypeStruct((peers, lines, HEAD_WIDTH), F32),
        ),
        in_specs=[whole] * 5,
        out_specs=(whole, whole),
        scratch_shapes=[
            pltpu.VMEM((kv_rows, CHUNK), BF16),
            pltpu.VMEM((kv_rows, CHUNK), BF16),
        ],
        compiler_params=PARAMS,
    )(text, vision_keys, video_value_rows, off, stats)

    blocks = 8
    part = pl.pallas_call(
        weight_kernel,
        out_shape=jax.ShapeDtypeStruct((features, 2 * HEAD_WIDTH), BF16),
        grid=(blocks,),
        in_specs=[
            pl.BlockSpec((features // blocks, kv_rows), lambda i: (i, 0)),
            pl.BlockSpec((kv_rows, 2 * HEAD_WIDTH), lambda i: (0, 0)),
        ],
        out_specs=pl.BlockSpec((features // blocks, 2 * HEAD_WIDTH), lambda i: (i, 0)),
        compiler_params=PARAMS,
    )(vision_t, kv_data)

    got = lax.all_to_all(
        part.reshape(near, features // near, 2 * HEAD_WIDTH), "tok_2", 0, 0, tiled=True
    )
    part = jnp.sum(got.astype(F32), axis=0).astype(BF16)
    got = lax.all_to_all(
        part.reshape(far, features // peers, 2 * HEAD_WIDTH), ("tok_0", "tok_1"), 0, 0, tiled=True
    )
    weights = jnp.sum(got.astype(F32), axis=0)

    dq = jnp.sum(lax.all_to_all(dq, TOK, 0, 0, tiled=True), axis=0).astype(BF16)
    query_grad = from_everyone(dq.reshape(own_rows, -1), TOK).reshape(peers * own_rows, -1)
    return query_grad, weights[:, :HEAD_WIDTH], weights[:, HEAD_WIDTH:]


def solution(mesh):
    finer = Mesh(
        mesh.devices.reshape(2, 8, 4, mesh.shape["head"]), ("tok_0", "tok_1", "tok_2", "head")
    )
    return jax.shard_map(
        shards,
        mesh=finer,
        in_specs=(
            P(TOK, "head"),
            P(TOK, "head"),
            P(TOK, "head"),
            P(TOK, "head"),
            P(TOK, None),
            P(),
            P(),
        ),
        out_specs=(P(None, "head"), P(TOK, "head"), P(TOK, "head")),
        check_vma=False,
    )
```

time: 353 us -> 218 us (0.62)
  the two profiles are of different devices: /device:TPU:64 before, /device:TPU:14 now
where the time goes in v1:
time: 218 us; the launch traced here: 217 us
  waiting for transfers between devices  91.4 us (42%)
  starting transfers between devices  50.1 us (23%)
  blocking collectives  41.6 us (19%)
  local copies, waits for them, and re-layouts  19.6 us (9%)
  Pallas kernels  11.4 us (5%)
  other arithmetic  2.47 us (1%)
    all_to_all x3, waiting for transfers between devices, from_everyone(): lax.all_to_all(jnp.broadcast_to(x[None], (peers, *x.shape)), axis, 0, 0,...  48.8 us
    all_to_all x3, starting transfers between devices, from_everyone(): lax.all_to_all(jnp.broadcast_to(x[None], (peers, *x.shape)), axis, 0, 0,...  32.6 us
    all_to_all x1, blocking collectives, shards(): lax.all_to_all(part.reshape(near, features // near, 2 * HEAD_WIDTH), 'tok...  28.5 us
    all_to_all x1, waiting for transfers between devices, shards(): dq = jnp.sum(lax.all_to_all(dq, TOK, 0, 0, tiled=True), axis=0).astype(BF16)  27.2 us
    all_to_all x1, waiting for transfers between devices, shards(): lax.all_to_all(part.reshape(far, features // peers, 2 * HEAD_WIDTH), ('to...  15.3 us
    all_to_all x1, blocking collectives, from_everyone(): lax.all_to_all(jnp.broadcast_to(x[None], (peers, *x.shape)), axis, 0, 0,...  13.1 us
    all_to_all x1, starting transfers between devices, shards(): dq = jnp.sum(lax.all_to_all(dq, TOK, 0, 0, tiled=True), axis=0).astype(BF16)  10.2 us
    unnamed x9, local copies, waits for them, and re-layouts  8.36 us
  transfers between devices with their start and end apart: 5, of which 4 were waited for; matrix products, arithmetic and copies ran while one was open for 7% of the time, Pallas kernels for 0%

profile of v1, /device:TPU:14, one launch (start us, length us, event | category | flops | bytes accessed | tf_op | source)
XLA Modules:
  0.0 217.5 jit_solution(46354559364503029)
XLA Ops:
  0.6 0.7 stack_reshape.6
  1.3 0.7 stack_reshape.7
  2.1 1.2 broadcast_in_dim.28
  3.3 18.2 %all-to-all-start = ((bf16[64,2,32,128]{3,2,1,0:T(8,128)(2,1)}), bf16[64,2,32,128]{3,2,1,0:T(8,128)(2,1)S(1)}, u32[]{:S(2)}, u32[]{:S(2)}) async-start(bf16[64,2,32,128]{3,2,1,0:T(8,128)(2,1)} %broadcast_in_dim.28), calls=%async_computation | async-start | bytes 2097152 | tf_op jit(solution)/shard_map/all_to_all | solution.py:26
  21.5 0.8 select_reduce_fusion.2
  22.3 0.1 convert_reduce_fusion.1
  22.4 0.8 slice_bitcast_fusion
  23.1 0.1 select_reduce_fusion.1
  23.3 0.1 and_select_fusion.off_ref
  23.4 31.4 %all-to-all-done.text_ref = bf16[64,2,32,128]{3,2,1,0:T(8,128)(2,1)S(1)} async-done(((bf16[64,2,32,128]{3,2,1,0:T(8,128)(2,1)}), bf16[64,2,32,128]{3,2,1,0:T(8,128)(2,1)S(1)}, u32[]{:S(2)}, u32[]{:S(2)}) %all-to-all-start) | async-done | bytes 1048608 | tf_op jit(solution)/shard_map/all_to_all | solution.py:26
  54.8 0.0 copy-start
  54.8 0.9 copy-done
  55.7 0.0 copy-start.2
  55.7 0.9 copy-done.2
  56.6 1.8 shard_map.94
  58.4 13.1 %all_to_all.35.stats_ref = f32[8,24,256]{2,1,0:T(8,128)S(1)} all-to-all(f32[8,24,256]{2,1,0:T(8,128)S(1)} %broadcast_in_dim.33), channel_id=1, replica_groups=mesh['tok_0'=2,'tok_1'=8,'tok_2'=4,'head'=8] {'tok_0','tok_2'}, dimensions={0} | all-to-all | bytes 393216 | tf_op jit(solution)/shard_map/all_to_all | solution.py:26
  71.5 0.7 broadcast_in_dim.34
  72.2 3.9 %all-to-all-start.2 = ((f32[8,24,256]{2,1,0:T(8,128)}), f32[8,24,256]{2,1,0:T(8,128)S(1)}, u32[]{:S(2)}, u32[]{:S(2)}) async-start(f32[8,24,256]{2,1,0:T(8,128)} %broadcast_in_dim.34), calls=%async_computation.2 | async-start | bytes 393216 | tf_op jit(solution)/shard_map/all_to_all | solution.py:26
  76.1 6.5 %copy.13 = bf16[512,4096]{0,1:T(8,128)(2,1)} copy(bf16[512,4096]{1,0:T(8,128)(2,1)} %param.11) | data formatting | bytes 8388608 | tf_op args[4]
  82.7 0.0 copy-start.1
  82.7 0.0 copy-start.3
  82.7 4.7 %copy.14 = bf16[4,16,64,512]{3,2,1,0:T(8,128)(2,1)} copy(bf16[4,16,64,512]{3,2,0,1:T(8,128)(2,1)} %bitcast.12) | data formatting | bytes 8388608 | tf_op jit(solution)/shard_map/transpose | solution.py:149
  87.4 0.0 all-to-all-done.2.stats_ref
  87.4 0.0 copy-done.1
  87.4 0.0 copy-done.3
  87.4 3.8 %shard_map.96 = (bf16[512,256]{1,0:T(8,128)(2,1)S(1)}, f32[64,32,128]{2,1,0:T(8,128)}) custom-call(bf16[64,2,32,128]{3,2,1,0:T(8,128)(2,1)S(1)} %all-to-all-done.text_ref, bf16[512,128]{1,0:T(8,128)(2,1)S(1)} %copy-done.1, bf16[512,128]{1,0:T(8,128)(2,1)S(1)} %copy-done.3, f32[8,4,256]{2,1,0:T(4,128)S(1)} %and_select_fusion.off_ref, ...), custom_call_target="tpu_custom_call" | custom-call | tf_op jit(solution)/shard_map/pallas_call | solution.py:173
  91.2 5.8 %shard_map.97 = bf16[4096,256]{1,0:T(8,128)(2,1)S(1)} custom-call(bf16[4096,512]{1,0:T(8,128)(2,1)} %bitcast.11, bf16[512,256]{1,0:T(8,128)(2,1)S(1)} %get-tuple-element.6.kv_ref), custom_call_target="tpu_custom_call" | custom-call | tf_op jit(solution)/shard_map/pallas_call | solution.py:189
  97.0 28.5 %all_to_all.36 = bf16[4,1024,256]{2,1,0:T(8,128)(2,1)S(1)} all-to-all(bf16[4,1024,256]{2,1,0:T(8,128)(2,1)S(1)} %bitcast.10), channel_id=1, replica_groups=mesh['tok_0'=2,'tok_1'=8,'tok_2'=4,'head'=8] {'tok_2'}, dimensions={0} | all-to-all | bytes 4194304 | tf_op jit(solution)/shard_map/all_to_all | solution.py:201
  125.5 10.2 %all-to-all-start.3 = ((f32[64,32,128]{2,1,0:T(8,128)}), f32[64,32,128]{2,1,0:T(8,128)S(1)}, u32[]{:S(2)}, u32[]{:S(2)}) async-start(f32[64,32,128]{2,1,0:T(8,128)} %get-tuple-element.5), calls=%async_computation.3 | async-start | bytes 2097152 | tf_op jit(solution)/shard_map/all_to_all | solution.py:210
  135.7 1.2 reduce_sum.71
  136.9 27.2 %all-to-all-done.3 = f32[64,32,128]{2,1,0:T(8,128)S(1)} async-done(((f32[64,32,128]{2,1,0:T(8,128)}), f32[64,32,128]{2,1,0:T(8,128)S(1)}, u32[]{:S(2)}, u32[]{:S(2)}) %all-to-all-start.3) | async-done | bytes 1048608 | tf_op jit(solution)/shard_map/all_to_all | solution.py:210
  164.1 7.4 %all-to-all-start.6 = ((bf16[16,64,256]{2,1,0:T(8,128)(2,1)}), bf16[16,64,256]{2,1,0:T(8,128)(2,1)S(1)}, u32[]{:S(2)}, u32[]{:S(2)}) async-start(bf16[16,64,256]{2,1,0:T(8,128)(2,1)} %bitcast.13), calls=%async_computation.6 | async-start | bytes 1048576 | tf_op jit(solution)/shard_map/all_to_all | solution.py:205
  171.5 0.1 reduce_sum.70
  171.6 15.3 %all-to-all-done.6 = bf16[16,64,256]{2,1,0:T(8,128)(2,1)S(1)} async-done(((bf16[16,64,256]{2,1,0:T(8,128)(2,1)}), bf16[16,64,256]{2,1,0:T(8,128)(2,1)S(1)}, u32[]{:S(2)}, u32[]{:S(2)}) %all-to-all-start.6) | async-done | bytes 524320 | tf_op jit(solution)/shard_map/all_to_all | solution.py:205
  186.9 0.9 broadcast_in_dim.35
  187.9 10.5 %all-to-all-start.4 = ((bf16[64,4,1024]{2,1,0:T(4,128)(2,1)}), bf16[64,4,1024]{2,1,0:T(4,128)(2,1)S(1)}, u32[]{:S(2)}, u32[]{:S(2)}) async-start(bf16[64,4,1024]{2,1,0:T(4,128)(2,1)} %broadcast_in_dim.35), calls=%async_computation.4 | async-start | bytes 1048576 | tf_op jit(solution)/shard_map/all_to_all | solution.py:26
  198.4 0.1 convert_reduce_fusion
  198.5 0.6 fusion.3
  199.1 17.4 %all-to-all-done.4 = bf16[64,4,1024]{2,1,0:T(4,128)(2,1)S(1)} async-done(((bf16[64,4,1024]{2,1,0:T(4,128)(2,1)}), bf16[64,4,1024]{2,1,0:T(4,128)(2,1)S(1)}, u32[]{:S(2)}, u32[]{:S(2)}) %all-to-all-start.4) | async-done | bytes 524320 | tf_op jit(solution)/shard_map/all_to_all | solution.py:26
  216.5 0.9 reshape.75
  (8 shorter events, 0.1 us)
Async XLA Ops:
  3.3 51.5 %all-to-all-start = ((bf16[64,2,32,128]{3,2,1,0:T(8,128)(2,1)}), bf16[64,2,32,128]{3,2,1,0:T(8,128)(2,1)S(1)}, u32[]{:S(2)}, u32[]{:S(2)}) async-start(bf16[64,2,32,128]{3,2,1,0:T(8,128)(2,1)} %broadcast_in_dim.28), calls=%async_computation | async-start | bytes 2097152 | tf_op jit(solution)/shard_map/all_to_all | solution.py:26
  54.8 0.9 copy-start
  55.7 0.9 copy-start.2
  72.2 15.1 %all-to-all-start.2 = ((f32[8,24,256]{2,1,0:T(8,128)}), f32[8,24,256]{2,1,0:T(8,128)S(1)}, u32[]{:S(2)}, u32[]{:S(2)}) async-start(f32[8,24,256]{2,1,0:T(8,128)} %broadcast_in_dim.34), calls=%async_computation.2 | async-start | bytes 393216 | tf_op jit(solution)/shard_map/all_to_all | solution.py:26
  82.7 4.7 %copy-start.1 = (bf16[512,128]{1,0:T(8,128)(2,1)S(1)}, bf16[512,128]{1,0:T(8,128)(2,1)}, u32[]{:S(2)}) copy-start(bf16[512,128]{1,0:T(8,128)(2,1)} %k_ref.3) | copy-start | bytes 393220
  82.7 4.7 %copy-start.3 = (bf16[512,128]{1,0:T(8,128)(2,1)S(1)}, bf16[512,128]{1,0:T(8,128)(2,1)}, u32[]{:S(2)}) copy-start(bf16[512,128]{1,0:T(8,128)(2,1)} %v_ref.3) | copy-start | bytes 393220
  125.5 38.6 %all-to-all-start.3 = ((f32[64,32,128]{2,1,0:T(8,128)}), f32[64,32,128]{2,1,0:T(8,128)S(1)}, u32[]{:S(2)}, u32[]{:S(2)}) async-start(f32[64,32,128]{2,1,0:T(8,128)} %get-tuple-element.5), calls=%async_computation.3 | async-start | bytes 2097152 | tf_op jit(solution)/shard_map/all_to_all | solution.py:210
  164.1 22.8 %all-to-all-start.6 = ((bf16[16,64,256]{2,1,0:T(8,128)(2,1)}), bf16[16,64,256]{2,1,0:T(8,128)(2,1)S(1)}, u32[]{:S(2)}, u32[]{:S(2)}) async-start(bf16[16,64,256]{2,1,0:T(8,128)(2,1)} %bitcast.13), calls=%async_computation.6 | async-start | bytes 1048576 | tf_op jit(solution)/shard_map/all_to_all | solution.py:205
  187.9 28.7 %all-to-all-start.4 = ((bf16[64,4,1024]{2,1,0:T(4,128)(2,1)}), bf16[64,4,1024]{2,1,0:T(4,128)(2,1)S(1)}, u32[]{:S(2)}, u32[]{:S(2)}) async-start(bf16[64,4,1024]{2,1,0:T(4,128)(2,1)} %broadcast_in_dim.35), calls=%async_computation.4 | async-start | bytes 1048576 | tf_op jit(solution)/shard_map/all_to_all | solution.py:26

commit v2 on v1

v2 whole, which is shorter than its diff:
```python
import jax
import jax.numpy as jnp
from jax import lax
from jax.experimental import pallas as pl
from jax.experimental.pallas import tpu as pltpu
from jax.sharding import Mesh
from jax.sharding import PartitionSpec as P

HEAD_WIDTH = 128
FRAME_DEV = 4
TOK = ("tok_0", "tok_1", "tok_2")
FAR = ("tok_0", "tok_1")
NEAR = "tok_2"
CHUNK = 256
SCALE = HEAD_WIDTH**-0.5
LOG2E = 1.4426950408889634
OFF = 1e30
LOW = -1e29
F32 = jnp.float32
BF16 = jnp.bfloat16
NT = (((1,), (1,)), ((), ()))
NN = (((1,), (0,)), ((), ()))
PARAMS = pltpu.CompilerParams(vmem_limit_bytes=32 * 2**20)
WHOLE = pl.BlockSpec(memory_space=pltpu.VMEM)
SCALARS = pl.BlockSpec(memory_space=pltpu.SMEM)


def from_everyone(x, axis):
    peers = lax.axis_size(axis)
    return lax.all_to_all(jnp.broadcast_to(x[None], (peers, *x.shape)), axis, 0, 0, tiled=True)


def shifted(x, axis, step):
    peers = lax.axis_size(axis)
    return lax.ppermute(x, axis, [(i, (i + step) % peers) for i in range(peers)])


def dot(a, b, dims):
    return lax.dot_general(a, b, dims, preferred_element_type=F32)


def chunk_of(text_ref, c, which):
    per = CHUNK // text_ref.shape[2]
    return text_ref[c * per : (c + 1) * per, which].reshape(CHUNK, HEAD_WIDTH)


def frame_slices(off_ref, c, rows, frames):
    for f in range(frames):
        yield slice(f * rows, (f + 1) * rows), off_ref[c, f : f + 1, :]


def join(parts):
    top = parts[0][0]
    for part in parts[1:]:
        top = jnp.maximum(top, part[0])
    total = jnp.zeros_like(top)
    weighted = jnp.zeros_like(top)
    for part in parts:
        factor = jnp.exp2(part[0] - top)
        total += part[1] * factor
        weighted += part[2] * factor
    return top, total, weighted


def stats_kernel(text_ref, off_ref, *refs):
    kv_refs, out_ref = refs[:-1], refs[-1]
    chunks = out_ref.shape[0] // 3
    for c in range(chunks):
        q_c, g_c = chunk_of(text_ref, c, 0), chunk_of(text_ref, c, 1)
        parts = []
        for p, kv_ref in enumerate(kv_refs):
            rows = kv_ref.shape[1] // FRAME_DEV
            scores = dot(kv_ref[0], q_c, NT) * (SCALE * LOG2E)
            dprobs = dot(kv_ref[1], g_c, NT)
            offs = off_ref.at[:, p * FRAME_DEV : (p + 1) * FRAME_DEV]
            top = jnp.full((1, CHUNK), LOW, F32)
            for here, off in frame_slices(offs, c, rows, FRAME_DEV):
                top = jnp.maximum(top, jnp.max(scores[here], axis=0, keepdims=True) - off)
            total = jnp.zeros((1, CHUNK), F32)
            weighted = jnp.zeros((1, CHUNK), F32)
            for here, off in frame_slices(offs, c, rows, FRAME_DEV):
                terms = jnp.exp2(scores[here] - (top + off))
                total += jnp.sum(terms, axis=0, keepdims=True)
                weighted += jnp.sum(terms * dprobs[here], axis=0, keepdims=True)
            parts.append((top, total, weighted))
        for k, part in enumerate(join(parts)):
            out_ref[k * chunks + c : k * chunks + c + 1, :] = part


def join_kernel(stats_ref, out_ref):
    lines = stats_ref.shape[1] // 3
    parts = [
        [stats_ref[k, j * lines : (j + 1) * lines] for j in range(3)]
        for k in range(stats_ref.shape[0])
    ]
    top, total, weighted = join(parts)
    out_ref[:lines] = top + jnp.log2(total)
    out_ref[lines:] = weighted / total


def query_kernel(text_ref, off_ref, norm_ref, *refs):
    kv_refs, dq_ref, ds_scr = refs[:-2], refs[-2], refs[-1]
    chunks = norm_ref.shape[0] // 2
    per = CHUNK // dq_ref.shape[1]
    for c in range(chunks):
        q_c, g_c = chunk_of(text_ref, c, 0), chunk_of(text_ref, c, 1)
        shift = norm_ref[c : c + 1, :]
        delta = norm_ref[chunks + c : chunks + c + 1, :]
        dq = jnp.zeros((HEAD_WIDTH, CHUNK), F32)
        for p, kv_ref in enumerate(kv_refs):
            rows = kv_ref.shape[1] // FRAME_DEV
            scores = dot(kv_ref[0], q_c, NT) * (SCALE * LOG2E)
            dprobs = dot(kv_ref[1], g_c, NT)
            offs = off_ref.at[:, p * FRAME_DEV : (p + 1) * FRAME_DEV]
            for here, off in frame_slices(offs, c, rows, FRAME_DEV):
                probs = jnp.exp2(scores[here] - (shift + off))
                ds_scr[here] = (probs * (dprobs[here] - delta)).astype(BF16)
            dq += dot(kv_ref[0].T, ds_scr[...], NN)
        dq_ref[c * per : (c + 1) * per] = (dq * SCALE).T.reshape(per, dq_ref.shape[1], HEAD_WIDTH)


def token_kernel(near_ref, kv_ref, off_ref, norm_ref, far_vision_ref, *refs):
    pieces = off_ref.shape[0]
    text_refs, out_refs = refs[:pieces], refs[pieces : 2 * pieces]
    p_scr, ds_scr, kv_scr, vision_ref, vision_sem = refs[2 * pieces :]
    vision_copy = pltpu.make_async_copy(far_vision_ref, vision_ref, vision_sem)
    vision_copy.start()
    chunks = norm_ref.shape[1] // 2
    rows = kv_ref.shape[1] // FRAME_DEV
    key_sum = jnp.zeros(kv_ref.shape[1:], F32)
    value_sum = jnp.zeros(kv_ref.shape[1:], F32)
    for p, text_ref in enumerate(text_refs):
        norm = norm_ref[(near_ref[0] + (pieces - p)) % pieces]
        for c in range(chunks):
            q_c, g_c = chunk_of(text_ref, c, 0), chunk_of(text_ref, c, 1)
            shift, delta = norm[c : c + 1], norm[chunks + c : chunks + c + 1]
            scores = dot(kv_ref[0], q_c, NT) * (SCALE * LOG2E)
            dprobs = dot(kv_ref[1], g_c, NT)
            for here, off in frame_slices(off_ref.at[p], c, rows, FRAME_DEV):
                probs = jnp.exp2(scores[here] - (shift + off))
                p_scr[here] = probs.astype(BF16)
                ds_scr[here] = (probs * (dprobs[here] - delta)).astype(BF16)
            value_sum += dot(p_scr[...], g_c, NN)
            key_sum += dot(ds_scr[...], q_c, NN)
    kv_scr[:, :HEAD_WIDTH] = (key_sum * SCALE).astype(BF16)
    kv_scr[:, HEAD_WIDTH:] = value_sum.astype(BF16)
    vision_copy.wait()
    size = 512
    for p, out_ref in enumerate(out_refs):
        for at in range(0, out_ref.shape[0], size):
            block = vision_ref[p, at : at + size]
            out_ref[at : at + size] = dot(block, kv_scr[...], NN).astype(BF16)


def turn_kernel(near_ref, vision_ref, out_ref):
    pieces, _, size, _ = out_ref.shape
    turned = vision_ref[...].T
    for p in range(pieces):
        at = (p + pieces - near_ref[0]) % pieces
        out_ref[at, 0] = turned[p * size : (p + 1) * size]


def bases_from(at, peers):
    return [lax.rem(at + peers - k, jnp.int32(peers)) for k in range(peers)]


def row_bounds(lengths, frame_range, rows):
    part_ids = jnp.arange(lengths.shape[0], dtype=jnp.int32)
    ends = jnp.sum(jnp.where(part_ids[None, :] <= part_ids[:, None], lengths[None, :], 0), axis=1)
    segment = jnp.sum((rows[:, None] >= ends[None, :]).astype(jnp.int32), axis=1)
    pick = (segment[:, None] == part_ids[None, :]).astype(jnp.int32)
    begin = jnp.sum(pick * frame_range[None, :, 0], axis=1)
    end = jnp.sum(pick * frame_range[None, :, 1], axis=1)
    return begin, end


def offsets(begin, end, at):
    allowed = (at[:, None] >= begin[None, :]) & (at[:, None] < end[None, :])
    off = jnp.where(allowed, 0.0, OFF).astype(F32)
    return off.reshape(at.shape[0], -1, CHUNK).transpose(1, 0, 2)


def shards(text_queries, text_grads, vision_keys, video_value_rows, vision, lengths, frame_range):
    far, near = lax.axis_size(FAR), lax.axis_size(NEAR)
    my_far, my_near = lax.axis_index(FAR), lax.axis_index(NEAR)
    peers = far * near
    own_rows = text_queries.shape[0]
    members = text_queries.shape[1] // HEAD_WIDTH
    lines = own_rows * members
    kv_rows = vision_keys.shape[0]
    features = vision.shape[1]
    near_id = my_near.reshape(1).astype(jnp.int32)

    own_text = jnp.stack(
        (text_queries.reshape(lines, HEAD_WIDTH), text_grads.reshape(lines, HEAD_WIDTH))
    )
    text = from_everyone(own_text, FAR).reshape(far, 2, lines, HEAD_WIDTH)
    own_kv = jnp.stack((vision_keys, video_value_rows))
    all_kv = [own_kv] + [shifted(own_kv, NEAR, k) for k in range(1, near)]
    all_text = [text] + [shifted(text, NEAR, k) for k in range(1, near)]

    line_ids = jnp.arange(far * lines, dtype=jnp.int32)
    sources = jnp.stack(bases_from(my_near, near))
    row_of = (
        (line_ids // lines)[None, :] * (near * own_rows)
        + sources[:, None] * own_rows
        + (line_ids % lines // members)[None, :]
    )
    begin, end = row_bounds(lengths, frame_range, row_of.reshape(-1))
    steps = jnp.arange(FRAME_DEV, dtype=jnp.int32)
    first = (my_far * near + sources) * FRAME_DEV
    group_frames = (first[:, None] + steps[None, :]).reshape(-1)
    own_off = offsets(begin[: far * lines], end[: far * lines], group_frames)
    all_off = offsets(begin, end, first[0] + steps)
    chunks = far * lines // CHUNK
    all_off = all_off.reshape(near, chunks, FRAME_DEV, CHUNK)

    part = features // peers
    turned = pl.pallas_call(
        turn_kernel,
        out_shape=jax.ShapeDtypeStruct((near, far, part, kv_rows), BF16),
        grid=(far,),
        in_specs=[SCALARS, pl.BlockSpec((kv_rows, near * part), lambda i: (0, i))],
        out_specs=pl.BlockSpec((near, 1, part, kv_rows), lambda i: (0, i, 0, 0)),
        compiler_params=PARAMS,
    )(near_id, vision)
    turned = turned.reshape(near, far * part, kv_rows)
    text, turned = lax.optimization_barrier((text, turned))

    stats = pl.pallas_call(
        stats_kernel,
        out_shape=jax.ShapeDtypeStruct((3 * chunks, CHUNK), F32),
        in_specs=[WHOLE] * (2 + near),
        out_specs=WHOLE,
        compiler_params=PARAMS,
    )(text, own_off, *all_kv)
    stats = from_everyone(stats, FAR).reshape(far, 3 * chunks, CHUNK)
    norm = pl.pallas_call(
        join_kernel,
        out_shape=jax.ShapeDtypeStruct((2 * chunks, CHUNK), F32),
        in_specs=[WHOLE],
        out_specs=WHOLE,
        compiler_params=PARAMS,
    )(stats)
    all_norm = from_everyone(norm, NEAR).reshape(near, 2 * chunks, CHUNK)

    dq = pl.pallas_call(
        query_kernel,
        out_shape=jax.ShapeDtypeStruct((far, lines, HEAD_WIDTH), F32),
        in_specs=[WHOLE] * (3 + near),
        out_specs=WHOLE,
        scratch_shapes=[pltpu.VMEM((kv_rows, CHUNK), BF16)],
        compiler_params=PARAMS,
    )(text, own_off, norm, *all_kv)

    sums = pl.pallas_call(
        token_kernel,
        out_shape=[jax.ShapeDtypeStruct((far * part, 2 * HEAD_WIDTH), BF16)] * near,
        in_specs=[SCALARS] + [WHOLE] * 3 + [pl.BlockSpec(memory_space=pl.ANY)] + [WHOLE] * near,
        out_specs=[WHOLE] * near,
        scratch_shapes=[
            pltpu.VMEM((kv_rows, CHUNK), BF16),
            pltpu.VMEM((kv_rows, CHUNK), BF16),
            pltpu.VMEM((kv_rows, 2 * HEAD_WIDTH), BF16),
            pltpu.VMEM((near, far * part, kv_rows), BF16),
            pltpu.SemaphoreType.DMA,
        ],
        compiler_params=PARAMS,
    )(near_id, own_kv, all_off, all_norm, turned, *all_text)

    sums, dq = lax.optimization_barrier((sums, dq))
    got = [sums[0]] + [shifted(sums[k], NEAR, k) for k in range(1, near)]

    dq = jnp.sum(lax.all_to_all(dq, FAR, 0, 0, tiled=True), axis=0).astype(BF16)
    dq = from_everyone(dq.reshape(own_rows, -1), FAR).reshape(far, own_rows, -1)

    weights = sum(one.astype(F32) for one in got).astype(BF16)
    weights, dq = lax.optimization_barrier((weights, dq))
    weights = lax.all_to_all(
        weights.reshape(far, part, 2 * HEAD_WIDTH), FAR, 0, 0, tiled=True
    )
    all_dq = [dq] + [shifted(dq, NEAR, k) for k in range(1, near)]
    query_grad = jnp.stack([lax.select_n(base, *all_dq) for base in bases_from(my_near, near)], 1)
    query_grad = query_grad.reshape(peers * own_rows, -1)
    weights = jnp.sum(weights.astype(F32), axis=0)
    return query_grad, weights[:, :HEAD_WIDTH], weights[:, HEAD_WIDTH:]


def solution(mesh):
    finer = Mesh(
        mesh.devices.reshape(2, 8, 4, mesh.shape["head"]), ("tok_0", "tok_1", "tok_2", "head")
    )
    return jax.shard_map(
        shards,
        mesh=finer,
        in_specs=(
            P(TOK, "head"),
            P(TOK, "head"),
            P(TOK, "head"),
            P(TOK, "head"),
            P(TOK, None),
            P(),
            P(),
        ),
        out_specs=(P(None, "head"), P(TOK, "head"), P(TOK, "head")),
        check_vma=False,
    )
```

time: 218 us -> 155 us (0.71)
  the two profiles are of different devices: /device:TPU:14 before, /device:TPU:40 now
where the time goes in v2:
time: 155 us; the launch traced here: 154 us
  starting transfers between devices  89.1 us (57%)
  blocking collectives  20.6 us (13%)
  waiting for transfers between devices  14.5 us (9%)
  local copies, waits for them, and re-layouts  12.9 us (8%)
  Pallas kernels  10.9 us (7%)
  other arithmetic  5.28 us (3%)
    all_to_all x4, starting transfers between devices, from_everyone(): lax.all_to_all(jnp.broadcast_to(x[None], (peers, *x.shape)), axis, 0, 0,...  40.6 us
    ppermute x12, starting transfers between devices, shifted(): lax.ppermute(x, axis, [(i, (i + step) % peers) for i in range(peers)])  39.9 us
    all_to_all x1, blocking collectives, shards(): dq = jnp.sum(lax.all_to_all(dq, FAR, 0, 0, tiled=True), axis=0).astype(BF16)  20.6 us
    all_to_all x1, starting transfers between devices, shards(): lax.all_to_all(weights.reshape(far, part, 2 * HEAD_WIDTH), FAR, 0, 0, til...  8.6 us
    all_to_all x4, waiting for transfers between devices, from_everyone(): lax.all_to_all(jnp.broadcast_to(x[None], (peers, *x.shape)), axis, 0, 0,...  8.58 us
    unnamed x7, local copies, waits for them, and re-layouts  6.31 us
    ppermute x12, waiting for transfers between devices, shifted(): lax.ppermute(x, axis, [(i, (i + step) % peers) for i in range(peers)])  5.89 us
    pallas_call x1, Pallas kernels, shards(): pl.pallas_call(token_kernel, out_shape=[jax.ShapeDtypeStruct((far * part,...  4.14 us
  transfers between devices with their start and end apart: 17, of which 4 were waited for; matrix products, arithmetic and copies ran while one was open for 6% of the time, Pallas kernels for 3%

profile of v2, /device:TPU:40, one launch (start us, length us, event | category | flops | bytes accessed | tf_op | source)
XLA Modules:
  0.0 154.3 jit_solution(15387010509628957509)
XLA Ops:
  0.6 1.0 pad_maximum_fusion.1.refs_0_.kv_ref
  1.6 3.4 %collective-permute-start = (bf16[2,512,128]{2,1,0:T(8,128)(2,1)S(1)}, bf16[2,512,128]{2,1,0:T(8,128)(2,1)S(1)}, u32[]{:S(2)}, u32[]{:S(2)}) collective-permute-start(bf16[2,512,128]{2,1,0:T(8,128)(2,1)S(1)} %pad_maximum_fusion.1.refs_0_.kv_ref), channel_id=1, source_target_pairs={{0,8},{8,16},{16,24},{24,0},{1,9},{9,17},{17,25},{25,1},{2,10},{10... | collective-permute-start | bytes 786440 | tf_op jit(solution)/shard_map/ppermute | solution.py:35
  5.0 4.6 %collective-permute-start.1 = (bf16[2,512,128]{2,1,0:T(8,128)(2,1)S(1)}, bf16[2,512,128]{2,1,0:T(8,128)(2,1)S(1)}, u32[]{:S(2)}, u32[]{:S(2)}) collective-permute-start(bf16[2,512,128]{2,1,0:T(8,128)(2,1)S(1)} %pad_maximum_fusion.1.refs_0_.kv_ref), channel_id=1, source_target_pairs={{0,16},{8,24},{16,0},{24,8},{1,17},{9,25},{17,1},{25,9},{2,18},{10... | collective-permute-start | bytes 786440 | tf_op jit(solution)/shard_map/ppermute | solution.py:35
  9.7 3.3 %collective-permute-start.2 = (bf16[2,512,128]{2,1,0:T(8,128)(2,1)S(1)}, bf16[2,512,128]{2,1,0:T(8,128)(2,1)S(1)}, u32[]{:S(2)}, u32[]{:S(2)}) collective-permute-start(bf16[2,512,128]{2,1,0:T(8,128)(2,1)S(1)} %pad_maximum_fusion.1.refs_0_.kv_ref), channel_id=1, source_target_pairs={{0,24},{8,0},{16,8},{24,16},{1,25},{9,1},{17,9},{25,17},{2,26},{10... | collective-permute-start | bytes 786440 | tf_op jit(solution)/shard_map/ppermute | solution.py:35
  13.0 0.7 stack_reshape.6
  13.7 0.7 stack_reshape.7
  14.5 0.8 broadcast_in_dim.40
  15.2 15.7 %all-to-all-start = ((bf16[16,2,32,128]{3,2,1,0:T(8,128)(2,1)}), bf16[16,2,32,128]{3,2,1,0:T(8,128)(2,1)S(1)}, u32[]{:S(2)}, u32[]{:S(2)}) async-start(bf16[16,2,32,128]{3,2,1,0:T(8,128)(2,1)} %broadcast_in_dim.40), calls=%async_computation | async-start | bytes 524288 | tf_op jit(solution)/shard_map/all_to_all | solution.py:30
  30.9 0.1 add_multiply_fusion
  31.0 0.8 slice_bitcast_fusion
  31.8 0.1 iota_add_fusion
  31.9 0.1 add_bitcast_fusion
  31.9 0.8 select_reduce_fusion.2
  32.7 0.1 convert_reduce_fusion.1
  32.8 0.1 select_reduce_fusion.1
  33.0 0.1 add.140
  33.0 2.2 %copy-done.2 = bf16[512,4096]{1,0:T(8,128)(2,1)S(1)} copy-done((bf16[512,4096]{1,0:T(8,128)(2,1)S(1)}, bf16[512,4096]{1,0:T(8,128)(2,1)}, u32[]{:S(2)}) %copy-start.2) | copy-done | bytes 4194328
  35.2 3.0 %shard_map.94 = bf16[4,16,64,512]{3,2,1,0:T(8,128)(2,1)S(1)} custom-call(s32[1]{0:T(128)} %bitcast.near_ref, bf16[512,4096]{1,0:T(8,128)(2,1)S(1)} %copy-done.2), custom_call_target="tpu_custom_call" | custom-call | tf_op jit(solution)/shard_map/pallas_call | solution.py:219
  38.2 1.9 %copy-done = bf16[4,16,64,512]{3,2,1,0:T(8,128)(2,1)} copy-done((bf16[4,16,64,512]{3,2,1,0:T(8,128)(2,1)}, bf16[4,16,64,512]{3,2,1,0:T(8,128)(2,1)S(1)}, u32[]{:S(2)}) %copy-start) | copy-done | bytes 4194328
  40.2 0.1 and_select_fusion.off_ref
  40.2 0.0 all-to-all-done.text_ref.refs_0_
  40.2 0.0 collective-permute-done.refs_1_
  40.2 0.0 collective-permute-done.1.refs_2_
  40.2 0.0 collective-permute-done.2.refs_3_
  40.3 1.8 %shard_map.95 = f32[6,256]{1,0:T(8,128)S(1)} custom-call(bf16[16,2,32,128]{3,2,1,0:T(8,128)(2,1)S(1)} %all-to-all-done.text_ref.refs_0_, f32[2,16,256]{2,1,0:T(8,128)S(1)} %and_select_fusion.off_ref, bf16[2,512,128]{2,1,0:T(8,128)(2,1)S(1)} %pad_maximum_fusion.1.refs_0_.kv_ref, bf16[2,512,128]{2,1,0:T(8,128)(2,1)S(1)} %collective-permute-done.refs_1_, ...), custom_call_target="tpu_custom_call" | custom-call | tf_op jit(solution)/shard_map/pallas_call | solution.py:230
  42.0 0.7 broadcast_in_dim.43
  42.7 12.0 %all-to-all-start.1 = ((f32[16,6,256]{2,1,0:T(8,128)}), f32[16,6,256]{2,1,0:T(8,128)S(1)}, u32[]{:S(2)}, u32[]{:S(2)}) async-start(f32[16,6,256]{2,1,0:T(8,128)} %broadcast_in_dim.43), calls=%async_computation.1 | async-start | bytes 262144 | tf_op jit(solution)/shard_map/all_to_all | solution.py:30
  54.8 2.5 %collective-permute-start.3 = (bf16[16,2,32,128]{3,2,1,0:T(8,128)(2,1)S(1)}, bf16[16,2,32,128]{3,2,1,0:T(8,128)(2,1)S(1)}, u32[]{:S(2)}, u32[]{:S(2)}) collective-permute-start(bf16[16,2,32,128]{3,2,1,0:T(8,128)(2,1)S(1)} %all-to-all-done.text_ref.refs_0_), channel_id=1, source_target_pairs={{0,8},{8,16},{16,24},{24,0},{1,9},{9,17},{17,25},{25,1},{2,10},{10... | collective-permute-start | bytes 786440 | tf_op jit(solution)/shard_map/ppermute | solution.py:35
  57.2 2.8 %collective-permute-start.4 = (bf16[16,2,32,128]{3,2,1,0:T(8,128)(2,1)S(1)}, bf16[16,2,32,128]{3,2,1,0:T(8,128)(2,1)S(1)}, u32[]{:S(2)}, u32[]{:S(2)}) collective-permute-start(bf16[16,2,32,128]{3,2,1,0:T(8,128)(2,1)S(1)} %all-to-all-done.text_ref.refs_0_), channel_id=1, source_target_pairs={{0,16},{8,24},{16,0},{24,8},{1,17},{9,25},{17,1},{25,9},{2,18},{10... | collective-permute-start | bytes 786440 | tf_op jit(solution)/shard_map/ppermute | solution.py:35
  60.1 3.7 %collective-permute-start.5 = (bf16[16,2,32,128]{3,2,1,0:T(8,128)(2,1)S(1)}, bf16[16,2,32,128]{3,2,1,0:T(8,128)(2,1)S(1)}, u32[]{:S(2)}, u32[]{:S(2)}) collective-permute-start(bf16[16,2,32,128]{3,2,1,0:T(8,128)(2,1)S(1)} %all-to-all-done.text_ref.refs_0_), channel_id=1, source_target_pairs={{0,24},{8,0},{16,8},{24,16},{1,25},{9,1},{17,9},{25,17},{2,26},{10... | collective-permute-start | bytes 786440 | tf_op jit(solution)/shard_map/ppermute | solution.py:35
  63.8 0.0 all-to-all-done.1.stats_ref
  63.9 0.1 shard_map.96.norm_ref
  63.9 0.6 broadcast_in_dim.44
  64.5 4.2 %all-to-all-start.2 = ((f32[4,4,256]{2,1,0:T(4,128)}), f32[4,4,256]{2,1,0:T(4,128)S(1)}, u32[]{:S(2)}, u32[]{:S(2)}) async-start(f32[4,4,256]{2,1,0:T(4,128)} %broadcast_in_dim.44), calls=%async_computation.2 | async-start | bytes 32768 | tf_op jit(solution)/shard_map/all_to_all | solution.py:30
  68.7 0.1 and_select_fusion.1.off_ref
  68.8 2.0 %shard_map.98 = f32[16,32,128]{2,1,0:T(8,128)S(1)} custom-call(bf16[16,2,32,128]{3,2,1,0:T(8,128)(2,1)S(1)} %all-to-all-done.text_ref.refs_0_, f32[2,16,256]{2,1,0:T(8,128)S(1)} %and_select_fusion.off_ref, f32[4,256]{1,0:T(4,128)S(1)} %shard_map.96.norm_ref, bf16[2,512,128]{2,1,0:T(8,128)(2,1)S(1)} %pad_maximum_fusion.1.refs_0_.kv_ref, ...), custom_call_target="tpu_custom_call" | custom-call | tf_op jit(solution)/shard_map/pallas_call | solution.py:247
  70.7 3.3 %all-to-all-done.2.norm_ref = f32[4,4,256]{2,1,0:T(4,128)S(1)} async-done(((f32[4,4,256]{2,1,0:T(4,128)}), f32[4,4,256]{2,1,0:T(4,128)S(1)}, u32[]{:S(2)}, u32[]{:S(2)}) %all-to-all-start.2) | async-done | bytes 16416 | tf_op jit(solution)/shard_map/all_to_all | solution.py:30
  74.0 0.0 collective-permute-done.3.refs_1_
  74.0 0.0 collective-permute-done.4.refs_2_
  74.1 0.0 collective-permute-done.5.refs_3_
  74.1 2.2 %copy-done.1 = bf16[4,16,64,512]{3,2,1,0:T(8,128)(2,1)S(1)} copy-done((bf16[4,16,64,512]{3,2,1,0:T(8,128)(2,1)S(1)}, bf16[4,16,64,512]{3,2,1,0:T(8,128)(2,1)}, u32[]{:S(2)}) %copy-start.1) | copy-done | bytes 4194328
  76.2 4.1 %shard_map.97 = (bf16[1024,256]{1,0:T(8,128)(2,1)S(1)}, bf16[1024,256]{1,0:T(8,128)(2,1)}, bf16[1024,256]{1,0:T(8,128)(2,1)S(1)}, bf16[1024,256]{1,0:T(8,128)(2,1)S(1)}) custom-call(s32[1]{0:T(128)} %bitcast.near_ref, bf16[2,512,128]{2,1,0:T(8,128)(2,1)S(1)} %pad_maximum_fusion.1.refs_0_.kv_ref, f32[4,2,4,256]{3,2,1,0:T(4,128)S(1)} %and_select_fusion.1.off_ref, ...), custom_call_target="tpu_custom_call" | custom-call | tf_op jit(solution)/shard_map/pallas_call | solution.py:256
  80.4 2.5 %collective-permute-start.6 = (bf16[1024,256]{1,0:T(8,128)(2,1)}, bf16[1024,256]{1,0:T(8,128)(2,1)S(1)}, u32[]{:S(2)}, u32[]{:S(2)}) collective-permute-start(bf16[1024,256]{1,0:T(8,128)(2,1)} %get-tuple-element.23), channel_id=1, source_target_pairs={{0,8},{8,16},{16,24},{24,0},{1,9},{9,17},{17,25},{25,1},{2,10},{10... | collective-permute-start | bytes 1572872 | tf_op jit(solution)/shard_map/ppermute | solution.py:35
  82.9 4.0 %collective-permute-start.7 = (bf16[1024,256]{1,0:T(8,128)(2,1)S(1)}, bf16[1024,256]{1,0:T(8,128)(2,1)S(1)}, u32[]{:S(2)}, u32[]{:S(2)}) collective-permute-start(bf16[1024,256]{1,0:T(8,128)(2,1)S(1)} %get-tuple-element.24), channel_id=1, source_target_pairs={{0,16},{8,24},{16,0},{24,8},{1,17},{9,25},{17,1},{25,9},{2,18},{10... | collective-permute-start | bytes 1572872 | tf_op jit(solution)/shard_map/ppermute | solution.py:35
  86.9 3.0 %collective-permute-start.8 = (bf16[1024,256]{1,0:T(8,128)(2,1)S(1)}, bf16[1024,256]{1,0:T(8,128)(2,1)}, u32[]{:S(2)}, u32[]{:S(2)}) collective-permute-start(bf16[1024,256]{1,0:T(8,128)(2,1)S(1)} %get-tuple-element.25), channel_id=1, source_target_pairs={{0,24},{8,0},{16,8},{24,16},{1,25},{9,1},{17,9},{25,17},{2,26},{10... | collective-permute-start | bytes 1572872 | tf_op jit(solution)/shard_map/ppermute | solution.py:35
  89.9 20.6 %all_to_all.30 = f32[16,32,128]{2,1,0:T(8,128)S(1)} all-to-all(f32[16,32,128]{2,1,0:T(8,128)S(1)} %shard_map.98), channel_id=1, replica_groups=mesh['tok_0'=2,'tok_1'=8,'tok_2'=4,'head'=8] {'tok_0','tok_1'}, dimensions={0} | all-to-all | bytes 524288 | tf_op jit(solution)/shard_map/all_to_all | solution.py:274
  110.6 0.7 broadcast_in_dim.45
  111.3 8.7 %all-to-all-start.4 = ((bf16[16,4,1024]{2,1,0:T(4,128)(2,1)}), bf16[16,4,1024]{2,1,0:T(4,128)(2,1)S(1)}, u32[]{:S(2)}, u32[]{:S(2)}) async-start(bf16[16,4,1024]{2,1,0:T(4,128)(2,1)} %broadcast_in_dim.45), calls=%async_computation.4 | async-start | bytes 262144 | tf_op jit(solution)/shard_map/all_to_all | solution.py:30
  120.0 0.0 collective-permute-done.7
  120.0 0.0 collective-permute-done.8
  120.0 2.1 %add_convert_fusion = bf16[1024,256]{1,0:T(8,128)(2,1)} fusion(bf16[1024,256]{1,0:T(8,128)(2,1)} %collective-permute-done.8, bf16[1024,256]{1,0:T(8,128)(2,1)S(1)} %collective-permute-done.7, bf16[1024,256]{1,0:T(8,128)(2,1)S(1)} %collective-permute-done.6, bf16[1024,256]{1,0:T(8,128)(2,1)S(1)} %get-tuple-element.22), kind=kLoop, calls=%fused_computation.1 | loop fusion | flops 2097152 | bytes 2621440 | tf_op jit(solution)/shard_map/convert_element_type | solution.py:277
  122.1 5.3 %all-to-all-done.4 = bf16[16,4,1024]{2,1,0:T(4,128)(2,1)S(1)} async-done(((bf16[16,4,1024]{2,1,0:T(4,128)(2,1)}), bf16[16,4,1024]{2,1,0:T(4,128)(2,1)S(1)}, u32[]{:S(2)}, u32[]{:S(2)}) %all-to-all-start.4) | async-done | bytes 131104 | tf_op jit(solution)/shard_map/all_to_all | solution.py:30
  127.3 8.6 %all-to-all-start.5 = ((bf16[16,64,256]{2,1,0:T(8,128)(2,1)}), bf16[16,64,256]{2,1,0:T(8,128)(2,1)S(1)}, u32[]{:S(2)}, u32[]{:S(2)}) async-start(bf16[16,64,256]{2,1,0:T(8,128)(2,1)} %bitcast.18), calls=%async_computation.5 | async-start | bytes 1048576 | tf_op jit(solution)/shard_map/all_to_all | solution.py:279
  135.9 4.3 %collective-permute-start.10 = (bf16[16,4,1024]{2,1,0:T(4,128)(2,1)S(1)}, bf16[16,4,1024]{2,1,0:T(4,128)(2,1)S(1)}, u32[]{:S(2)}, u32[]{:S(2)}) collective-permute-start(bf16[16,4,1024]{2,1,0:T(4,128)(2,1)S(1)} %all-to-all-done.4), channel_id=1, source_target_pairs={{0,16},{8,24},{16,0},{24,8},{1,17},{9,25},{17,1},{25,9},{2,18},{10... | collective-permute-start | bytes 393224 | tf_op jit(solution)/shard_map/ppermute | solution.py:35
  140.2 3.7 %collective-permute-start.11 = (bf16[16,4,1024]{2,1,0:T(4,128)(2,1)S(1)}, bf16[16,4,1024]{2,1,0:T(4,128)(2,1)S(1)}, u32[]{:S(2)}, u32[]{:S(2)}) collective-permute-start(bf16[16,4,1024]{2,1,0:T(4,128)(2,1)S(1)} %all-to-all-done.4), channel_id=1, source_target_pairs={{0,24},{8,0},{16,8},{24,16},{1,25},{9,1},{17,9},{25,17},{2,26},{10... | collective-permute-start | bytes 393224 | tf_op jit(solution)/shard_map/ppermute | solution.py:35
  143.9 2.2 %collective-permute-start.9 = (bf16[16,4,1024]{2,1,0:T(4,128)(2,1)S(1)}, bf16[16,4,1024]{2,1,0:T(4,128)(2,1)S(1)}, u32[]{:S(2)}, u32[]{:S(2)}) collective-permute-start(bf16[16,4,1024]{2,1,0:T(4,128)(2,1)S(1)} %all-to-all-done.4), channel_id=1, source_target_pairs={{0,8},{8,16},{16,24},{24,0},{1,9},{9,17},{17,25},{25,1},{2,10},{10... | collective-permute-start | bytes 393224 | tf_op jit(solution)/shard_map/ppermute | solution.py:35
  146.1 1.0 collective-permute-done.11
  147.1 4.9 %collective-permute-done.9 = bf16[16,4,1024]{2,1,0:T(4,128)(2,1)S(1)} collective-permute-done((bf16[16,4,1024]{2,1,0:T(4,128)(2,1)S(1)}, bf16[16,4,1024]{2,1,0:T(4,128)(2,1)S(1)}, u32[]{:S(2)}, u32[]{:S(2)}) %collective-permute-start.9) | collective-permute-done | bytes 131104 | tf_op jit(solution)/shard_map/ppermute | solution.py:35
  152.0 0.3 select_bitcast_fusion.3
  152.3 0.4 pad_maximum_fusion
  152.7 0.9 reshape.244
  153.6 0.0 all-to-all-done.5
  153.6 0.1 convert_reduce_fusion
  153.7 0.6 fusion.10
  (18 shorter events, 0.2 us)
Async XLA Ops:
  1.6 38.6 %collective-permute-start = (bf16[2,512,128]{2,1,0:T(8,128)(2,1)S(1)}, bf16[2,512,128]{2,1,0:T(8,128)(2,1)S(1)}, u32[]{:S(2)}, u32[]{:S(2)}) collective-permute-start(bf16[2,512,128]{2,1,0:T(8,128)(2,1)S(1)} %pad_maximum_fusion.1.refs_0_.kv_ref), channel_id=1, source_target_pairs={{0,8},{8,16},{16,24},{24,0},{1,9},{9,17},{17,25},{25,1},{2,10},{10... | collective-permute-start | bytes 786440 | tf_op jit(solution)/shard_map/ppermute | solution.py:35
  5.0 35.2 %collective-permute-start.1 = (bf16[2,512,128]{2,1,0:T(8,128)(2,1)S(1)}, bf16[2,512,128]{2,1,0:T(8,128)(2,1)S(1)}, u32[]{:S(2)}, u32[]{:S(2)}) collective-permute-start(bf16[2,512,128]{2,1,0:T(8,128)(2,1)S(1)} %pad_maximum_fusion.1.refs_0_.kv_ref), channel_id=1, source_target_pairs={{0,16},{8,24},{16,0},{24,8},{1,17},{9,25},{17,1},{25,9},{2,18},{10... | collective-permute-start | bytes 786440 | tf_op jit(solution)/shard_map/ppermute | solution.py:35
  9.7 30.6 %collective-permute-start.2 = (bf16[2,512,128]{2,1,0:T(8,128)(2,1)S(1)}, bf16[2,512,128]{2,1,0:T(8,128)(2,1)S(1)}, u32[]{:S(2)}, u32[]{:S(2)}) collective-permute-start(bf16[2,512,128]{2,1,0:T(8,128)(2,1)S(1)} %pad_maximum_fusion.1.refs_0_.kv_ref), channel_id=1, source_target_pairs={{0,24},{8,0},{16,8},{24,16},{1,25},{9,1},{17,9},{25,17},{2,26},{10... | collective-permute-start | bytes 786440 | tf_op jit(solution)/shard_map/ppermute | solution.py:35
  15.2 25.0 %all-to-all-start = ((bf16[16,2,32,128]{3,2,1,0:T(8,128)(2,1)}), bf16[16,2,32,128]{3,2,1,0:T(8,128)(2,1)S(1)}, u32[]{:S(2)}, u32[]{:S(2)}) async-start(bf16[16,2,32,128]{3,2,1,0:T(8,128)(2,1)} %broadcast_in_dim.40), calls=%async_computation | async-start | bytes 524288 | tf_op jit(solution)/shard_map/all_to_all | solution.py:30
  33.0 2.2 %copy-start.2 = (bf16[512,4096]{1,0:T(8,128)(2,1)S(1)}, bf16[512,4096]{1,0:T(8,128)(2,1)}, u32[]{:S(2)}) copy-start(bf16[512,4096]{1,0:T(8,128)(2,1)} %vision_ref.1) | copy-start | bytes 12582916
  38.2 1.9 %copy-start = (bf16[4,16,64,512]{3,2,1,0:T(8,128)(2,1)}, bf16[4,16,64,512]{3,2,1,0:T(8,128)(2,1)S(1)}, u32[]{:S(2)}) copy-start(bf16[4,16,64,512]{3,2,1,0:T(8,128)(2,1)S(1)} %shard_map.94) | copy-start | bytes 12582916
  42.7 21.1 %all-to-all-start.1 = ((f32[16,6,256]{2,1,0:T(8,128)}), f32[16,6,256]{2,1,0:T(8,128)S(1)}, u32[]{:S(2)}, u32[]{:S(2)}) async-start(f32[16,6,256]{2,1,0:T(8,128)} %broadcast_in_dim.43), calls=%async_computation.1 | async-start | bytes 262144 | tf_op jit(solution)/shard_map/all_to_all | solution.py:30
  54.8 19.3 %collective-permute-start.3 = (bf16[16,2,32,128]{3,2,1,0:T(8,128)(2,1)S(1)}, bf16[16,2,32,128]{3,2,1,0:T(8,128)(2,1)S(1)}, u32[]{:S(2)}, u32[]{:S(2)}) collective-permute-start(bf16[16,2,32,128]{3,2,1,0:T(8,128)(2,1)S(1)} %all-to-all-done.text_ref.refs_0_), channel_id=1, source_target_pairs={{0,8},{8,16},{16,24},{24,0},{1,9},{9,17},{17,25},{25,1},{2,10},{10... | collective-permute-start | bytes 786440 | tf_op jit(solution)/shard_map/ppermute | solution.py:35
  57.2 16.8 %collective-permute-start.4 = (bf16[16,2,32,128]{3,2,1,0:T(8,128)(2,1)S(1)}, bf16[16,2,32,128]{3,2,1,0:T(8,128)(2,1)S(1)}, u32[]{:S(2)}, u32[]{:S(2)}) collective-permute-start(bf16[16,2,32,128]{3,2,1,0:T(8,128)(2,1)S(1)} %all-to-all-done.text_ref.refs_0_), channel_id=1, source_target_pairs={{0,16},{8,24},{16,0},{24,8},{1,17},{9,25},{17,1},{25,9},{2,18},{10... | collective-permute-start | bytes 786440 | tf_op jit(solution)/shard_map/ppermute | solution.py:35
  60.1 14.0 %collective-permute-start.5 = (bf16[16,2,32,128]{3,2,1,0:T(8,128)(2,1)S(1)}, bf16[16,2,32,128]{3,2,1,0:T(8,128)(2,1)S(1)}, u32[]{:S(2)}, u32[]{:S(2)}) collective-permute-start(bf16[16,2,32,128]{3,2,1,0:T(8,128)(2,1)S(1)} %all-to-all-done.text_ref.refs_0_), channel_id=1, source_target_pairs={{0,24},{8,0},{16,8},{24,16},{1,25},{9,1},{17,9},{25,17},{2,26},{10... | collective-permute-start | bytes 786440 | tf_op jit(solution)/shard_map/ppermute | solution.py:35
  64.5 9.5 %all-to-all-start.2 = ((f32[4,4,256]{2,1,0:T(4,128)}), f32[4,4,256]{2,1,0:T(4,128)S(1)}, u32[]{:S(2)}, u32[]{:S(2)}) async-start(f32[4,4,256]{2,1,0:T(4,128)} %broadcast_in_dim.44), calls=%async_computation.2 | async-start | bytes 32768 | tf_op jit(solution)/shard_map/all_to_all | solution.py:30
  74.1 2.2 %copy-start.1 = (bf16[4,16,64,512]{3,2,1,0:T(8,128)(2,1)S(1)}, bf16[4,16,64,512]{3,2,1,0:T(8,128)(2,1)}, u32[]{:S(2)}) copy-start(bf16[4,16,64,512]{3,2,1,0:T(8,128)(2,1)} %copy-done) | copy-start | bytes 12582916
  80.4 39.6 %collective-permute-start.6 = (bf16[1024,256]{1,0:T(8,128)(2,1)}, bf16[1024,256]{1,0:T(8,128)(2,1)S(1)}, u32[]{:S(2)}, u32[]{:S(2)}) collective-permute-start(bf16[1024,256]{1,0:T(8,128)(2,1)} %get-tuple-element.23), channel_id=1, source_target_pairs={{0,8},{8,16},{16,24},{24,0},{1,9},{9,17},{17,25},{25,1},{2,10},{10... | collective-permute-start | bytes 1572872 | tf_op jit(solution)/shard_map/ppermute | solution.py:35
  82.9 37.1 %collective-permute-start.7 = (bf16[1024,256]{1,0:T(8,128)(2,1)S(1)}, bf16[1024,256]{1,0:T(8,128)(2,1)S(1)}, u32[]{:S(2)}, u32[]{:S(2)}) collective-permute-start(bf16[1024,256]{1,0:T(8,128)(2,1)S(1)} %get-tuple-element.24), channel_id=1, source_target_pairs={{0,16},{8,24},{16,0},{24,8},{1,17},{9,25},{17,1},{25,9},{2,18},{10... | collective-permute-start | bytes 1572872 | tf_op jit(solution)/shard_map/ppermute | solution.py:35
  86.9 33.1 %collective-permute-start.8 = (bf16[1024,256]{1,0:T(8,128)(2,1)S(1)}, bf16[1024,256]{1,0:T(8,128)(2,1)}, u32[]{:S(2)}, u32[]{:S(2)}) collective-permute-start(bf16[1024,256]{1,0:T(8,128)(2,1)S(1)} %get-tuple-element.25), channel_id=1, source_target_pairs={{0,24},{8,0},{16,8},{24,16},{1,25},{9,1},{17,9},{25,17},{2,26},{10... | collective-permute-start | bytes 1572872 | tf_op jit(solution)/shard_map/ppermute | solution.py:35
  111.3 16.1 %all-to-all-start.4 = ((bf16[16,4,1024]{2,1,0:T(4,128)(2,1)}), bf16[16,4,1024]{2,1,0:T(4,128)(2,1)S(1)}, u32[]{:S(2)}, u32[]{:S(2)}) async-start(bf16[16,4,1024]{2,1,0:T(4,128)(2,1)} %broadcast_in_dim.45), calls=%async_computation.4 | async-start | bytes 262144 | tf_op jit(solution)/shard_map/all_to_all | solution.py:30
  127.3 26.3 %all-to-all-start.5 = ((bf16[16,64,256]{2,1,0:T(8,128)(2,1)}), bf16[16,64,256]{2,1,0:T(8,128)(2,1)S(1)}, u32[]{:S(2)}, u32[]{:S(2)}) async-start(bf16[16,64,256]{2,1,0:T(8,128)(2,1)} %bitcast.18), calls=%async_computation.5 | async-start | bytes 1048576 | tf_op jit(solution)/shard_map/all_to_all | solution.py:279
  135.9 10.2 %collective-permute-start.10 = (bf16[16,4,1024]{2,1,0:T(4,128)(2,1)S(1)}, bf16[16,4,1024]{2,1,0:T(4,128)(2,1)S(1)}, u32[]{:S(2)}, u32[]{:S(2)}) collective-permute-start(bf16[16,4,1024]{2,1,0:T(4,128)(2,1)S(1)} %all-to-all-done.4), channel_id=1, source_target_pairs={{0,16},{8,24},{16,0},{24,8},{1,17},{9,25},{17,1},{25,9},{2,18},{10... | collective-permute-start | bytes 393224 | tf_op jit(solution)/shard_map/ppermute | solution.py:35
  140.2 6.9 %collective-permute-start.11 = (bf16[16,4,1024]{2,1,0:T(4,128)(2,1)S(1)}, bf16[16,4,1024]{2,1,0:T(4,128)(2,1)S(1)}, u32[]{:S(2)}, u32[]{:S(2)}) collective-permute-start(bf16[16,4,1024]{2,1,0:T(4,128)(2,1)S(1)} %all-to-all-done.4), channel_id=1, source_target_pairs={{0,24},{8,0},{16,8},{24,16},{1,25},{9,1},{17,9},{25,17},{2,26},{10... | collective-permute-start | bytes 393224 | tf_op jit(solution)/shard_map/ppermute | solution.py:35
  143.9 8.1 %collective-permute-start.9 = (bf16[16,4,1024]{2,1,0:T(4,128)(2,1)S(1)}, bf16[16,4,1024]{2,1,0:T(4,128)(2,1)S(1)}, u32[]{:S(2)}, u32[]{:S(2)}) collective-permute-start(bf16[16,4,1024]{2,1,0:T(4,128)(2,1)S(1)} %all-to-all-done.4), channel_id=1, source_target_pairs={{0,8},{8,16},{16,24},{24,0},{1,9},{9,17},{17,25},{25,1},{2,10},{10... | collective-permute-start | bytes 393224 | tf_op jit(solution)/shard_map/ppermute | solution.py:35

commit v3 on v2

--- a/solution.py
+++ b/solution.py
@@ -21,6 +21,9 @@
 NT = (((1,), (1,)), ((), ()))
 NN = (((1,), (0,)), ((), ()))
 PARAMS = pltpu.CompilerParams(vmem_limit_bytes=32 * 2**20)
+LARGE = pltpu.CompilerParams(vmem_limit_bytes=52 * 2**20)
+LARGER = pltpu.CompilerParams(vmem_limit_bytes=58 * 2**20)
+HEAVY = pl.CostEstimate(flops=10**11, bytes_accessed=2**20, transcendentals=0)
 WHOLE = pl.BlockSpec(memory_space=pltpu.VMEM)
 SCALARS = pl.BlockSpec(memory_space=pltpu.SMEM)
 
@@ -62,44 +65,53 @@
     return top, total, weighted
 
 
+def piece_stats(q_c, g_c, kv_ref, off_ref, c):
+    rows = kv_ref.shape[1] // FRAME_DEV
+    scores = dot(kv_ref[0], q_c, NT) * (SCALE * LOG2E)
+    dprobs = dot(kv_ref[1], g_c, NT)
+    top = jnp.full((1, CHUNK), LOW, F32)
+    for here, off in frame_slices(off_ref, c, rows, FRAME_DEV):
+        top = jnp.maximum(top, jnp.max(scores[here], axis=0, keepdims=True) - off)
+    total = jnp.zeros((1, CHUNK), F32)
+    weighted = jnp.zeros((1, CHUNK), F32)
+    for here, off in frame_slices(off_ref, c, rows, FRAME_DEV):
+        terms = jnp.exp2(scores[here] - (top + off))
+        total += jnp.sum(terms, axis=0, keepdims=True)
+        weighted += jnp.sum(terms * dprobs[here], axis=0, keepdims=True)
+    return top, total, weighted
+
+
 def stats_kernel(text_ref, off_ref, *refs):
-    kv_refs, out_ref = refs[:-1], refs[-1]
-    chunks = out_ref.shape[0] // 3
+    kv_refs, all_ref, stats_scr = refs[:-2], refs[-2], refs[-1]
+    chunks = stats_scr.shape[0] // 3
     for c in range(chunks):
         q_c, g_c = chunk_of(text_ref, c, 0), chunk_of(text_ref, c, 1)
         parts = []
         for p, kv_ref in enumerate(kv_refs):
-            rows = kv_ref.shape[1] // FRAME_DEV
-            scores = dot(kv_ref[0], q_c, NT) * (SCALE * LOG2E)
-            dprobs = dot(kv_ref[1], g_c, NT)
             offs = off_ref.at[:, p * FRAME_DEV : (p + 1) * FRAME_DEV]
-            top = jnp.full((1, CHUNK), LOW, F32)
-            for here, off in frame_slices(offs, c, rows, FRAME_DEV):
-                top = jnp.maximum(top, jnp.max(scores[here], axis=0, keepdims=True) - off)
-            total = jnp.zeros((1, CHUNK), F32)
-            weighted = jnp.zeros((1, CHUNK), F32)
-            for here, off in frame_slices(offs, c, rows, FRAME_DEV):
-                terms = jnp.exp2(scores[here] - (top + off))
-                total += jnp.sum(terms, axis=0, keepdims=True)
-                weighted += jnp.sum(terms * dprobs[here], axis=0, keepdims=True)
-            parts.append((top, total, weighted))
+            parts.append(piece_stats(q_c, g_c, kv_ref, offs, c))
         for k, part in enumerate(join(parts)):
-            out_ref[k * chunks + c : k * chunks + c + 1, :] = part
+            stats_scr[k * chunks + c : k * chunks + c + 1, :] = part
+    stats = stats_scr[...]
+    for k in range(all_ref.shape[0]):
+        all_ref[k] = stats
 
 
 def join_kernel(stats_ref, out_ref):
-    lines = stats_ref.shape[1] // 3
-    parts = [
-        [stats_ref[k, j * lines : (j + 1) * lines] for j in range(3)]
-        for k in range(stats_ref.shape[0])
-    ]
-    top, total, weighted = join(parts)
-    out_ref[:lines] = top + jnp.log2(total)
-    out_ref[lines:] = weighted / total
-
-
-def query_kernel(text_ref, off_ref, norm_ref, *refs):
+    lines = stats_ref.shape[2] // 3
+    for p in range(out_ref.shape[0]):
+        parts = [
+            [stats_ref[k, p, j * lines : (j + 1) * lines] for j in range(3)]
+            for k in range(stats_ref.shape[0])
+        ]
+        top, total, weighted = join(parts)
+        out_ref[p, :lines] = top + jnp.log2(total)
+        out_ref[p, lines:] = weighted / total
+
+
+def query_kernel(near_ref, text_ref, off_ref, all_norm_ref, *refs):
     kv_refs, dq_ref, ds_scr = refs[:-2], refs[-2], refs[-1]
+    norm_ref = all_norm_ref.at[near_ref[0]]
     chunks = norm_ref.shape[0] // 2
     per = CHUNK // dq_ref.shape[1]
     for c in range(chunks):
@@ -152,6 +164,10 @@
             out_ref[at : at + size] = dot(block, kv_scr[...], NN).astype(BF16)
 
 
+def sum_kernel(parts_ref, out_ref):
+    out_ref[...] = jnp.sum(parts_ref[...], axis=0).astype(BF16)
+
+
 def turn_kernel(near_ref, vision_ref, out_ref):
     pieces, _, size, _ = out_ref.shape
     turned = vision_ref[...].T
@@ -194,7 +210,11 @@
     own_text = jnp.stack(
         (text_queries.reshape(lines, HEAD_WIDTH), text_grads.reshape(lines, HEAD_WIDTH))
     )
-    text = from_everyone(own_text, FAR).reshape(far, 2, lines, HEAD_WIDTH)
+    own_text = jnp.broadcast_to(own_text[None], (far, *own_text.shape))
+    own_text, vision_keys, video_value_rows = lax.optimization_barrier(
+        (own_text, vision_keys, video_value_rows)
+    )
+    text = lax.all_to_all(own_text, FAR, 0, 0, tiled=True)
     own_kv = jnp.stack((vision_keys, video_value_rows))
     all_kv = [own_kv] + [shifted(own_kv, NEAR, k) for k in range(1, near)]
     all_text = [text] + [shifted(text, NEAR, k) for k in range(1, near)]
@@ -222,41 +242,42 @@
         grid=(far,),
         in_specs=[SCALARS, pl.BlockSpec((kv_rows, near * part), lambda i: (0, i))],
         out_specs=pl.BlockSpec((near, 1, part, kv_rows), lambda i: (0, i, 0, 0)),
-        compiler_params=PARAMS,
+        compiler_params=LARGER,
     )(near_id, vision)
     turned = turned.reshape(near, far * part, kv_rows)
     text, turned = lax.optimization_barrier((text, turned))
 
     stats = pl.pallas_call(
         stats_kernel,
-        out_shape=jax.ShapeDtypeStruct((3 * chunks, CHUNK), F32),
+        out_shape=jax.ShapeDtypeStruct((peers, 3 * chunks, CHUNK), F32),
         in_specs=[WHOLE] * (2 + near),
         out_specs=WHOLE,
+        scratch_shapes=[pltpu.VMEM((3 * chunks, CHUNK), F32)],
         compiler_params=PARAMS,
     )(text, own_off, *all_kv)
-    stats = from_everyone(stats, FAR).reshape(far, 3 * chunks, CHUNK)
-    norm = pl.pallas_call(
+    stats = lax.all_to_all(stats, TOK, 0, 0, tiled=True)
+    all_norm = pl.pallas_call(
         join_kernel,
-        out_shape=jax.ShapeDtypeStruct((2 * chunks, CHUNK), F32),
+        out_shape=jax.ShapeDtypeStruct((near, 2 * chunks, CHUNK), F32),
         in_specs=[WHOLE],
         out_specs=WHOLE,
         compiler_params=PARAMS,
-    )(stats)
-    all_norm = from_everyone(norm, NEAR).reshape(near, 2 * chunks, CHUNK)
+    )(stats.reshape(far, near, 3 * chunks, CHUNK))
 
     dq = pl.pallas_call(
         query_kernel,
         out_shape=jax.ShapeDtypeStruct((far, lines, HEAD_WIDTH), F32),
-        in_specs=[WHOLE] * (3 + near),
+        in_specs=[SCALARS] + [WHOLE] * (3 + near),
         out_specs=WHOLE,
         scratch_shapes=[pltpu.VMEM((kv_rows, CHUNK), BF16)],
         compiler_params=PARAMS,
-    )(text, own_off, norm, *all_kv)
+    )(near_id, text, own_off, all_norm, *all_kv)
+    dq = lax.all_to_all(dq, FAR, 0, 0, tiled=True)
 
     sums = pl.pallas_call(
         token_kernel,
         out_shape=[jax.ShapeDtypeStruct((far * part, 2 * HEAD_WIDTH), BF16)] * near,
-        in_specs=[SCALARS] + [WHOLE] * 3 + [pl.BlockSpec(memory_space=pl.ANY)] + [WHOLE] * near,
+        in_specs=[SCALARS] + [WHOLE] * 3 + [pl.BlockSpec(memory_space=pltpu.HBM)] + [WHOLE] * near,
         out_specs=[WHOLE] * near,
         scratch_shapes=[
             pltpu.VMEM((kv_rows, CHUNK), BF16),
@@ -265,13 +286,20 @@
             pltpu.VMEM((near, far * part, kv_rows), BF16),
             pltpu.SemaphoreType.DMA,
         ],
+        compiler_params=LARGE,
+        cost_estimate=HEAVY,
+    )(near_id, own_kv, all_off, all_norm, turned, *all_text)
+
+    got = [sums[0]] + [shifted(sums[k], NEAR, k) for k in range(1, near)]
+
+    dq = pl.pallas_call(
+        sum_kernel,
+        out_shape=jax.ShapeDtypeStruct((lines, HEAD_WIDTH), BF16),
+        in_specs=[WHOLE],
+        out_specs=WHOLE,
         compiler_params=PARAMS,
-    )(near_id, own_kv, all_off, all_norm, turned, *all_text)
-
-    sums, dq = lax.optimization_barrier((sums, dq))
-    got = [sums[0]] + [shifted(sums[k], NEAR, k) for k in range(1, near)]
-
-    dq = jnp.sum(lax.all_to_all(dq, FAR, 0, 0, tiled=True), axis=0).astype(BF16)
+        cost_estimate=HEAVY,
+    )(dq)
     dq = from_everyone(dq.reshape(own_rows, -1), FAR).reshape(far, own_rows, -1)
 
     weights = sum(one.astype(F32) for one in got).astype(BF16)

time: 155 us -> 159 us (1.026)
  the two profiles are of different devices: /device:TPU:40 before, /device:TPU:14 now
where the time goes in v3:
time: 159 us; the launch traced here: 158 us
  starting transfers between devices  89.5 us (56%)
  waiting for transfers between devices  34.9 us (22%)
  Pallas kernels  22.9 us (14%)
  local copies, waits for them, and re-layouts  5.31 us (3%)
  other arithmetic  4.22 us (3%)
    ppermute x12, starting transfers between devices, shifted(): lax.ppermute(x, axis, [(i, (i + step) % peers) for i in range(peers)])  35.1 us
    all_to_all x1, starting transfers between devices, shards(): text = lax.all_to_all(own_text, FAR, 0, 0, tiled=True)  14.8 us
    all_to_all x1, starting transfers between devices, shards(): stats = lax.all_to_all(stats, TOK, 0, 0, tiled=True)  14.2 us
    ppermute x12, waiting for transfers between devices, shifted(): lax.ppermute(x, axis, [(i, (i + step) % peers) for i in range(peers)])  12.4 us
    all_to_all x1, waiting for transfers between devices, shards(): stats = lax.all_to_all(stats, TOK, 0, 0, tiled=True)  12.2 us
    all_to_all x1, starting transfers between devices, from_everyone(): lax.all_to_all(jnp.broadcast_to(x[None], (peers, *x.shape)), axis, 0, 0,...  12 us
    pallas_call x1, Pallas kernels, shards(): pl.pallas_call(turn_kernel, out_shape=jax.ShapeDtypeStruct((near, far, pa...  10.9 us
    all_to_all x1, starting transfers between devices, shards(): lax.all_to_all(weights.reshape(far, part, 2 * HEAD_WIDTH), FAR, 0, 0, til...  9.79 us
  transfers between devices with their start and end apart: 17, of which 8 were waited for; matrix products, arithmetic and copies ran while one was open for 4% of the time, Pallas kernels for 13%

profile of v3, /device:TPU:14, one launch (start us, length us, event | category | flops | bytes accessed | tf_op | source)
XLA Modules:
  0.0 157.8 jit_solution(8446451272482250827)
XLA Ops:
  0.6 0.7 stack_reshape.6
  1.3 0.7 stack_reshape.7
  2.1 0.8 broadcast_in_dim.32
  2.8 1.0 pad_maximum_fusion.1.refs_0_.kv_ref
  3.8 2.4 %collective-permute-start = (bf16[2,512,128]{2,1,0:T(8,128)(2,1)S(1)}, bf16[2,512,128]{2,1,0:T(8,128)(2,1)S(1)}, u32[]{:S(2)}, u32[]{:S(2)}) collective-permute-start(bf16[2,512,128]{2,1,0:T(8,128)(2,1)S(1)} %pad_maximum_fusion.1.refs_0_.kv_ref), channel_id=1, source_target_pairs={{0,8},{8,16},{16,24},{24,0},{1,9},{9,17},{17,25},{25,1},{2,10},{10... | collective-permute-start | bytes 786440 | tf_op jit(solution)/shard_map/ppermute | solution.py:38
  6.2 4.3 %collective-permute-start.1 = (bf16[2,512,128]{2,1,0:T(8,128)(2,1)S(1)}, bf16[2,512,128]{2,1,0:T(8,128)(2,1)S(1)}, u32[]{:S(2)}, u32[]{:S(2)}) collective-permute-start(bf16[2,512,128]{2,1,0:T(8,128)(2,1)S(1)} %pad_maximum_fusion.1.refs_0_.kv_ref), channel_id=1, source_target_pairs={{0,16},{8,24},{16,0},{24,8},{1,17},{9,25},{17,1},{25,9},{2,18},{10... | collective-permute-start | bytes 786440 | tf_op jit(solution)/shard_map/ppermute | solution.py:38
  10.5 1.9 %collective-permute-start.2 = (bf16[2,512,128]{2,1,0:T(8,128)(2,1)S(1)}, bf16[2,512,128]{2,1,0:T(8,128)(2,1)S(1)}, u32[]{:S(2)}, u32[]{:S(2)}) collective-permute-start(bf16[2,512,128]{2,1,0:T(8,128)(2,1)S(1)} %pad_maximum_fusion.1.refs_0_.kv_ref), channel_id=1, source_target_pairs={{0,24},{8,0},{16,8},{24,16},{1,25},{9,1},{17,9},{25,17},{2,26},{10... | collective-permute-start | bytes 786440 | tf_op jit(solution)/shard_map/ppermute | solution.py:38
  12.5 14.8 %all-to-all-start = ((bf16[16,2,32,128]{3,2,1,0:T(8,128)(2,1)}), bf16[16,2,32,128]{3,2,1,0:T(8,128)(2,1)S(1)}, u32[]{:S(2)}, u32[]{:S(2)}) async-start(bf16[16,2,32,128]{3,2,1,0:T(8,128)(2,1)} %broadcast_in_dim.32), calls=%async_computation | async-start | bytes 524288 | tf_op jit(solution)/shard_map/all_to_all | solution.py:217
  27.3 0.1 add_multiply_fusion
  27.4 0.8 slice_bitcast_fusion
  28.1 0.1 iota_add_fusion
  28.2 0.1 add_bitcast_fusion
  28.3 0.8 select_reduce_fusion.2
  29.1 0.1 convert_reduce_fusion.1
  29.2 0.1 select_reduce_fusion.1
  29.3 0.1 add.140
  29.4 10.9 %shard_map.94 = bf16[4,16,64,512]{3,2,1,0:T(8,128)(2,1)} custom-call(s32[1]{0:T(128)} %bitcast.near_ref, bf16[512,4096]{1,0:T(8,128)(2,1)} %vision_ref.1), custom_call_target="tpu_custom_call" | custom-call | tf_op jit(solution)/shard_map/pallas_call | solution.py:239
  40.3 0.1 and_select_fusion.off_ref
  40.4 1.5 all-to-all-done.text_ref.refs_0_
  41.9 0.0 collective-permute-done.refs_1_
  41.9 0.0 collective-permute-done.1.refs_2_
  41.9 0.0 collective-permute-done.2.refs_3_
  41.9 2.6 %shard_map.95 = f32[64,6,256]{2,1,0:T(8,128)} custom-call(bf16[16,2,32,128]{3,2,1,0:T(8,128)(2,1)S(1)} %all-to-all-done.text_ref.refs_0_, f32[2,16,256]{2,1,0:T(8,128)S(1)} %and_select_fusion.off_ref, bf16[2,512,128]{2,1,0:T(8,128)(2,1)S(1)} %pad_maximum_fusion.1.refs_0_.kv_ref, bf16[2,512,128]{2,1,0:T(8,128)(2,1)S(1)} %collective-permute-done.refs_1_, ...), custom_call_target="tpu_custom_call" | custom-call | tf_op jit(solution)/shard_map/pallas_call | solution.py:250
  44.6 14.2 %all-to-all-start.1 = ((f32[64,6,256]{2,1,0:T(8,128)}), f32[64,6,256]{2,1,0:T(8,128)S(1)}, u32[]{:S(2)}, u32[]{:S(2)}) async-start(f32[64,6,256]{2,1,0:T(8,128)} %shard_map.95), calls=%async_computation.1 | async-start | bytes 1048576 | tf_op jit(solution)/shard_map/all_to_all | solution.py:258
  58.8 2.4 %collective-permute-start.3 = (bf16[16,2,32,128]{3,2,1,0:T(8,128)(2,1)S(1)}, bf16[16,2,32,128]{3,2,1,0:T(8,128)(2,1)S(1)}, u32[]{:S(2)}, u32[]{:S(2)}) collective-permute-start(bf16[16,2,32,128]{3,2,1,0:T(8,128)(2,1)S(1)} %all-to-all-done.text_ref.refs_0_), channel_id=1, source_target_pairs={{0,8},{8,16},{16,24},{24,0},{1,9},{9,17},{17,25},{25,1},{2,10},{10... | collective-permute-start | bytes 786440 | tf_op jit(solution)/shard_map/ppermute | solution.py:38
  61.1 4.4 %collective-permute-start.4 = (bf16[16,2,32,128]{3,2,1,0:T(8,128)(2,1)S(1)}, bf16[16,2,32,128]{3,2,1,0:T(8,128)(2,1)S(1)}, u32[]{:S(2)}, u32[]{:S(2)}) collective-permute-start(bf16[16,2,32,128]{3,2,1,0:T(8,128)(2,1)S(1)} %all-to-all-done.text_ref.refs_0_), channel_id=1, source_target_pairs={{0,16},{8,24},{16,0},{24,8},{1,17},{9,25},{17,1},{25,9},{2,18},{10... | collective-permute-start | bytes 786440 | tf_op jit(solution)/shard_map/ppermute | solution.py:38
  65.5 1.9 %collective-permute-start.5 = (bf16[16,2,32,128]{3,2,1,0:T(8,128)(2,1)S(1)}, bf16[16,2,32,128]{3,2,1,0:T(8,128)(2,1)S(1)}, u32[]{:S(2)}, u32[]{:S(2)}) collective-permute-start(bf16[16,2,32,128]{3,2,1,0:T(8,128)(2,1)S(1)} %all-to-all-done.text_ref.refs_0_), channel_id=1, source_target_pairs={{0,24},{8,0},{16,8},{24,16},{1,25},{9,1},{17,9},{25,17},{2,26},{10... | collective-permute-start | bytes 786440 | tf_op jit(solution)/shard_map/ppermute | solution.py:38
  67.5 0.1 and_select_fusion.1.off_ref
  67.6 12.2 %all-to-all-done.1 = f32[64,6,256]{2,1,0:T(8,128)S(1)} async-done(((f32[64,6,256]{2,1,0:T(8,128)}), f32[64,6,256]{2,1,0:T(8,128)S(1)}, u32[]{:S(2)}, u32[]{:S(2)}) %all-to-all-start.1) | async-done | bytes 393248 | tf_op jit(solution)/shard_map/all_to_all | solution.py:258
  79.8 0.2 shard_map.96.norm_ref.all_norm_ref
  80.0 2.7 %shard_map.98 = f32[16,32,128]{2,1,0:T(8,128)} custom-call(s32[1]{0:T(128)} %bitcast.near_ref, bf16[16,2,32,128]{3,2,1,0:T(8,128)(2,1)S(1)} %all-to-all-done.text_ref.refs_0_, f32[2,16,256]{2,1,0:T(8,128)S(1)} %and_select_fusion.off_ref, f32[4,4,256]{2,1,0:T(4,128)S(1)} %shard_map.96.norm_ref.all_norm_ref, ...), custom_call_target="tpu_custom_call" | custom-call | tf_op jit(solution)/shard_map/pallas_call | solution.py:267
  82.7 3.5 %all-to-all-start.2 = ((f32[16,32,128]{2,1,0:T(8,128)}), f32[16,32,128]{2,1,0:T(8,128)S(1)}, u32[]{:S(2)}, u32[]{:S(2)}) async-start(f32[16,32,128]{2,1,0:T(8,128)} %shard_map.98), calls=%async_computation.2 | async-start | bytes 524288 | tf_op jit(solution)/shard_map/all_to_all | solution.py:275
  86.3 0.0 collective-permute-done.3.refs_1_
  86.3 0.0 collective-permute-done.4.refs_2_
  86.3 0.0 collective-permute-done.5.refs_3_
  86.3 6.4 %shard_map.97 = (bf16[1024,256]{1,0:T(8,128)(2,1)S(1)}, bf16[1024,256]{1,0:T(8,128)(2,1)}, bf16[1024,256]{1,0:T(8,128)(2,1)}, bf16[1024,256]{1,0:T(8,128)(2,1)}) custom-call(s32[1]{0:T(128)} %bitcast.near_ref, bf16[2,512,128]{2,1,0:T(8,128)(2,1)S(1)} %pad_maximum_fusion.1.refs_0_.kv_ref, f32[4,2,4,256]{3,2,1,0:T(4,128)S(1)} %and_select_fusion.1.off_ref, ...), custom_call_target="tpu_custom_call" | custom-call | flops 99999997952 | bytes 1048576 | tf_op jit(solution)/shard_map/pallas_call | solution.py:277
  92.8 3.1 %collective-permute-start.6 = (bf16[1024,256]{1,0:T(8,128)(2,1)}, bf16[1024,256]{1,0:T(8,128)(2,1)S(1)}, u32[]{:S(2)}, u32[]{:S(2)}) collective-permute-start(bf16[1024,256]{1,0:T(8,128)(2,1)} %get-tuple-element.20), channel_id=1, source_target_pairs={{0,8},{8,16},{16,24},{24,0},{1,9},{9,17},{17,25},{25,1},{2,10},{10... | collective-permute-start | bytes 1572872 | tf_op jit(solution)/shard_map/ppermute | solution.py:38
  95.9 2.6 %collective-permute-start.7 = (bf16[1024,256]{1,0:T(8,128)(2,1)}, bf16[1024,256]{1,0:T(8,128)(2,1)S(1)}, u32[]{:S(2)}, u32[]{:S(2)}) collective-permute-start(bf16[1024,256]{1,0:T(8,128)(2,1)} %get-tuple-element.21), channel_id=1, source_target_pairs={{0,16},{8,24},{16,0},{24,8},{1,17},{9,25},{17,1},{25,9},{2,18},{10... | collective-permute-start | bytes 1572872 | tf_op jit(solution)/shard_map/ppermute | solution.py:38
  98.6 2.5 %collective-permute-start.8 = (bf16[1024,256]{1,0:T(8,128)(2,1)}, bf16[1024,256]{1,0:T(8,128)(2,1)S(1)}, u32[]{:S(2)}, u32[]{:S(2)}) collective-permute-start(bf16[1024,256]{1,0:T(8,128)(2,1)} %get-tuple-element.22), channel_id=1, source_target_pairs={{0,24},{8,0},{16,8},{24,16},{1,25},{9,1},{17,9},{25,17},{2,26},{10... | collective-permute-start | bytes 1572872 | tf_op jit(solution)/shard_map/ppermute | solution.py:38
  101.1 0.0 all-to-all-done.2.parts_ref
  101.1 0.7 broadcast_in_dim.66
  101.8 12.0 %all-to-all-start.3 = ((bf16[16,4,1024]{2,1,0:T(4,128)(2,1)}), bf16[16,4,1024]{2,1,0:T(4,128)(2,1)S(1)}, u32[]{:S(2)}, u32[]{:S(2)}) async-start(bf16[16,4,1024]{2,1,0:T(4,128)(2,1)} %broadcast_in_dim.66), calls=%async_computation.3 | async-start | bytes 262144 | tf_op jit(solution)/shard_map/all_to_all | solution.py:33
  113.8 0.0 collective-permute-done.6
  113.8 0.6 collective-permute-done.7
  114.4 9.2 %collective-permute-done.8 = bf16[1024,256]{1,0:T(8,128)(2,1)S(1)} collective-permute-done((bf16[1024,256]{1,0:T(8,128)(2,1)}, bf16[1024,256]{1,0:T(8,128)(2,1)S(1)}, u32[]{:S(2)}, u32[]{:S(2)}) %collective-permute-start.8) | collective-permute-done | bytes 524320 | tf_op jit(solution)/shard_map/ppermute | solution.py:38
  123.6 1.0 add_convert_fusion
  124.7 2.0 %all-to-all-done.3 = bf16[16,4,1024]{2,1,0:T(4,128)(2,1)S(1)} async-done(((bf16[16,4,1024]{2,1,0:T(4,128)(2,1)}), bf16[16,4,1024]{2,1,0:T(4,128)(2,1)S(1)}, u32[]{:S(2)}, u32[]{:S(2)}) %all-to-all-start.3) | async-done | bytes 131104 | tf_op jit(solution)/shard_map/all_to_all | solution.py:33
  126.6 9.8 %all-to-all-start.4 = ((bf16[16,64,256]{2,1,0:T(8,128)(2,1)}), bf16[16,64,256]{2,1,0:T(8,128)(2,1)S(1)}, u32[]{:S(2)}, u32[]{:S(2)}) async-start(bf16[16,64,256]{2,1,0:T(8,128)(2,1)} %bitcast.19), calls=%async_computation.4 | async-start | bytes 1048576 | tf_op jit(solution)/shard_map/all_to_all | solution.py:307
  136.4 2.5 %collective-permute-start.10 = (bf16[16,4,1024]{2,1,0:T(4,128)(2,1)S(1)}, bf16[16,4,1024]{2,1,0:T(4,128)(2,1)S(1)}, u32[]{:S(2)}, u32[]{:S(2)}) collective-permute-start(bf16[16,4,1024]{2,1,0:T(4,128)(2,1)S(1)} %all-to-all-done.3), channel_id=1, source_target_pairs={{0,16},{8,24},{16,0},{24,8},{1,17},{9,25},{17,1},{25,9},{2,18},{10... | collective-permute-start | bytes 393224 | tf_op jit(solution)/shard_map/ppermute | solution.py:38
  138.9 2.8 %collective-permute-start.11 = (bf16[16,4,1024]{2,1,0:T(4,128)(2,1)S(1)}, bf16[16,4,1024]{2,1,0:T(4,128)(2,1)S(1)}, u32[]{:S(2)}, u32[]{:S(2)}) collective-permute-start(bf16[16,4,1024]{2,1,0:T(4,128)(2,1)S(1)} %all-to-all-done.3), channel_id=1, source_target_pairs={{0,24},{8,0},{16,8},{24,16},{1,25},{9,1},{17,9},{25,17},{2,26},{10... | collective-permute-start | bytes 393224 | tf_op jit(solution)/shard_map/ppermute | solution.py:38
  141.7 4.3 %collective-permute-start.9 = (bf16[16,4,1024]{2,1,0:T(4,128)(2,1)S(1)}, bf16[16,4,1024]{2,1,0:T(4,128)(2,1)S(1)}, u32[]{:S(2)}, u32[]{:S(2)}) collective-permute-start(bf16[16,4,1024]{2,1,0:T(4,128)(2,1)S(1)} %all-to-all-done.3), channel_id=1, source_target_pairs={{0,8},{8,16},{16,24},{24,0},{1,9},{9,17},{17,25},{25,1},{2,10},{10... | collective-permute-start | bytes 393224 | tf_op jit(solution)/shard_map/ppermute | solution.py:38
  146.0 0.0 collective-permute-done.10
  146.1 1.7 %collective-permute-done.11 = bf16[16,4,1024]{2,1,0:T(4,128)(2,1)S(1)} collective-permute-done((bf16[16,4,1024]{2,1,0:T(4,128)(2,1)S(1)}, bf16[16,4,1024]{2,1,0:T(4,128)(2,1)S(1)}, u32[]{:S(2)}, u32[]{:S(2)}) %collective-permute-start.11) | collective-permute-done | bytes 131104 | tf_op jit(solution)/shard_map/ppermute | solution.py:38
  147.8 0.8 collective-permute-done.9
  148.6 0.3 select_bitcast_fusion.3
  148.9 0.4 pad_maximum_fusion
  149.3 0.9 reshape.241
  150.2 6.9 %all-to-all-done.4 = bf16[16,64,256]{2,1,0:T(8,128)(2,1)S(1)} async-done(((bf16[16,64,256]{2,1,0:T(8,128)(2,1)}), bf16[16,64,256]{2,1,0:T(8,128)(2,1)S(1)}, u32[]{:S(2)}, u32[]{:S(2)}) %all-to-all-start.4) | async-done | bytes 524320 | tf_op jit(solution)/shard_map/all_to_all | solution.py:307
  157.1 0.1 convert_reduce_fusion
  157.2 0.6 fusion.10
  (13 shorter events, 0.1 us)
Async XLA Ops:
  3.8 38.1 %collective-permute-start = (bf16[2,512,128]{2,1,0:T(8,128)(2,1)S(1)}, bf16[2,512,128]{2,1,0:T(8,128)(2,1)S(1)}, u32[]{:S(2)}, u32[]{:S(2)}) collective-permute-start(bf16[2,512,128]{2,1,0:T(8,128)(2,1)S(1)} %pad_maximum_fusion.1.refs_0_.kv_ref), channel_id=1, source_target_pairs={{0,8},{8,16},{16,24},{24,0},{1,9},{9,17},{17,25},{25,1},{2,10},{10... | collective-permute-start | bytes 786440 | tf_op jit(solution)/shard_map/ppermute | solution.py:38
  6.2 35.7 %collective-permute-start.1 = (bf16[2,512,128]{2,1,0:T(8,128)(2,1)S(1)}, bf16[2,512,128]{2,1,0:T(8,128)(2,1)S(1)}, u32[]{:S(2)}, u32[]{:S(2)}) collective-permute-start(bf16[2,512,128]{2,1,0:T(8,128)(2,1)S(1)} %pad_maximum_fusion.1.refs_0_.kv_ref), channel_id=1, source_target_pairs={{0,16},{8,24},{16,0},{24,8},{1,17},{9,25},{17,1},{25,9},{2,18},{10... | collective-permute-start | bytes 786440 | tf_op jit(solution)/shard_map/ppermute | solution.py:38
  10.5 31.4 %collective-permute-start.2 = (bf16[2,512,128]{2,1,0:T(8,128)(2,1)S(1)}, bf16[2,512,128]{2,1,0:T(8,128)(2,1)S(1)}, u32[]{:S(2)}, u32[]{:S(2)}) collective-permute-start(bf16[2,512,128]{2,1,0:T(8,128)(2,1)S(1)} %pad_maximum_fusion.1.refs_0_.kv_ref), channel_id=1, source_target_pairs={{0,24},{8,0},{16,8},{24,16},{1,25},{9,1},{17,9},{25,17},{2,26},{10... | collective-permute-start | bytes 786440 | tf_op jit(solution)/shard_map/ppermute | solution.py:38
  12.5 29.4 %all-to-all-start = ((bf16[16,2,32,128]{3,2,1,0:T(8,128)(2,1)}), bf16[16,2,32,128]{3,2,1,0:T(8,128)(2,1)S(1)}, u32[]{:S(2)}, u32[]{:S(2)}) async-start(bf16[16,2,32,128]{3,2,1,0:T(8,128)(2,1)} %broadcast_in_dim.32), calls=%async_computation | async-start | bytes 524288 | tf_op jit(solution)/shard_map/all_to_all | solution.py:217
  44.6 35.3 %all-to-all-start.1 = ((f32[64,6,256]{2,1,0:T(8,128)}), f32[64,6,256]{2,1,0:T(8,128)S(1)}, u32[]{:S(2)}, u32[]{:S(2)}) async-start(f32[64,6,256]{2,1,0:T(8,128)} %shard_map.95), calls=%async_computation.1 | async-start | bytes 1048576 | tf_op jit(solution)/shard_map/all_to_all | solution.py:258
  58.8 27.5 %collective-permute-start.3 = (bf16[16,2,32,128]{3,2,1,0:T(8,128)(2,1)S(1)}, bf16[16,2,32,128]{3,2,1,0:T(8,128)(2,1)S(1)}, u32[]{:S(2)}, u32[]{:S(2)}) collective-permute-start(bf16[16,2,32,128]{3,2,1,0:T(8,128)(2,1)S(1)} %all-to-all-done.text_ref.refs_0_), channel_id=1, source_target_pairs={{0,8},{8,16},{16,24},{24,0},{1,9},{9,17},{17,25},{25,1},{2,10},{10... | collective-permute-start | bytes 786440 | tf_op jit(solution)/shard_map/ppermute | solution.py:38
  61.1 25.1 %collective-permute-start.4 = (bf16[16,2,32,128]{3,2,1,0:T(8,128)(2,1)S(1)}, bf16[16,2,32,128]{3,2,1,0:T(8,128)(2,1)S(1)}, u32[]{:S(2)}, u32[]{:S(2)}) collective-permute-start(bf16[16,2,32,128]{3,2,1,0:T(8,128)(2,1)S(1)} %all-to-all-done.text_ref.refs_0_), channel_id=1, source_target_pairs={{0,16},{8,24},{16,0},{24,8},{1,17},{9,25},{17,1},{25,9},{2,18},{10... | collective-permute-start | bytes 786440 | tf_op jit(solution)/shard_map/ppermute | solution.py:38
  65.5 20.8 %collective-permute-start.5 = (bf16[16,2,32,128]{3,2,1,0:T(8,128)(2,1)S(1)}, bf16[16,2,32,128]{3,2,1,0:T(8,128)(2,1)S(1)}, u32[]{:S(2)}, u32[]{:S(2)}) collective-permute-start(bf16[16,2,32,128]{3,2,1,0:T(8,128)(2,1)S(1)} %all-to-all-done.text_ref.refs_0_), channel_id=1, source_target_pairs={{0,24},{8,0},{16,8},{24,16},{1,25},{9,1},{17,9},{25,17},{2,26},{10... | collective-permute-start | bytes 786440 | tf_op jit(solution)/shard_map/ppermute | solution.py:38
  82.7 18.3 %all-to-all-start.2 = ((f32[16,32,128]{2,1,0:T(8,128)}), f32[16,32,128]{2,1,0:T(8,128)S(1)}, u32[]{:S(2)}, u32[]{:S(2)}) async-start(f32[16,32,128]{2,1,0:T(8,128)} %shard_map.98), calls=%async_computation.2 | async-start | bytes 524288 | tf_op jit(solution)/shard_map/all_to_all | solution.py:275
  92.8 21.1 %collective-permute-start.6 = (bf16[1024,256]{1,0:T(8,128)(2,1)}, bf16[1024,256]{1,0:T(8,128)(2,1)S(1)}, u32[]{:S(2)}, u32[]{:S(2)}) collective-permute-start(bf16[1024,256]{1,0:T(8,128)(2,1)} %get-tuple-element.20), channel_id=1, source_target_pairs={{0,8},{8,16},{16,24},{24,0},{1,9},{9,17},{17,25},{25,1},{2,10},{10... | collective-permute-start | bytes 1572872 | tf_op jit(solution)/shard_map/ppermute | solution.py:38
  95.9 18.5 %collective-permute-start.7 = (bf16[1024,256]{1,0:T(8,128)(2,1)}, bf16[1024,256]{1,0:T(8,128)(2,1)S(1)}, u32[]{:S(2)}, u32[]{:S(2)}) collective-permute-start(bf16[1024,256]{1,0:T(8,128)(2,1)} %get-tuple-element.21), channel_id=1, source_target_pairs={{0,16},{8,24},{16,0},{24,8},{1,17},{9,25},{17,1},{25,9},{2,18},{10... | collective-permute-start | bytes 1572872 | tf_op jit(solution)/shard_map/ppermute | solution.py:38
  98.6 25.1 %collective-permute-start.8 = (bf16[1024,256]{1,0:T(8,128)(2,1)}, bf16[1024,256]{1,0:T(8,128)(2,1)S(1)}, u32[]{:S(2)}, u32[]{:S(2)}) collective-permute-start(bf16[1024,256]{1,0:T(8,128)(2,1)} %get-tuple-element.22), channel_id=1, source_target_pairs={{0,24},{8,0},{16,8},{24,16},{1,25},{9,1},{17,9},{25,17},{2,26},{10... | collective-permute-start | bytes 1572872 | tf_op jit(solution)/shard_map/ppermute | solution.py:38
  101.8 24.8 %all-to-all-start.3 = ((bf16[16,4,1024]{2,1,0:T(4,128)(2,1)}), bf16[16,4,1024]{2,1,0:T(4,128)(2,1)S(1)}, u32[]{:S(2)}, u32[]{:S(2)}) async-start(bf16[16,4,1024]{2,1,0:T(4,128)(2,1)} %broadcast_in_dim.66), calls=%async_computation.3 | async-start | bytes 262144 | tf_op jit(solution)/shard_map/all_to_all | solution.py:33
  126.6 30.5 %all-to-all-start.4 = ((bf16[16,64,256]{2,1,0:T(8,128)(2,1)}), bf16[16,64,256]{2,1,0:T(8,128)(2,1)S(1)}, u32[]{:S(2)}, u32[]{:S(2)}) async-start(bf16[16,64,256]{2,1,0:T(8,128)(2,1)} %bitcast.19), calls=%async_computation.4 | async-start | bytes 1048576 | tf_op jit(solution)/shard_map/all_to_all | solution.py:307
  136.4 9.6 %collective-permute-start.10 = (bf16[16,4,1024]{2,1,0:T(4,128)(2,1)S(1)}, bf16[16,4,1024]{2,1,0:T(4,128)(2,1)S(1)}, u32[]{:S(2)}, u32[]{:S(2)}) collective-permute-start(bf16[16,4,1024]{2,1,0:T(4,128)(2,1)S(1)} %all-to-all-done.3), channel_id=1, source_target_pairs={{0,16},{8,24},{16,0},{24,8},{1,17},{9,25},{17,1},{25,9},{2,18},{10... | collective-permute-start | bytes 393224 | tf_op jit(solution)/shard_map/ppermute | solution.py:38
  138.9 8.8 %collective-permute-start.11 = (bf16[16,4,1024]{2,1,0:T(4,128)(2,1)S(1)}, bf16[16,4,1024]{2,1,0:T(4,128)(2,1)S(1)}, u32[]{:S(2)}, u32[]{:S(2)}) collective-permute-start(bf16[16,4,1024]{2,1,0:T(4,128)(2,1)S(1)} %all-to-all-done.3), channel_id=1, source_target_pairs={{0,24},{8,0},{16,8},{24,16},{1,25},{9,1},{17,9},{25,17},{2,26},{10... | collective-permute-start | bytes 393224 | tf_op jit(solution)/shard_map/ppermute | solution.py:38
  141.7 6.9 %collective-permute-start.9 = (bf16[16,4,1024]{2,1,0:T(4,128)(2,1)S(1)}, bf16[16,4,1024]{2,1,0:T(4,128)(2,1)S(1)}, u32[]{:S(2)}, u32[]{:S(2)}) collective-permute-start(bf16[16,4,1024]{2,1,0:T(4,128)(2,1)S(1)} %all-to-all-done.3), channel_id=1, source_target_pairs={{0,8},{8,16},{16,24},{24,0},{1,9},{9,17},{17,25},{25,1},{2,10},{10... | collective-permute-start | bytes 393224 | tf_op jit(solution)/shard_map/ppermute | solution.py:38

commit v4 on v3

v4 whole, which is shorter than its diff:
```python
import jax
import jax.numpy as jnp
from jax import lax
from jax.experimental import pallas as pl
from jax.experimental.pallas import tpu as pltpu
from jax.sharding import Mesh
from jax.sharding import PartitionSpec as P

HEAD_WIDTH = 128
FRAME_DEV = 4
TOK = ("tok_0", "tok_1", "tok_2")
FAR = ("tok_0", "tok_1")
NEAR = "tok_2"
CHUNK = 256
PART = 64
STATS_LINES = 12
SCALE = HEAD_WIDTH**-0.5
LOG2E = 1.4426950408889634
OFF = 1e30
LOW = -1e29
F32 = jnp.float32
BF16 = jnp.bfloat16
NT = (((1,), (1,)), ((), ()))
NN = (((1,), (0,)), ((), ()))
PARAMS = pltpu.CompilerParams(vmem_limit_bytes=32 * 2**20)
LARGE = pltpu.CompilerParams(vmem_limit_bytes=52 * 2**20)
HEAVY = pl.CostEstimate(flops=10**11, bytes_accessed=2**20, transcendentals=0)
WHOLE = pl.BlockSpec(memory_space=pltpu.VMEM)
SCALARS = pl.BlockSpec(memory_space=pltpu.SMEM)


def from_everyone(x, axis):
    peers = lax.axis_size(axis)
    return lax.all_to_all(jnp.broadcast_to(x[None], (peers, *x.shape)), axis, 0, 0, tiled=True)


def shifted(x, axis, step):
    peers = lax.axis_size(axis)
    return lax.ppermute(x, axis, [(i, (i + step) % peers) for i in range(peers)])


def dot(a, b, dims):
    return lax.dot_general(a, b, dims, preferred_element_type=F32)


def chunk_of(text_ref, c, which):
    per = CHUNK // text_ref.shape[2]
    return text_ref[c * per : (c + 1) * per, which].reshape(CHUNK, HEAD_WIDTH)


def row_bounds(place_ref, lengths_ref, range_ref, near_at, c):
    near, own_rows, lines = place_ref[1], place_ref[2], place_ref[3]
    line = lax.broadcasted_iota(jnp.int32, (1, CHUNK), 1) + c * CHUNK
    row = (lax.div(line, lines) * near + near_at) * own_rows + lax.rem(line, own_rows)
    begin = jnp.zeros((1, CHUNK), jnp.int32)
    end = jnp.zeros((1, CHUNK), jnp.int32)
    at = jnp.int32(0)
    for k in range(lengths_ref.shape[0]):
        stop = at + lengths_ref[k]
        inside = (row >= at) & (row < stop)
        begin = jnp.where(inside, range_ref[k, 0], begin)
        end = jnp.where(inside, range_ref[k, 1], end)
        at = stop
    return begin, end


def frame_slices(bounds, first, rows):
    begin, end = bounds
    for f in range(FRAME_DEV):
        allowed = (begin <= first + f) & (end > first + f)
        off = jnp.where(allowed, 0.0, OFF).astype(F32)
        yield slice(f * rows, (f + 1) * rows), off


def source(near_at, piece, near):
    return lax.rem(near_at + (near - piece), jnp.int32(near))


def join(parts):
    top = parts[0][0]
    for part in parts[1:]:
        top = jnp.maximum(top, part[0])
    total = jnp.zeros_like(top)
    weighted = jnp.zeros_like(top)
    for part in parts:
        factor = jnp.exp2(part[0] - top)
        total += part[1] * factor
        weighted += part[2] * factor
    return top, total, weighted


def piece_stats(q_c, g_c, kv_ref, bounds, first):
    rows = kv_ref.shape[1] // FRAME_DEV
    offs = list(frame_slices(bounds, first, rows))
    scores = dot(kv_ref[0], q_c, NT) * (SCALE * LOG2E)
    dprobs = dot(kv_ref[1], g_c, NT)
    top = jnp.full((1, CHUNK), LOW, F32)
    for here, off in offs:
        top = jnp.maximum(top, jnp.max(scores[here], axis=0, keepdims=True) - off)
    total = jnp.zeros((1, CHUNK), F32)
    weighted = jnp.zeros((1, CHUNK), F32)
    for here, off in offs:
        terms = jnp.exp2(scores[here] - (top + off))
        total += jnp.sum(terms, axis=0, keepdims=True)
        weighted += jnp.sum(terms * dprobs[here], axis=0, keepdims=True)
    return top, total, weighted


def prepare_kernel(q_ref, g_ref, text_ref):
    members = q_ref.shape[1] // HEAD_WIDTH
    for which, ref in enumerate((q_ref, g_ref)):
        rows = ref[...].astype(F32)
        lines = jnp.concatenate(
            [rows[:, m * HEAD_WIDTH : (m + 1) * HEAD_WIDTH] for m in range(members)], axis=0
        ).astype(BF16)
        for k in range(text_ref.shape[0]):
            text_ref[k, which] = lines


def mask_kernel(place_ref, lengths_ref, range_ref, out_ref):
    pieces, chunks = out_ref.shape[:2]
    first = (place_ref[4] + place_ref[0]) * FRAME_DEV
    for p in range(pieces):
        near_at = source(place_ref[0], p, pieces)
        for c in range(chunks):
            bounds = row_bounds(place_ref, lengths_ref, range_ref, near_at, c)
            for f, (_, off) in enumerate(frame_slices(bounds, first, 1)):
                out_ref[p, c, f : f + 1, :] = off


def stats_kernel(place_ref, lengths_ref, range_ref, text_ref, *refs):
    kv_refs, all_ref, stats_scr = refs[:-2], refs[-2], refs[-1]
    chunks, near = text_ref.shape[0] * text_ref.shape[2] // CHUNK, len(kv_refs)
    stats_scr[...] = jnp.zeros_like(stats_scr)
    for c in range(chunks):
        q_c, g_c = chunk_of(text_ref, c, 0), chunk_of(text_ref, c, 1)
        bounds = row_bounds(place_ref, lengths_ref, range_ref, place_ref[0], c)
        parts = []
        for p, kv_ref in enumerate(kv_refs):
            first = (place_ref[4] + source(place_ref[0], p, near)) * FRAME_DEV
            parts.append(piece_stats(q_c, g_c, kv_ref, bounds, first))
        for k, part in enumerate(join(parts)):
            stats_scr[k * chunks + c : k * chunks + c + 1, :] = part
    stats = stats_scr[...]
    for k in range(all_ref.shape[0]):
        all_ref[k] = stats


def join_kernel(stats_ref, out_ref):
    lines = out_ref.shape[1] // 2
    parts = [
        [stats_ref[k, j * lines : (j + 1) * lines] for j in range(3)]
        for k in range(stats_ref.shape[0])
    ]
    top, total, weighted = join(parts)
    norm = jnp.concatenate((top + jnp.log2(total), weighted / total), axis=0)
    for k in range(out_ref.shape[0]):
        out_ref[k] = norm


def query_kernel(place_ref, lengths_ref, range_ref, text_ref, copies_ref, *refs):
    kv_refs, dq_ref, ds_scr = refs[:-2], refs[-2], refs[-1]
    norm_ref = copies_ref.at[0]
    chunks, near = norm_ref.shape[0] // 2, len(kv_refs)
    per = CHUNK // dq_ref.shape[1]
    for c in range(chunks):
        q_c, g_c = chunk_of(text_ref, c, 0), chunk_of(text_ref, c, 1)
        bounds = row_bounds(place_ref, lengths_ref, range_ref, place_ref[0], c)
        shift = norm_ref[c : c + 1, :]
        delta = norm_ref[chunks + c : chunks + c + 1, :]
        dq = jnp.zeros((HEAD_WIDTH, CHUNK), F32)
        for p, kv_ref in enumerate(kv_refs):
            rows = kv_ref.shape[1] // FRAME_DEV
            first = (place_ref[4] + source(place_ref[0], p, near)) * FRAME_DEV
            scores = dot(kv_ref[0], q_c, NT) * (SCALE * LOG2E)
            dprobs = dot(kv_ref[1], g_c, NT)
            for here, off in frame_slices(bounds, first, rows):
                probs = jnp.exp2(scores[here] - (shift + off))
                ds_scr[here] = (probs * (dprobs[here] - delta)).astype(BF16)
            dq += dot(kv_ref[0].T, ds_scr[...], NN)
        dq_ref[c * per : (c + 1) * per] = (dq * SCALE).T.reshape(per, dq_ref.shape[1], HEAD_WIDTH)


def token_kernel(place_ref, off_ref, kv_ref, norm_ref, far_vision_ref, *refs):
    pieces = norm_ref.shape[0]
    text_refs, out_refs = refs[:pieces], refs[pieces : 2 * pieces]
    p_scr, ds_scr, vision_ref, vision_sem = refs[2 * pieces :]
    parts = vision_sem.shape[0]
    width = vision_ref.shape[1] // parts
    copies = [
        pltpu.make_async_copy(
            far_vision_ref.at[:, p * width : (p + 1) * width],
            vision_ref.at[:, p * width : (p + 1) * width],
            vision_sem.at[p],
        )
        for p in range(parts)
    ]
    for copy in copies:
        copy.start()
    chunks = norm_ref.shape[1] // 2
    rows = kv_ref.shape[1] // FRAME_DEV
    key_sum = jnp.zeros(kv_ref.shape[1:], F32)
    value_sum = jnp.zeros(kv_ref.shape[1:], F32)
    for p, text_ref in enumerate(text_refs):
        near_at = source(place_ref[0], p, pieces)
        norm = norm_ref[near_at]
        for c in range(chunks):
            q_c, g_c = chunk_of(text_ref, c, 0), chunk_of(text_ref, c, 1)
            shift, delta = norm[c : c + 1], norm[chunks + c : chunks + c + 1]
            scores = dot(kv_ref[0], q_c, NT) * (SCALE * LOG2E)
            dprobs = dot(kv_ref[1], g_c, NT)
            for f in range(FRAME_DEV):
                here, off = slice(f * rows, (f + 1) * rows), off_ref[p, c, f : f + 1, :]
                probs = jnp.exp2(scores[here] - (shift + off))
                p_scr[here] = probs.astype(BF16)
                ds_scr[here] = (probs * (dprobs[here] - delta)).astype(BF16)
            value_sum += dot(p_scr[...], g_c, NN)
            key_sum += dot(ds_scr[...], q_c, NN)
    turned = jnp.concatenate(((key_sum * SCALE).T, value_sum.T), axis=0).astype(BF16)
    part = PART
    block = pieces * part
    for b in range(vision_ref.shape[1] // block):
        if b * block % width == 0:
            copies[b * block // width].wait()
        sums = dot(turned, vision_ref[:, b * block : (b + 1) * block], NN).T.astype(BF16)
        for m in range(pieces):

            @pl.when(place_ref[0] == m)
            def _(m=m, b=b, sums=sums):
                for x in range(pieces):
                    out_ref = out_refs[(x - m) % pieces]
                    out_ref[b * part : (b + 1) * part] = sums[x * part : (x + 1) * part]


def sum_kernel(parts_ref, out_ref):
    out_ref[...] = jnp.sum(parts_ref[...], axis=0).astype(BF16)


def shards(text_queries, text_grads, vision_keys, video_value_rows, vision, lengths, frame_range):
    far, near = lax.axis_size(FAR), lax.axis_size(NEAR)
    my_far, my_near = lax.axis_index(FAR), lax.axis_index(NEAR)
    peers = far * near
    own_rows = text_queries.shape[0]
    members = text_queries.shape[1] // HEAD_WIDTH
    lines = own_rows * members
    kv_rows = vision_keys.shape[0]
    features = vision.shape[1]
    place = jnp.stack(
        [
            my_near.astype(jnp.int32),
            jnp.int32(near),
            jnp.int32(own_rows),
            jnp.int32(lines),
            (my_far * near).astype(jnp.int32),
        ]
    )
    where = (place, lengths, frame_range)

    own_text = pl.pallas_call(
        prepare_kernel,
        out_shape=jax.ShapeDtypeStruct((far, 2, lines, HEAD_WIDTH), BF16),
        in_specs=[WHOLE] * 2,
        out_specs=WHOLE,
        compiler_params=PARAMS,
    )(text_queries, text_grads)
    own_kv = jnp.stack((vision_keys, video_value_rows))
    text = lax.all_to_all(own_text, FAR, 0, 0, tiled=True)
    all_kv = [own_kv] + [shifted(own_kv, NEAR, k) for k in range(1, near)]
    chunks = far * lines // CHUNK
    part = features // peers
    assert part == PART

    stats = pl.pallas_call(
        stats_kernel,
        out_shape=jax.ShapeDtypeStruct((far, STATS_LINES, CHUNK), F32),
        in_specs=[SCALARS] * 3 + [WHOLE] * (1 + near),
        out_specs=WHOLE,
        scratch_shapes=[pltpu.VMEM((STATS_LINES, CHUNK), F32)],
        compiler_params=PARAMS,
    )(*where, text, *all_kv)
    stats, text, where = lax.optimization_barrier((stats, text, where))
    stats = lax.all_to_all(stats, FAR, 0, 0, tiled=True)
    off = pl.pallas_call(
        mask_kernel,
        out_shape=jax.ShapeDtypeStruct((near, chunks, FRAME_DEV, CHUNK), F32),
        in_specs=[SCALARS] * 3,
        out_specs=WHOLE,
        compiler_params=PARAMS,
    )(*where)
    all_text = [text] + [shifted(text, NEAR, k) for k in range(1, near)]
    norms = pl.pallas_call(
        join_kernel,
        out_shape=jax.ShapeDtypeStruct((near, 2 * chunks, CHUNK), F32),
        in_specs=[WHOLE],
        out_specs=WHOLE,
        compiler_params=PARAMS,
    )(stats)
    all_norm = lax.all_to_all(norms, NEAR, 0, 0, tiled=True)

    dq = pl.pallas_call(
        query_kernel,
        out_shape=jax.ShapeDtypeStruct((far, lines, HEAD_WIDTH), F32),
        in_specs=[SCALARS] * 3 + [WHOLE] * (2 + near),
        out_specs=WHOLE,
        scratch_shapes=[pltpu.VMEM((kv_rows, CHUNK), BF16)],
        compiler_params=PARAMS,
    )(*where, text, norms, *all_kv)
    dq, all_norm = lax.optimization_barrier((dq, all_norm))
    dq = lax.all_to_all(dq, FAR, 0, 0, tiled=True)

    sums = pl.pallas_call(
        token_kernel,
        out_shape=[jax.ShapeDtypeStruct((far * part, 2 * HEAD_WIDTH), BF16)] * near,
        in_specs=[SCALARS]
        + [WHOLE] * 3
        + [pl.BlockSpec(memory_space=pltpu.HBM)]
        + [WHOLE] * near,
        out_specs=[WHOLE] * near,
        scratch_shapes=[
            pltpu.VMEM((kv_rows, CHUNK), BF16),
            pltpu.VMEM((kv_rows, CHUNK), BF16),
            pltpu.VMEM((kv_rows, features), BF16),
            pltpu.SemaphoreType.DMA((4,)),
        ],
        compiler_params=LARGE,
        cost_estimate=HEAVY,
    )(place, off, own_kv, all_norm, vision, *all_text)

    got = [sums[0]] + [shifted(sums[k], NEAR, k) for k in range(1, near)]

    dq = pl.pallas_call(
        sum_kernel,
        out_shape=jax.ShapeDtypeStruct((lines, HEAD_WIDTH), BF16),
        in_specs=[WHOLE],
        out_specs=WHOLE,
        compiler_params=PARAMS,
        cost_estimate=HEAVY,
    )(dq)
    dq = dq.reshape(members, own_rows, HEAD_WIDTH).transpose(1, 0, 2)
    dq = from_everyone(dq.reshape(own_rows, -1), FAR).reshape(far, own_rows, -1)

    weights = sum(one.astype(F32) for one in got).astype(BF16)
    weights, dq = lax.optimization_barrier((weights, dq))
    weights = lax.all_to_all(
        weights.reshape(far, part, 2 * HEAD_WIDTH), FAR, 0, 0, tiled=True
    )
    all_dq = [dq] + [shifted(dq, NEAR, k) for k in range(1, near)]
    query_grad = jnp.stack([lax.select_n(source(my_near, k, near), *all_dq) for k in range(near)], 1)
    query_grad = query_grad.reshape(peers * own_rows, -1)
    weights = jnp.sum(weights.astype(F32), axis=0)
    return query_grad, weights[:, :HEAD_WIDTH], weights[:, HEAD_WIDTH:]


def solution(mesh):
    finer = Mesh(
        mesh.devices.reshape(2, 8, 4, mesh.shape["head"]), ("tok_0", "tok_1", "tok_2", "head")
    )
    return jax.shard_map(
        shards,
        mesh=finer,
        in_specs=(
            P(TOK, "head"),
            P(TOK, "head"),
            P(TOK, "head"),
            P(TOK, "head"),
            P(TOK, None),
            P(),
            P(),
        ),
        out_specs=(P(None, "head"), P(TOK, "head"), P(TOK, "head")),
        check_vma=False,
    )
```

time: 159 us -> 164 us (1.031)
  the two profiles are of different devices: /device:TPU:14 before, /device:TPU:10 now
where the time goes in v4:
time: 164 us; the launch traced here: 163 us
  starting transfers between devices  99.5 us (61%)
  waiting for transfers between devices  32.4 us (20%)
  Pallas kernels  20.8 us (13%)
  local copies, waits for them, and re-layouts  6.44 us (4%)
  other arithmetic  2.92 us (2%)
    ppermute x12, starting transfers between devices, shifted(): lax.ppermute(x, axis, [(i, (i + step) % peers) for i in range(peers)])  40.7 us
    ppermute x12, waiting for transfers between devices, shifted(): lax.ppermute(x, axis, [(i, (i + step) % peers) for i in range(peers)])  17.9 us
    all_to_all x1, starting transfers between devices, shards(): text = lax.all_to_all(own_text, FAR, 0, 0, tiled=True)  14.8 us
    all_to_all x1, starting transfers between devices, from_everyone(): lax.all_to_all(jnp.broadcast_to(x[None], (peers, *x.shape)), axis, 0, 0,...  12 us
    all_to_all x1, starting transfers between devices, shards(): stats = lax.all_to_all(stats, FAR, 0, 0, tiled=True)  11.7 us
    pallas_call x1, Pallas kernels, shards(): pl.pallas_call(token_kernel, out_shape=[jax.ShapeDtypeStruct((far * part,...  11.2 us
    all_to_all x1, starting transfers between devices, shards(): all_norm = lax.all_to_all(norms, NEAR, 0, 0, tiled=True)  7.19 us
    all_to_all x1, starting transfers between devices, shards(): dq = lax.all_to_all(dq, FAR, 0, 0, tiled=True)  6.96 us
  transfers between devices with their start and end apart: 18, of which 8 were waited for; matrix products, arithmetic and copies ran while one was open for 4% of the time, Pallas kernels for 10%

profile of v4, /device:TPU:10, one launch (start us, length us, event | category | flops | bytes accessed | tf_op | source)
XLA Modules:
  0.0 162.9 jit_solution(18337487954750726443)
XLA Ops:
  0.6 0.0 copy-start
  0.6 0.7 copy-done
  1.3 0.0 copy-start.1
  1.3 0.7 copy-done.1
  2.0 0.8 shard_map.94
  2.8 14.8 %all-to-all-start = ((bf16[16,2,32,128]{3,2,1,0:T(8,128)(2,1)}), bf16[16,2,32,128]{3,2,1,0:T(8,128)(2,1)S(1)}, u32[]{:S(2)}, u32[]{:S(2)}) async-start(bf16[16,2,32,128]{3,2,1,0:T(8,128)(2,1)} %shard_map.94), calls=%async_computation | async-start | bytes 524288 | tf_op jit(solution)/shard_map/all_to_all | solution.py:267
  17.6 1.0 pad_maximum_fusion.1.refs_0_.kv_ref
  18.6 2.4 %collective-permute-start.2 = (bf16[2,512,128]{2,1,0:T(8,128)(2,1)S(1)}, bf16[2,512,128]{2,1,0:T(8,128)(2,1)S(1)}, u32[]{:S(2)}, u32[]{:S(2)}) collective-permute-start(bf16[2,512,128]{2,1,0:T(8,128)(2,1)S(1)} %pad_maximum_fusion.1.refs_0_.kv_ref), channel_id=1, source_target_pairs={{0,24},{8,0},{16,8},{24,16},{1,25},{9,1},{17,9},{25,17},{2,26},{10... | collective-permute-start | bytes 786440 | tf_op jit(solution)/shard_map/ppermute | solution.py:39
  21.0 4.3 %collective-permute-start.1 = (bf16[2,512,128]{2,1,0:T(8,128)(2,1)S(1)}, bf16[2,512,128]{2,1,0:T(8,128)(2,1)S(1)}, u32[]{:S(2)}, u32[]{:S(2)}) collective-permute-start(bf16[2,512,128]{2,1,0:T(8,128)(2,1)S(1)} %pad_maximum_fusion.1.refs_0_.kv_ref), channel_id=1, source_target_pairs={{0,16},{8,24},{16,0},{24,8},{1,17},{9,25},{17,1},{25,9},{2,18},{10... | collective-permute-start | bytes 786440 | tf_op jit(solution)/shard_map/ppermute | solution.py:39
  25.4 3.7 %collective-permute-start = (bf16[2,512,128]{2,1,0:T(8,128)(2,1)S(1)}, bf16[2,512,128]{2,1,0:T(8,128)(2,1)S(1)}, u32[]{:S(2)}, u32[]{:S(2)}) collective-permute-start(bf16[2,512,128]{2,1,0:T(8,128)(2,1)S(1)} %pad_maximum_fusion.1.refs_0_.kv_ref), channel_id=1, source_target_pairs={{0,8},{8,16},{16,24},{24,0},{1,9},{9,17},{17,25},{25,1},{2,10},{10... | collective-permute-start | bytes 786440 | tf_op jit(solution)/shard_map/ppermute | solution.py:39
  29.1 0.8 copy.10.range_ref
  29.8 0.1 pad_add_fusion.place_ref
  29.9 0.0 collective-permute-done.2.refs_3_
  29.9 4.9 %collective-permute-done.1.refs_2_ = bf16[2,512,128]{2,1,0:T(8,128)(2,1)S(1)} collective-permute-done((bf16[2,512,128]{2,1,0:T(8,128)(2,1)S(1)}, bf16[2,512,128]{2,1,0:T(8,128)(2,1)S(1)}, u32[]{:S(2)}, u32[]{:S(2)}) %collective-permute-start.1) | collective-permute-done | bytes 262176 | tf_op jit(solution)/shard_map/ppermute | solution.py:39
  34.8 2.8 %collective-permute-done.refs_1_ = bf16[2,512,128]{2,1,0:T(8,128)(2,1)S(1)} collective-permute-done((bf16[2,512,128]{2,1,0:T(8,128)(2,1)S(1)}, bf16[2,512,128]{2,1,0:T(8,128)(2,1)S(1)}, u32[]{:S(2)}, u32[]{:S(2)}) %collective-permute-start) | collective-permute-done | bytes 262176 | tf_op jit(solution)/shard_map/ppermute | solution.py:39
  37.5 0.0 all-to-all-done.text_ref.refs_0_
  37.6 0.0 copy-start.2
  37.6 0.7 copy-done.2
  38.2 3.3 %shard_map.95 = f32[16,12,256]{2,1,0:T(8,128)} custom-call(s32[5]{0:T(128)S(1)} %pad_add_fusion.place_ref, s32[8]{0:T(128)S(1)} %copy-done.2, s32[8,2]{1,0:T(8,128)S(1)} %copy.10.range_ref, bf16[16,2,32,128]{3,2,1,0:T(8,128)(2,1)S(1)} %all-to-all-done.text_ref.refs_0_, bf16[2,512,128]{2,1,0:T(8,128)(2,1)S(1)} %pad_maximum_fusion.1.refs_0_.kv_ref, ...), custom_call_target="tpu_custom_call" | custom-call | tf_op jit(solution)/shard_map/pallas_call | solution.py:273
  41.5 11.7 %all-to-all-start.1 = ((f32[16,12,256]{2,1,0:T(8,128)}), f32[16,12,256]{2,1,0:T(8,128)S(1)}, u32[]{:S(2)}, u32[]{:S(2)}) async-start(f32[16,12,256]{2,1,0:T(8,128)} %shard_map.95), calls=%async_computation.1 | async-start | bytes 524288 | tf_op jit(solution)/shard_map/all_to_all | solution.py:282
  53.3 4.6 %collective-permute-start.5 = (bf16[16,2,32,128]{3,2,1,0:T(8,128)(2,1)S(1)}, bf16[16,2,32,128]{3,2,1,0:T(8,128)(2,1)S(1)}, u32[]{:S(2)}, u32[]{:S(2)}) collective-permute-start(bf16[16,2,32,128]{3,2,1,0:T(8,128)(2,1)S(1)} %all-to-all-done.text_ref.refs_0_), channel_id=1, source_target_pairs={{0,24},{8,0},{16,8},{24,16},{1,25},{9,1},{17,9},{25,17},{2,26},{10... | collective-permute-start | bytes 786440 | tf_op jit(solution)/shard_map/ppermute | solution.py:39
  57.9 2.1 %collective-permute-start.4 = (bf16[16,2,32,128]{3,2,1,0:T(8,128)(2,1)S(1)}, bf16[16,2,32,128]{3,2,1,0:T(8,128)(2,1)S(1)}, u32[]{:S(2)}, u32[]{:S(2)}) collective-permute-start(bf16[16,2,32,128]{3,2,1,0:T(8,128)(2,1)S(1)} %all-to-all-done.text_ref.refs_0_), channel_id=1, source_target_pairs={{0,16},{8,24},{16,0},{24,8},{1,17},{9,25},{17,1},{25,9},{2,18},{10... | collective-permute-start | bytes 786440 | tf_op jit(solution)/shard_map/ppermute | solution.py:39
  60.0 3.7 %collective-permute-start.3 = (bf16[16,2,32,128]{3,2,1,0:T(8,128)(2,1)S(1)}, bf16[16,2,32,128]{3,2,1,0:T(8,128)(2,1)S(1)}, u32[]{:S(2)}, u32[]{:S(2)}) collective-permute-start(bf16[16,2,32,128]{3,2,1,0:T(8,128)(2,1)S(1)} %all-to-all-done.text_ref.refs_0_), channel_id=1, source_target_pairs={{0,8},{8,16},{16,24},{24,0},{1,9},{9,17},{17,25},{25,1},{2,10},{10... | collective-permute-start | bytes 786440 | tf_op jit(solution)/shard_map/ppermute | solution.py:39
  63.8 3.3 %all-to-all-done.1.stats_ref = f32[16,12,256]{2,1,0:T(8,128)S(1)} async-done(((f32[16,12,256]{2,1,0:T(8,128)}), f32[16,12,256]{2,1,0:T(8,128)S(1)}, u32[]{:S(2)}, u32[]{:S(2)}) %all-to-all-start.1) | async-done | bytes 196640 | tf_op jit(solution)/shard_map/all_to_all | solution.py:282
  67.0 0.7 shard_map.97.copies_ref
  67.7 7.2 %all-to-all-start.2 = ((f32[4,4,256]{2,1,0:T(4,128)}), f32[4,4,256]{2,1,0:T(4,128)S(1)}, u32[]{:S(2)}, u32[]{:S(2)}) async-start(f32[4,4,256]{2,1,0:T(4,128)} %shard_map.97.copies_ref), calls=%async_computation.2 | async-start | bytes 32768 | tf_op jit(solution)/shard_map/all_to_all | solution.py:298
  74.9 0.8 copy.11.range_ref
  75.6 0.0 copy-start.3
  75.6 0.7 copy-done.3
  76.3 1.3 shard_map.96.off_ref
  77.6 3.6 %shard_map.98 = f32[16,32,128]{2,1,0:T(8,128)} custom-call(s32[5]{0:T(128)S(1)} %pad_add_fusion.place_ref, s32[8]{0:T(128)S(1)} %copy-done.3, s32[8,2]{1,0:T(8,128)S(1)} %copy.11.range_ref, bf16[16,2,32,128]{3,2,1,0:T(8,128)(2,1)S(1)} %all-to-all-done.text_ref.refs_0_, f32[4,4,256]{2,1,0:T(4,128)} %shard_map.97.copies_ref, ...), custom_call_target="tpu_custom_call" | custom-call | tf_op jit(solution)/shard_map/pallas_call | solution.py:300
  81.2 0.0 all-to-all-done.2.norm_ref
  81.2 7.0 %all-to-all-start.3 = ((f32[16,32,128]{2,1,0:T(8,128)}), f32[16,32,128]{2,1,0:T(8,128)S(1)}, u32[]{:S(2)}, u32[]{:S(2)}) async-start(f32[16,32,128]{2,1,0:T(8,128)} %shard_map.98), calls=%async_computation.3 | async-start | bytes 524288 | tf_op jit(solution)/shard_map/all_to_all | solution.py:309
  88.1 0.0 collective-permute-done.5.refs_3_
  88.1 0.0 collective-permute-done.4.refs_2_
  88.2 0.0 collective-permute-done.3.refs_1_
  88.2 11.2 %shard_map.99 = (bf16[1024,256]{1,0:T(8,128)(2,1)S(1)}, bf16[1024,256]{1,0:T(8,128)(2,1)}, bf16[1024,256]{1,0:T(8,128)(2,1)}, bf16[1024,256]{1,0:T(8,128)(2,1)}) custom-call(s32[5]{0:T(128)S(1)} %pad_add_fusion.place_ref, f32[4,2,4,256]{3,2,1,0:T(4,128)S(1)} %shard_map.96.off_ref, bf16[2,512,128]{2,1,0:T(8,128)(2,1)S(1)} %pad_maximum_fusion.1.refs_0_.kv_ref, ...), custom_call_target="tpu_custom_call" | custom-call | flops 99999997952 | bytes 1048576 | tf_op jit(solution)/shard_map/pallas_call | solution.py:311
  99.4 3.4 %collective-permute-start.6 = (bf16[1024,256]{1,0:T(8,128)(2,1)}, bf16[1024,256]{1,0:T(8,128)(2,1)S(1)}, u32[]{:S(2)}, u32[]{:S(2)}) collective-permute-start(bf16[1024,256]{1,0:T(8,128)(2,1)} %get-tuple-element.23), channel_id=1, source_target_pairs={{0,8},{8,16},{16,24},{24,0},{1,9},{9,17},{17,25},{25,1},{2,10},{10... | collective-permute-start | bytes 1572872 | tf_op jit(solution)/shard_map/ppermute | solution.py:39
  102.7 2.6 %collective-permute-start.7 = (bf16[1024,256]{1,0:T(8,128)(2,1)}, bf16[1024,256]{1,0:T(8,128)(2,1)S(1)}, u32[]{:S(2)}, u32[]{:S(2)}) collective-permute-start(bf16[1024,256]{1,0:T(8,128)(2,1)} %get-tuple-element.24), channel_id=1, source_target_pairs={{0,16},{8,24},{16,0},{24,8},{1,17},{9,25},{17,1},{25,9},{2,18},{10... | collective-permute-start | bytes 1572872 | tf_op jit(solution)/shard_map/ppermute | solution.py:39
  105.3 4.5 %collective-permute-start.8 = (bf16[1024,256]{1,0:T(8,128)(2,1)}, bf16[1024,256]{1,0:T(8,128)(2,1)S(1)}, u32[]{:S(2)}, u32[]{:S(2)}) collective-permute-start(bf16[1024,256]{1,0:T(8,128)(2,1)} %get-tuple-element.25), channel_id=1, source_target_pairs={{0,24},{8,0},{16,8},{24,16},{1,25},{9,1},{17,9},{25,17},{2,26},{10... | collective-permute-start | bytes 1572872 | tf_op jit(solution)/shard_map/ppermute | solution.py:39
  109.8 0.0 all-to-all-done.3.parts_ref
  109.8 0.7 broadcast_in_dim.8
  110.5 12.0 %all-to-all-start.4 = ((bf16[16,4,1024]{2,1,0:T(4,128)(2,1)}), bf16[16,4,1024]{2,1,0:T(4,128)(2,1)S(1)}, u32[]{:S(2)}, u32[]{:S(2)}) async-start(bf16[16,4,1024]{2,1,0:T(4,128)(2,1)} %broadcast_in_dim.8), calls=%async_computation.4 | async-start | bytes 262144 | tf_op jit(solution)/shard_map/all_to_all | solution.py:34
  122.6 0.0 collective-permute-done.6
  122.6 0.0 collective-permute-done.7
  122.6 5.9 %collective-permute-done.8 = bf16[1024,256]{1,0:T(8,128)(2,1)S(1)} collective-permute-done((bf16[1024,256]{1,0:T(8,128)(2,1)}, bf16[1024,256]{1,0:T(8,128)(2,1)S(1)}, u32[]{:S(2)}, u32[]{:S(2)}) %collective-permute-start.8) | collective-permute-done | bytes 524320 | tf_op jit(solution)/shard_map/ppermute | solution.py:39
  128.5 1.1 add_convert_fusion
  129.6 5.6 %all-to-all-done.4 = bf16[16,4,1024]{2,1,0:T(4,128)(2,1)S(1)} async-done(((bf16[16,4,1024]{2,1,0:T(4,128)(2,1)}), bf16[16,4,1024]{2,1,0:T(4,128)(2,1)S(1)}, u32[]{:S(2)}, u32[]{:S(2)}) %all-to-all-start.4) | async-done | bytes 131104 | tf_op jit(solution)/shard_map/all_to_all | solution.py:34
  135.2 6.1 %all-to-all-start.5 = ((bf16[16,64,256]{2,1,0:T(8,128)(2,1)}), bf16[16,64,256]{2,1,0:T(8,128)(2,1)S(1)}, u32[]{:S(2)}, u32[]{:S(2)}) async-start(bf16[16,64,256]{2,1,0:T(8,128)(2,1)} %bitcast.14), calls=%async_computation.5 | async-start | bytes 1048576 | tf_op jit(solution)/shard_map/all_to_all | solution.py:344
  141.3 1.9 %collective-permute-start.11 = (bf16[16,4,1024]{2,1,0:T(4,128)(2,1)S(1)}, bf16[16,4,1024]{2,1,0:T(4,128)(2,1)S(1)}, u32[]{:S(2)}, u32[]{:S(2)}) collective-permute-start(bf16[16,4,1024]{2,1,0:T(4,128)(2,1)S(1)} %all-to-all-done.4), channel_id=1, source_target_pairs={{0,24},{8,0},{16,8},{24,16},{1,25},{9,1},{17,9},{25,17},{2,26},{10... | collective-permute-start | bytes 393224 | tf_op jit(solution)/shard_map/ppermute | solution.py:39
  143.3 4.0 %collective-permute-start.10 = (bf16[16,4,1024]{2,1,0:T(4,128)(2,1)S(1)}, bf16[16,4,1024]{2,1,0:T(4,128)(2,1)S(1)}, u32[]{:S(2)}, u32[]{:S(2)}) collective-permute-start(bf16[16,4,1024]{2,1,0:T(4,128)(2,1)S(1)} %all-to-all-done.4), channel_id=1, source_target_pairs={{0,16},{8,24},{16,0},{24,8},{1,17},{9,25},{17,1},{25,9},{2,18},{10... | collective-permute-start | bytes 393224 | tf_op jit(solution)/shard_map/ppermute | solution.py:39
  147.2 3.4 %collective-permute-start.9 = (bf16[16,4,1024]{2,1,0:T(4,128)(2,1)S(1)}, bf16[16,4,1024]{2,1,0:T(4,128)(2,1)S(1)}, u32[]{:S(2)}, u32[]{:S(2)}) collective-permute-start(bf16[16,4,1024]{2,1,0:T(4,128)(2,1)S(1)} %all-to-all-done.4), channel_id=1, source_target_pairs={{0,8},{8,16},{16,24},{24,0},{1,9},{9,17},{17,25},{25,1},{2,10},{10... | collective-permute-start | bytes 393224 | tf_op jit(solution)/shard_map/ppermute | solution.py:39
  150.7 0.0 collective-permute-done.11
  150.7 1.1 collective-permute-done.10
  151.8 3.2 %collective-permute-done.9 = bf16[16,4,1024]{2,1,0:T(4,128)(2,1)S(1)} collective-permute-done((bf16[16,4,1024]{2,1,0:T(4,128)(2,1)S(1)}, bf16[16,4,1024]{2,1,0:T(4,128)(2,1)S(1)}, u32[]{:S(2)}, u32[]{:S(2)}) %collective-permute-start.9) | collective-permute-done | bytes 131104 | tf_op jit(solution)/shard_map/ppermute | solution.py:39
  155.0 0.3 select_bitcast_fusion.3
  155.3 0.4 pad_maximum_fusion
  155.7 0.9 reshape.17
  156.6 5.6 %all-to-all-done.5 = bf16[16,64,256]{2,1,0:T(8,128)(2,1)S(1)} async-done(((bf16[16,64,256]{2,1,0:T(8,128)(2,1)}), bf16[16,64,256]{2,1,0:T(8,128)(2,1)S(1)}, u32[]{:S(2)}, u32[]{:S(2)}) %all-to-all-start.5) | async-done | bytes 524320 | tf_op jit(solution)/shard_map/all_to_all | solution.py:344
  162.2 0.1 convert_reduce_fusion
  162.3 0.6 fusion
  (2 shorter events, 0.0 us)
Async XLA Ops:
  0.6 0.7 copy-start
  1.3 0.7 copy-start.1
  2.8 34.8 %all-to-all-start = ((bf16[16,2,32,128]{3,2,1,0:T(8,128)(2,1)}), bf16[16,2,32,128]{3,2,1,0:T(8,128)(2,1)S(1)}, u32[]{:S(2)}, u32[]{:S(2)}) async-start(bf16[16,2,32,128]{3,2,1,0:T(8,128)(2,1)} %shard_map.94), calls=%async_computation | async-start | bytes 524288 | tf_op jit(solution)/shard_map/all_to_all | solution.py:267
  18.6 11.4 %collective-permute-start.2 = (bf16[2,512,128]{2,1,0:T(8,128)(2,1)S(1)}, bf16[2,512,128]{2,1,0:T(8,128)(2,1)S(1)}, u32[]{:S(2)}, u32[]{:S(2)}) collective-permute-start(bf16[2,512,128]{2,1,0:T(8,128)(2,1)S(1)} %pad_maximum_fusion.1.refs_0_.kv_ref), channel_id=1, source_target_pairs={{0,24},{8,0},{16,8},{24,16},{1,25},{9,1},{17,9},{25,17},{2,26},{10... | collective-permute-start | bytes 786440 | tf_op jit(solution)/shard_map/ppermute | solution.py:39
  21.0 13.8 %collective-permute-start.1 = (bf16[2,512,128]{2,1,0:T(8,128)(2,1)S(1)}, bf16[2,512,128]{2,1,0:T(8,128)(2,1)S(1)}, u32[]{:S(2)}, u32[]{:S(2)}) collective-permute-start(bf16[2,512,128]{2,1,0:T(8,128)(2,1)S(1)} %pad_maximum_fusion.1.refs_0_.kv_ref), channel_id=1, source_target_pairs={{0,16},{8,24},{16,0},{24,8},{1,17},{9,25},{17,1},{25,9},{2,18},{10... | collective-permute-start | bytes 786440 | tf_op jit(solution)/shard_map/ppermute | solution.py:39
  25.4 12.2 %collective-permute-start = (bf16[2,512,128]{2,1,0:T(8,128)(2,1)S(1)}, bf16[2,512,128]{2,1,0:T(8,128)(2,1)S(1)}, u32[]{:S(2)}, u32[]{:S(2)}) collective-permute-start(bf16[2,512,128]{2,1,0:T(8,128)(2,1)S(1)} %pad_maximum_fusion.1.refs_0_.kv_ref), channel_id=1, source_target_pairs={{0,8},{8,16},{16,24},{24,0},{1,9},{9,17},{17,25},{25,1},{2,10},{10... | collective-permute-start | bytes 786440 | tf_op jit(solution)/shard_map/ppermute | solution.py:39
  37.6 0.7 copy-start.2
  41.5 25.5 %all-to-all-start.1 = ((f32[16,12,256]{2,1,0:T(8,128)}), f32[16,12,256]{2,1,0:T(8,128)S(1)}, u32[]{:S(2)}, u32[]{:S(2)}) async-start(f32[16,12,256]{2,1,0:T(8,128)} %shard_map.95), calls=%async_computation.1 | async-start | bytes 524288 | tf_op jit(solution)/shard_map/all_to_all | solution.py:282
  53.3 34.9 %collective-permute-start.5 = (bf16[16,2,32,128]{3,2,1,0:T(8,128)(2,1)S(1)}, bf16[16,2,32,128]{3,2,1,0:T(8,128)(2,1)S(1)}, u32[]{:S(2)}, u32[]{:S(2)}) collective-permute-start(bf16[16,2,32,128]{3,2,1,0:T(8,128)(2,1)S(1)} %all-to-all-done.text_ref.refs_0_), channel_id=1, source_target_pairs={{0,24},{8,0},{16,8},{24,16},{1,25},{9,1},{17,9},{25,17},{2,26},{10... | collective-permute-start | bytes 786440 | tf_op jit(solution)/shard_map/ppermute | solution.py:39
  57.9 30.2 %collective-permute-start.4 = (bf16[16,2,32,128]{3,2,1,0:T(8,128)(2,1)S(1)}, bf16[16,2,32,128]{3,2,1,0:T(8,128)(2,1)S(1)}, u32[]{:S(2)}, u32[]{:S(2)}) collective-permute-start(bf16[16,2,32,128]{3,2,1,0:T(8,128)(2,1)S(1)} %all-to-all-done.text_ref.refs_0_), channel_id=1, source_target_pairs={{0,16},{8,24},{16,0},{24,8},{1,17},{9,25},{17,1},{25,9},{2,18},{10... | collective-permute-start | bytes 786440 | tf_op jit(solution)/shard_map/ppermute | solution.py:39
  60.0 28.2 %collective-permute-start.3 = (bf16[16,2,32,128]{3,2,1,0:T(8,128)(2,1)S(1)}, bf16[16,2,32,128]{3,2,1,0:T(8,128)(2,1)S(1)}, u32[]{:S(2)}, u32[]{:S(2)}) collective-permute-start(bf16[16,2,32,128]{3,2,1,0:T(8,128)(2,1)S(1)} %all-to-all-done.text_ref.refs_0_), channel_id=1, source_target_pairs={{0,8},{8,16},{16,24},{24,0},{1,9},{9,17},{17,25},{25,1},{2,10},{10... | collective-permute-start | bytes 786440 | tf_op jit(solution)/shard_map/ppermute | solution.py:39
  67.7 13.5 %all-to-all-start.2 = ((f32[4,4,256]{2,1,0:T(4,128)}), f32[4,4,256]{2,1,0:T(4,128)S(1)}, u32[]{:S(2)}, u32[]{:S(2)}) async-start(f32[4,4,256]{2,1,0:T(4,128)} %shard_map.97.copies_ref), calls=%async_computation.2 | async-start | bytes 32768 | tf_op jit(solution)/shard_map/all_to_all | solution.py:298
  75.6 0.7 copy-start.3
  81.2 28.7 %all-to-all-start.3 = ((f32[16,32,128]{2,1,0:T(8,128)}), f32[16,32,128]{2,1,0:T(8,128)S(1)}, u32[]{:S(2)}, u32[]{:S(2)}) async-start(f32[16,32,128]{2,1,0:T(8,128)} %shard_map.98), calls=%async_computation.3 | async-start | bytes 524288 | tf_op jit(solution)/shard_map/all_to_all | solution.py:309
  99.4 23.2 %collective-permute-start.6 = (bf16[1024,256]{1,0:T(8,128)(2,1)}, bf16[1024,256]{1,0:T(8,128)(2,1)S(1)}, u32[]{:S(2)}, u32[]{:S(2)}) collective-permute-start(bf16[1024,256]{1,0:T(8,128)(2,1)} %get-tuple-element.23), channel_id=1, source_target_pairs={{0,8},{8,16},{16,24},{24,0},{1,9},{9,17},{17,25},{25,1},{2,10},{10... | collective-permute-start | bytes 1572872 | tf_op jit(solution)/shard_map/ppermute | solution.py:39
  102.7 19.8 %collective-permute-start.7 = (bf16[1024,256]{1,0:T(8,128)(2,1)}, bf16[1024,256]{1,0:T(8,128)(2,1)S(1)}, u32[]{:S(2)}, u32[]{:S(2)}) collective-permute-start(bf16[1024,256]{1,0:T(8,128)(2,1)} %get-tuple-element.24), channel_id=1, source_target_pairs={{0,16},{8,24},{16,0},{24,8},{1,17},{9,25},{17,1},{25,9},{2,18},{10... | collective-permute-start | bytes 1572872 | tf_op jit(solution)/shard_map/ppermute | solution.py:39
  105.3 23.2 %collective-permute-start.8 = (bf16[1024,256]{1,0:T(8,128)(2,1)}, bf16[1024,256]{1,0:T(8,128)(2,1)S(1)}, u32[]{:S(2)}, u32[]{:S(2)}) collective-permute-start(bf16[1024,256]{1,0:T(8,128)(2,1)} %get-tuple-element.25), channel_id=1, source_target_pairs={{0,24},{8,0},{16,8},{24,16},{1,25},{9,1},{17,9},{25,17},{2,26},{10... | collective-permute-start | bytes 1572872 | tf_op jit(solution)/shard_map/ppermute | solution.py:39
  110.5 24.7 %all-to-all-start.4 = ((bf16[16,4,1024]{2,1,0:T(4,128)(2,1)}), bf16[16,4,1024]{2,1,0:T(4,128)(2,1)S(1)}, u32[]{:S(2)}, u32[]{:S(2)}) async-start(bf16[16,4,1024]{2,1,0:T(4,128)(2,1)} %broadcast_in_dim.8), calls=%async_computation.4 | async-start | bytes 262144 | tf_op jit(solution)/shard_map/all_to_all | solution.py:34
  135.2 27.0 %all-to-all-start.5 = ((bf16[16,64,256]{2,1,0:T(8,128)(2,1)}), bf16[16,64,256]{2,1,0:T(8,128)(2,1)S(1)}, u32[]{:S(2)}, u32[]{:S(2)}) async-start(bf16[16,64,256]{2,1,0:T(8,128)(2,1)} %bitcast.14), calls=%async_computation.5 | async-start | bytes 1048576 | tf_op jit(solution)/shard_map/all_to_all | solution.py:344
  141.3 9.4 %collective-permute-start.11 = (bf16[16,4,1024]{2,1,0:T(4,128)(2,1)S(1)}, bf16[16,4,1024]{2,1,0:T(4,128)(2,1)S(1)}, u32[]{:S(2)}, u32[]{:S(2)}) collective-permute-start(bf16[16,4,1024]{2,1,0:T(4,128)(2,1)S(1)} %all-to-all-done.4), channel_id=1, source_target_pairs={{0,24},{8,0},{16,8},{24,16},{1,25},{9,1},{17,9},{25,17},{2,26},{10... | collective-permute-start | bytes 393224 | tf_op jit(solution)/shard_map/ppermute | solution.py:39
  143.3 8.5 %collective-permute-start.10 = (bf16[16,4,1024]{2,1,0:T(4,128)(2,1)S(1)}, bf16[16,4,1024]{2,1,0:T(4,128)(2,1)S(1)}, u32[]{:S(2)}, u32[]{:S(2)}) collective-permute-start(bf16[16,4,1024]{2,1,0:T(4,128)(2,1)S(1)} %all-to-all-done.4), channel_id=1, source_target_pairs={{0,16},{8,24},{16,0},{24,8},{1,17},{9,25},{17,1},{25,9},{2,18},{10... | collective-permute-start | bytes 393224 | tf_op jit(solution)/shard_map/ppermute | solution.py:39
  147.2 7.8 %collective-permute-start.9 = (bf16[16,4,1024]{2,1,0:T(4,128)(2,1)S(1)}, bf16[16,4,1024]{2,1,0:T(4,128)(2,1)S(1)}, u32[]{:S(2)}, u32[]{:S(2)}) collective-permute-start(bf16[16,4,1024]{2,1,0:T(4,128)(2,1)S(1)} %all-to-all-done.4), channel_id=1, source_target_pairs={{0,8},{8,16},{16,24},{24,0},{1,9},{9,17},{17,25},{25,1},{2,10},{10... | collective-permute-start | bytes 393224 | tf_op jit(solution)/shard_map/ppermute | solution.py:39

commit v5 on v4

v5 whole, which is shorter than its diff:
```python
import jax
import jax.numpy as jnp
from jax import lax
from jax.experimental import pallas as pl
from jax.experimental.pallas import tpu as pltpu
from jax.sharding import Mesh
from jax.sharding import PartitionSpec as P

HEAD_WIDTH = 128
FRAME_DEV = 4
TOK = ("tok_0", "tok_1", "tok_2")
FAR = ("tok_0", "tok_1")
NEAR = "tok_2"
CHUNK = 256
SCALE = HEAD_WIDTH**-0.5
LOG2E = 1.4426950408889634
OFF = 1e30
LOW = -1e29
F32 = jnp.float32
BF16 = jnp.bfloat16
NT = (((1,), (1,)), ((), ()))
NN = (((1,), (0,)), ((), ()))
PARAMS = pltpu.CompilerParams(vmem_limit_bytes=32 * 2**20)
LARGE = pltpu.CompilerParams(vmem_limit_bytes=52 * 2**20)
LARGER = pltpu.CompilerParams(vmem_limit_bytes=58 * 2**20)
WHOLE = pl.BlockSpec(memory_space=pltpu.VMEM)
SCALARS = pl.BlockSpec(memory_space=pltpu.SMEM)


def shifted(x, axis, step):
    peers = lax.axis_size(axis)
    return lax.ppermute(x, axis, [(i, (i + step) % peers) for i in range(peers)])


def dot(a, b, dims):
    return lax.dot_general(a, b, dims, preferred_element_type=F32)


def chunk_of(text_ref, near_at, c, which):
    per = CHUNK // text_ref.shape[3]
    return text_ref[c * per : (c + 1) * per, near_at, which].reshape(CHUNK, HEAD_WIDTH)


def row_bounds(place_ref, lengths_ref, range_ref, near_at, c):
    near, own_rows, lines = place_ref[1], place_ref[2], place_ref[3]
    line = lax.broadcasted_iota(jnp.int32, (1, CHUNK), 1) + c * CHUNK
    row = (lax.div(line, lines) * near + near_at) * own_rows + lax.rem(line, own_rows)
    begin = jnp.zeros((1, CHUNK), jnp.int32)
    end = jnp.zeros((1, CHUNK), jnp.int32)
    at = jnp.int32(0)
    for k in range(lengths_ref.shape[0]):
        stop = at + lengths_ref[k]
        inside = (row >= at) & (row < stop)
        begin = jnp.where(inside, range_ref[k, 0], begin)
        end = jnp.where(inside, range_ref[k, 1], end)
        at = stop
    return begin, end


def frame_offs(bounds, first):
    begin, end = bounds
    for f in range(FRAME_DEV):
        allowed = (begin <= first + f) & (end > first + f)
        yield jnp.where(allowed, 0.0, OFF).astype(F32)


def frame_slices(off_ref, rows):
    for f in range(FRAME_DEV):
        yield slice(f * rows, (f + 1) * rows), off_ref[f : f + 1, :]


def source(near_at, piece, near):
    return lax.rem(near_at + (near - piece), jnp.int32(near))


def join(parts):
    top = parts[0][0]
    for part in parts[1:]:
        top = jnp.maximum(top, part[0])
    total = jnp.zeros_like(top)
    weighted = jnp.zeros_like(top)
    for part in parts:
        factor = jnp.exp2(part[0] - top)
        total += part[1] * factor
        weighted += part[2] * factor
    return top, total, weighted


def piece_stats(q_c, g_c, kv_ref, off_ref):
    rows = kv_ref.shape[1] // FRAME_DEV
    scores = dot(kv_ref[0], q_c, NT) * (SCALE * LOG2E)
    dprobs = dot(kv_ref[1], g_c, NT)
    top = jnp.full((1, CHUNK), LOW, F32)
    for here, off in frame_slices(off_ref, rows):
        top = jnp.maximum(top, jnp.max(scores[here], axis=0, keepdims=True) - off)
    total = jnp.zeros((1, CHUNK), F32)
    weighted = jnp.zeros((1, CHUNK), F32)
    for here, off in frame_slices(off_ref, rows):
        terms = jnp.exp2(scores[here] - (top + off))
        total += jnp.sum(terms, axis=0, keepdims=True)
        weighted += jnp.sum(terms * dprobs[here], axis=0, keepdims=True)
    return top, total, weighted


def prepare_kernel(q_ref, g_ref, text_ref):
    members = q_ref.shape[1] // HEAD_WIDTH
    for which, ref in enumerate((q_ref, g_ref)):
        rows = ref[...].astype(F32)
        lines = jnp.concatenate(
            [rows[:, m * HEAD_WIDTH : (m + 1) * HEAD_WIDTH] for m in range(members)], axis=0
        ).astype(BF16)
        for k in range(text_ref.shape[0]):
            text_ref[k, which] = lines


def mask_kernel(place_ref, lengths_ref, range_ref, own_ref, all_ref):
    near, chunks = all_ref.shape[:2]
    base = place_ref[4]
    for c in range(chunks):
        bounds = row_bounds(place_ref, lengths_ref, range_ref, place_ref[0], c)
        for p in range(near):
            first = (base + source(place_ref[0], p, near)) * FRAME_DEV
            for f, off in enumerate(frame_offs(bounds, first)):
                own_ref[c, p, f : f + 1, :] = off
        for p in range(near):
            bounds = row_bounds(place_ref, lengths_ref, range_ref, p, c)
            first = (base + place_ref[0]) * FRAME_DEV
            for f, off in enumerate(frame_offs(bounds, first)):
                all_ref[p, c, f : f + 1, :] = off


def turn_kernel(vision_ref, out_ref):
    size = 256
    for at in range(0, out_ref.shape[0], size):
        out_ref[at : at + size] = vision_ref[:, at : at + size].T


def stats_kernel(place_ref, text_ref, off_ref, *refs):
    kv_refs, all_ref, stats_scr = refs[:-2], refs[-2], refs[-1]
    chunks = stats_scr.shape[0] // 3
    for c in range(chunks):
        q_c = chunk_of(text_ref, place_ref[0], c, 0)
        g_c = chunk_of(text_ref, place_ref[0], c, 1)
        parts = [
            piece_stats(q_c, g_c, kv_ref, off_ref.at[c, p]) for p, kv_ref in enumerate(kv_refs)
        ]
        for k, part in enumerate(join(parts)):
            stats_scr[k * chunks + c : k * chunks + c + 1, :] = part
    stats = stats_scr[...]
    for k in range(all_ref.shape[0]):
        all_ref[k] = stats


def join_kernel(stats_ref, out_ref):
    lines = stats_ref.shape[2] // 3
    for p in range(out_ref.shape[0]):
        parts = [
            [stats_ref[k, p, j * lines : (j + 1) * lines] for j in range(3)]
            for k in range(stats_ref.shape[0])
        ]
        top, total, weighted = join(parts)
        out_ref[p, :lines] = top + jnp.log2(total)
        out_ref[p, lines:] = weighted / total


def query_kernel(place_ref, text_ref, off_ref, norm_ref, *refs):
    kv_refs, dq_ref, ds_scr = refs[:-2], refs[-2], refs[-1]
    norm = norm_ref[place_ref[0]]
    chunks = norm.shape[0] // 2
    for c in range(chunks):
        q_c = chunk_of(text_ref, place_ref[0], c, 0)
        g_c = chunk_of(text_ref, place_ref[0], c, 1)
        shift, delta = norm[c : c + 1], norm[chunks + c : chunks + c + 1]
        dq = jnp.zeros((HEAD_WIDTH, CHUNK), F32)
        for p, kv_ref in enumerate(kv_refs):
            rows = kv_ref.shape[1] // FRAME_DEV
            scores = dot(kv_ref[0], q_c, NT) * (SCALE * LOG2E)
            dprobs = dot(kv_ref[1], g_c, NT)
            for here, off in frame_slices(off_ref.at[c, p], rows):
                probs = jnp.exp2(scores[here] - (shift + off))
                ds_scr[here] = (probs * (dprobs[here] - delta)).astype(BF16)
            dq += dot(kv_ref[0].T, ds_scr[...], NN)
        dq_ref[c * CHUNK : (c + 1) * CHUNK] = (dq * SCALE).T


def token_kernel(text_ref, off_ref, kv_ref, norm_ref, far_vision_ref, out_ref, *refs):
    p_scr, ds_scr, kv_scr, vision_ref, vision_sem = refs
    parts = vision_sem.shape[0]
    size = vision_ref.shape[0] // parts
    copies = [
        pltpu.make_async_copy(
            far_vision_ref.at[p * size : (p + 1) * size],
            vision_ref.at[p * size : (p + 1) * size],
            vision_sem.at[p],
        )
        for p in range(parts)
    ]
    for copy in copies:
        copy.start()
    pieces, chunks = off_ref.shape[:2]
    rows = kv_ref.shape[1] // FRAME_DEV
    key_sum = jnp.zeros(kv_ref.shape[1:], F32)
    value_sum = jnp.zeros(kv_ref.shape[1:], F32)
    for p in range(pieces):
        for c in range(chunks):
            q_c, g_c = chunk_of(text_ref, p, c, 0), chunk_of(text_ref, p, c, 1)
            shift = norm_ref[p, c : c + 1, :]
            delta = norm_ref[p, chunks + c : chunks + c + 1, :]
            scores = dot(kv_ref[0], q_c, NT) * (SCALE * LOG2E)
            dprobs = dot(kv_ref[1], g_c, NT)
            for here, off in frame_slices(off_ref.at[p, c], rows):
                probs = jnp.exp2(scores[here] - (shift + off))
                p_scr[here] = probs.astype(BF16)
                ds_scr[here] = (probs * (dprobs[here] - delta)).astype(BF16)
            value_sum += dot(p_scr[...], g_c, NN)
            key_sum += dot(ds_scr[...], q_c, NN)
    kv_scr[:, :HEAD_WIDTH] = (key_sum * SCALE).astype(BF16)
    kv_scr[:, HEAD_WIDTH:] = value_sum.astype(BF16)
    block = 512
    for at in range(0, out_ref.shape[0], block):
        if at % size == 0:
            copies[at // size].wait()
        out_ref[at : at + block] = dot(vision_ref[at : at + block], kv_scr[...], NN).astype(BF16)


def partner_sum(x, axis, step, kind):
    peers = lax.axis_size(axis)
    sent = x.astype(kind)
    got = lax.ppermute(sent, axis, [(i, i ^ step) for i in range(peers)])
    return sent.astype(F32) + got.astype(F32)


def shards(text_queries, text_grads, vision_keys, video_value_rows, vision, lengths, frame_range):
    far, near = lax.axis_size(FAR), lax.axis_size(NEAR)
    my_far, my_near = lax.axis_index(FAR), lax.axis_index(NEAR)
    peers = far * near
    own_rows = text_queries.shape[0]
    members = text_queries.shape[1] // HEAD_WIDTH
    lines = own_rows * members
    kv_rows = vision_keys.shape[0]
    features = vision.shape[1]
    place = jnp.stack(
        [
            my_near.astype(jnp.int32),
            jnp.int32(near),
            jnp.int32(own_rows),
            jnp.int32(lines),
            (my_far * near).astype(jnp.int32),
        ]
    )
    chunks = far * lines // CHUNK
    own_text = pl.pallas_call(
        prepare_kernel,
        out_shape=jax.ShapeDtypeStruct((peers, 2, lines, HEAD_WIDTH), BF16),
        in_specs=[WHOLE] * 2,
        out_specs=WHOLE,
        compiler_params=PARAMS,
    )(text_queries, text_grads)
    text = lax.all_to_all(own_text, TOK, 0, 0, tiled=True)
    text = text.reshape(far, near, 2, lines, HEAD_WIDTH)
    own_kv = jnp.stack((vision_keys, video_value_rows))
    all_kv = [own_kv] + [shifted(own_kv, NEAR, k) for k in range(1, near)]

    own_off, all_off = pl.pallas_call(
        mask_kernel,
        out_shape=(
            jax.ShapeDtypeStruct((chunks, near, FRAME_DEV, CHUNK), F32),
            jax.ShapeDtypeStruct((near, chunks, FRAME_DEV, CHUNK), F32),
        ),
        in_specs=[SCALARS] * 3,
        out_specs=(WHOLE, WHOLE),
        compiler_params=PARAMS,
    )(place, lengths, frame_range)
    turned = pl.pallas_call(
        turn_kernel,
        out_shape=jax.ShapeDtypeStruct((features, kv_rows), BF16),
        grid=(4,),
        in_specs=[pl.BlockSpec((kv_rows, features // 4), lambda i: (0, i))],
        out_specs=pl.BlockSpec((features // 4, kv_rows), lambda i: (i, 0)),
        compiler_params=LARGER,
    )(vision)
    text, turned, all_off = lax.optimization_barrier((text, turned, all_off))

    stats = pl.pallas_call(
        stats_kernel,
        out_shape=jax.ShapeDtypeStruct((peers, 3 * chunks, CHUNK), F32),
        in_specs=[SCALARS] + [WHOLE] * (2 + near),
        out_specs=WHOLE,
        scratch_shapes=[pltpu.VMEM((3 * chunks, CHUNK), F32)],
        compiler_params=PARAMS,
    )(place, text, own_off, *all_kv)
    stats = lax.all_to_all(stats, TOK, 0, 0, tiled=True)
    norm = pl.pallas_call(
        join_kernel,
        out_shape=jax.ShapeDtypeStruct((near, 2 * chunks, CHUNK), F32),
        in_specs=[WHOLE],
        out_specs=WHOLE,
        compiler_params=PARAMS,
    )(stats.reshape(far, near, 3 * chunks, CHUNK))

    sums = pl.pallas_call(
        token_kernel,
        out_shape=jax.ShapeDtypeStruct((features, 2 * HEAD_WIDTH), BF16),
        in_specs=[WHOLE] * 4 + [pl.BlockSpec(memory_space=pltpu.HBM)],
        out_specs=WHOLE,
        scratch_shapes=[
            pltpu.VMEM((kv_rows, CHUNK), BF16),
            pltpu.VMEM((kv_rows, CHUNK), BF16),
            pltpu.VMEM((kv_rows, 2 * HEAD_WIDTH), BF16),
            pltpu.VMEM((features, kv_rows), BF16),
            pltpu.SemaphoreType.DMA((4,)),
        ],
        compiler_params=LARGE,
    )(text, all_off, own_kv, norm, turned)
    sums, norm = lax.optimization_barrier((sums, norm))
    weights = lax.all_to_all(
        sums.reshape(peers, features // peers, 2 * HEAD_WIDTH), TOK, 0, 0, tiled=True
    )
    weights = jnp.sum(weights.astype(F32), axis=0)

    dq = pl.pallas_call(
        query_kernel,
        out_shape=jax.ShapeDtypeStruct((far * lines, HEAD_WIDTH), F32),
        in_specs=[SCALARS] + [WHOLE] * (3 + near),
        out_specs=WHOLE,
        scratch_shapes=[pltpu.VMEM((kv_rows, CHUNK), BF16)],
        compiler_params=PARAMS,
    )(place, text, own_off, norm, *all_kv)
    dq = partner_sum(dq, "tok_1", 1, F32)
    dq = partner_sum(dq, "tok_1", 2, BF16)
    dq = partner_sum(dq, "tok_1", 4, BF16)
    dq = partner_sum(dq, "tok_0", 1, BF16)
    dq = dq.astype(BF16).reshape(far, members, own_rows, HEAD_WIDTH)
    dq = dq.transpose(0, 2, 1, 3).reshape(far, own_rows, members * HEAD_WIDTH)
    all_dq = [dq] + [shifted(dq, NEAR, k) for k in range(1, near)]
    query_grad = jnp.stack(
        [lax.select_n(source(my_near, k, near), *all_dq) for k in range(near)], 1
    )
    query_grad = query_grad.reshape(peers * own_rows, -1)
    return query_grad, weights[:, :HEAD_WIDTH], weights[:, HEAD_WIDTH:]


def solution(mesh):
    finer = Mesh(
        mesh.devices.reshape(2, 8, 4, mesh.shape["head"]), ("tok_0", "tok_1", "tok_2", "head")
    )
    return jax.shard_map(
        shards,
        mesh=finer,
        in_specs=(
            P(TOK, "head"),
            P(TOK, "head"),
            P(TOK, "head"),
            P(TOK, "head"),
            P(TOK, None),
            P(),
            P(),
        ),
        out_specs=(P(None, "head"), P(TOK, "head"), P(TOK, "head")),
        check_vma=False,
    )
```

time: 164 us -> 210 us (1.28)
  the two profiles are of different devices: /device:TPU:10 before, /device:TPU:22 now
where the time goes in v5:
time: 210 us; the launch traced here: 209 us
  waiting for transfers between devices  77.4 us (37%)
  starting transfers between devices  72.2 us (34%)
  blocking collectives  31.7 us (15%)
  Pallas kernels  19.7 us (9%)
  other arithmetic  3.84 us (2%)
  local copies, waits for them, and re-layouts  3.69 us (2%)
    ppermute x4, waiting for transfers between devices, partner_sum(): got = lax.ppermute(sent, axis, [(i, i ^ step) for i in range(peers)])  55.2 us
    all_to_all x1, blocking collectives, shards(): stats = lax.all_to_all(stats, TOK, 0, 0, tiled=True)  31.7 us
    ppermute x4, starting transfers between devices, partner_sum(): got = lax.ppermute(sent, axis, [(i, i ^ step) for i in range(peers)])  29.1 us
    ppermute x6, starting transfers between devices, shifted(): lax.ppermute(x, axis, [(i, (i + step) % peers) for i in range(peers)])  19.7 us
    all_to_all x1, starting transfers between devices, shards(): text = lax.all_to_all(own_text, TOK, 0, 0, tiled=True)  17.3 us
    all_to_all x1, waiting for transfers between devices, shards(): text = lax.all_to_all(own_text, TOK, 0, 0, tiled=True)  16.1 us
    pallas_call x1, Pallas kernels, shards(): pl.pallas_call(token_kernel, out_shape=jax.ShapeDtypeStruct((features, 2...  6.55 us
    all_to_all x1, starting transfers between devices, shards(): lax.all_to_all(sums.reshape(peers, features // peers, 2 * HEAD_WIDTH), TO...  6.24 us
  transfers between devices with their start and end apart: 12, of which 7 were waited for; matrix products, arithmetic and copies ran while one was open for 2% of the time, Pallas kernels for 4%

profile of v5, /device:TPU:22, one launch (start us, length us, event | category | flops | bytes accessed | tf_op | source)
XLA Modules:
  0.0 209.4 jit_solution(861521343214384623)
XLA Ops:
  0.6 0.0 copy-start
  0.6 0.7 copy-done
  1.3 0.0 copy-start.1
  1.3 0.7 copy-done.1
  2.0 1.2 shard_map.94
  3.3 17.3 %all-to-all-start = ((bf16[64,2,32,128]{3,2,1,0:T(8,128)(2,1)}), bf16[64,2,32,128]{3,2,1,0:T(8,128)(2,1)S(1)}, u32[]{:S(2)}, u32[]{:S(2)}) async-start(bf16[64,2,32,128]{3,2,1,0:T(8,128)(2,1)} %shard_map.94), calls=%async_computation | async-start | bytes 2097152 | tf_op jit(solution)/shard_map/all_to_all | solution.py:259
  20.5 1.0 pad_maximum_fusion.1.refs_0_.kv_ref
  21.5 2.4 %collective-permute-start = (bf16[2,512,128]{2,1,0:T(8,128)(2,1)S(1)}, bf16[2,512,128]{2,1,0:T(8,128)(2,1)S(1)}, u32[]{:S(2)}, u32[]{:S(2)}) collective-permute-start(bf16[2,512,128]{2,1,0:T(8,128)(2,1)S(1)} %pad_maximum_fusion.1.refs_0_.kv_ref), channel_id=1, source_target_pairs={{0,8},{8,16},{16,24},{24,0},{1,9},{9,17},{17,25},{25,1},{2,10},{10... | collective-permute-start | bytes 786440 | tf_op jit(solution)/shard_map/ppermute | solution.py:32
  23.9 4.4 %collective-permute-start.1 = (bf16[2,512,128]{2,1,0:T(8,128)(2,1)S(1)}, bf16[2,512,128]{2,1,0:T(8,128)(2,1)S(1)}, u32[]{:S(2)}, u32[]{:S(2)}) collective-permute-start(bf16[2,512,128]{2,1,0:T(8,128)(2,1)S(1)} %pad_maximum_fusion.1.refs_0_.kv_ref), channel_id=1, source_target_pairs={{0,16},{8,24},{16,0},{24,8},{1,17},{9,25},{17,1},{25,9},{2,18},{10... | collective-permute-start | bytes 786440 | tf_op jit(solution)/shard_map/ppermute | solution.py:32
  28.3 1.9 collective-permute-start.2
  30.2 0.8 copy.10.range_ref
  31.0 0.0 copy-start.2
  31.0 5.3 %shard_map.95.far_vision_ref = bf16[4096,512]{1,0:T(8,128)(2,1)} custom-call(bf16[512,4096]{1,0:T(8,128)(2,1)} %vision_ref.1), custom_call_target="tpu_custom_call" | custom-call | tf_op jit(solution)/shard_map/pallas_call | solution.py:274
  36.3 0.1 pad_add_fusion.place_ref
  36.3 0.0 copy-done.2
  36.3 1.6 shard_map.96
  37.9 16.1 %all-to-all-done = bf16[64,2,32,128]{3,2,1,0:T(8,128)(2,1)S(1)} async-done(((bf16[64,2,32,128]{3,2,1,0:T(8,128)(2,1)}), bf16[64,2,32,128]{3,2,1,0:T(8,128)(2,1)S(1)}, u32[]{:S(2)}, u32[]{:S(2)}) %all-to-all-start) | async-done | bytes 1048608 | tf_op jit(solution)/shard_map/all_to_all | solution.py:259
  54.0 0.0 collective-permute-done.refs_1_
  54.0 0.0 collective-permute-done.1.refs_2_
  54.0 0.0 collective-permute-done.2.refs_3_
  54.0 2.4 %shard_map.97 = f32[64,6,256]{2,1,0:T(8,128)S(1)} custom-call(s32[5]{0:T(128)S(1)} %pad_add_fusion.place_ref, bf16[16,4,2,32,128]{4,3,2,1,0:T(8,128)(2,1)S(1)} %bitcast.26, f32[2,4,4,256]{3,2,1,0:T(4,128)S(1)} %get-tuple-element.12.off_ref, bf16[2,512,128]{2,1,0:T(8,128)(2,1)S(1)} %pad_maximum_fusion.1.refs_0_.kv_ref, ...), custom_call_target="tpu_custom_call" | custom-call | tf_op jit(solution)/shard_map/pallas_call | solution.py:284
  56.4 31.7 %all_to_all.15 = f32[64,6,256]{2,1,0:T(8,128)S(1)} all-to-all(f32[64,6,256]{2,1,0:T(8,128)S(1)} %shard_map.97), channel_id=1, replica_groups=mesh['tok_0'=2,'tok_1'=8,'tok_2'=4,'head'=8] {'tok_0','tok_1','tok_2'}, dimensions={0} | all-to-all | bytes 786432 | tf_op jit(solution)/shard_map/all_to_all | solution.py:292
  88.0 0.2 shard_map.98.norm_ref
  88.2 6.5 %shard_map.99 = bf16[4096,256]{1,0:T(8,128)(2,1)} custom-call(bf16[16,4,2,32,128]{4,3,2,1,0:T(8,128)(2,1)S(1)} %bitcast.27, f32[4,2,4,256]{3,2,1,0:T(4,128)S(1)} %get-tuple-element.13.off_ref, bf16[2,512,128]{2,1,0:T(8,128)(2,1)S(1)} %pad_maximum_fusion.1.refs_0_.kv_ref, f32[4,4,256]{2,1,0:T(4,128)S(1)} %shard_map.98.norm_ref, ...), custom_call_target="tpu_custom_call" | custom-call | tf_op jit(solution)/shard_map/pallas_call | solution.py:301
  94.8 6.2 %all-to-all-start.2 = ((bf16[64,64,256]{2,1,0:T(8,128)(2,1)}), bf16[64,64,256]{2,1,0:T(8,128)(2,1)}, u32[]{:S(2)}, u32[]{:S(2)}) async-start(bf16[64,64,256]{2,1,0:T(8,128)(2,1)} %bitcast.30), calls=%async_computation.2 | async-start | bytes 4194304 | tf_op jit(solution)/shard_map/all_to_all | solution.py:316
  101.0 2.5 %shard_map.100 = f32[512,128]{1,0:T(8,128)S(1)} custom-call(s32[5]{0:T(128)S(1)} %pad_add_fusion.place_ref, bf16[16,4,2,32,128]{4,3,2,1,0:T(8,128)(2,1)S(1)} %bitcast.28, f32[2,4,4,256]{3,2,1,0:T(4,128)S(1)} %get-tuple-element.12.off_ref, f32[4,4,256]{2,1,0:T(4,128)S(1)} %shard_map.98.norm_ref, bf16[2,512,128]{2,1,0:T(8,128)(2,1)S(1)} %pad_maximum_fusion.1.refs_0_.kv_ref, ...), custom_call_target="tpu_custom_call" | custom-call | tf_op jit(solution)/shard_map/pallas_call | solution.py:321
  103.5 3.4 %collective-permute-start.3 = (f32[512,128]{1,0:T(8,128)S(1)}, f32[512,128]{1,0:T(8,128)S(1)}, u32[]{:S(2)}, u32[]{:S(2)}) collective-permute-start(f32[512,128]{1,0:T(8,128)S(1)} %shard_map.100), channel_id=1, source_target_pairs={{0,32},{32,0},{64,96},{96,64},{128,160},{160,128},{192,224},{224,1... | collective-permute-start | bytes 786440 | tf_op jit(solution)/shard_map/ppermute | solution.py:229
  106.9 23.7 %collective-permute-done.3 = f32[512,128]{1,0:T(8,128)S(1)} collective-permute-done((f32[512,128]{1,0:T(8,128)S(1)}, f32[512,128]{1,0:T(8,128)S(1)}, u32[]{:S(2)}, u32[]{:S(2)}) %collective-permute-start.3) | collective-permute-done | bytes 262176 | tf_op jit(solution)/shard_map/ppermute | solution.py:229
  130.7 15.4 %collective-permute-start.4 = (bf16[512,128]{1,0:T(8,128)(2,1)S(1)}, bf16[512,128]{1,0:T(8,128)(2,1)S(1)}, u32[]{:S(2)}, u32[]{:S(2)}) collective-permute-start(bf16[512,128]{1,0:T(8,128)(2,1)S(1)} %add_convert_fusion.3), channel_id=1, source_target_pairs={{0,64},{32,96},{64,0},{96,32},{128,192},{160,224},{192,128},{224,1... | collective-permute-start | bytes 393224 | tf_op jit(solution)/shard_map/ppermute | solution.py:229
  146.1 15.7 %collective-permute-done.4 = bf16[512,128]{1,0:T(8,128)(2,1)S(1)} collective-permute-done((bf16[512,128]{1,0:T(8,128)(2,1)S(1)}, bf16[512,128]{1,0:T(8,128)(2,1)S(1)}, u32[]{:S(2)}, u32[]{:S(2)}) %collective-permute-start.4) | collective-permute-done | bytes 131104 | tf_op jit(solution)/shard_map/ppermute | solution.py:229
  161.9 6.2 %collective-permute-start.5 = (bf16[512,128]{1,0:T(8,128)(2,1)S(1)}, bf16[512,128]{1,0:T(8,128)(2,1)S(1)}, u32[]{:S(2)}, u32[]{:S(2)}) collective-permute-start(bf16[512,128]{1,0:T(8,128)(2,1)S(1)} %add_convert_fusion.2), channel_id=1, source_target_pairs={{0,128},{32,160},{64,192},{96,224},{128,0},{160,32},{192,64},{224,... | collective-permute-start | bytes 393224 | tf_op jit(solution)/shard_map/ppermute | solution.py:229
  168.1 7.7 %collective-permute-done.5 = bf16[512,128]{1,0:T(8,128)(2,1)S(1)} collective-permute-done((bf16[512,128]{1,0:T(8,128)(2,1)S(1)}, bf16[512,128]{1,0:T(8,128)(2,1)S(1)}, u32[]{:S(2)}, u32[]{:S(2)}) %collective-permute-start.5) | collective-permute-done | bytes 131104 | tf_op jit(solution)/shard_map/ppermute | solution.py:229
  175.9 4.1 %collective-permute-start.6 = (bf16[512,128]{1,0:T(8,128)(2,1)S(1)}, bf16[512,128]{1,0:T(8,128)(2,1)S(1)}, u32[]{:S(2)}, u32[]{:S(2)}) collective-permute-start(bf16[512,128]{1,0:T(8,128)(2,1)S(1)} %add_convert_fusion.1), channel_id=1, source_target_pairs={{0,256},{256,0},{1,257},{257,1},{2,258},{258,2},{3,259},{259,3},{4... | collective-permute-start | bytes 393224 | tf_op jit(solution)/shard_map/ppermute | solution.py:229
  180.0 8.0 %collective-permute-done.6 = bf16[512,128]{1,0:T(8,128)(2,1)S(1)} collective-permute-done((bf16[512,128]{1,0:T(8,128)(2,1)S(1)}, bf16[512,128]{1,0:T(8,128)(2,1)S(1)}, u32[]{:S(2)}, u32[]{:S(2)}) %collective-permute-start.6) | collective-permute-done | bytes 131104 | tf_op jit(solution)/shard_map/ppermute | solution.py:229
  188.0 1.9 collective-permute-start.7
  190.0 7.2 %collective-permute-start.8 = (bf16[16,4,1024]{2,1,0:T(4,128)(2,1)S(1)}, bf16[16,4,1024]{2,1,0:T(4,128)(2,1)S(1)}, u32[]{:S(2)}, u32[]{:S(2)}) collective-permute-start(bf16[16,4,1024]{2,1,0:T(4,128)(2,1)S(1)} %bitcast.32), channel_id=1, source_target_pairs={{0,16},{8,24},{16,0},{24,8},{1,17},{9,25},{17,1},{25,9},{2,18},{10... | collective-permute-start | bytes 393224 | tf_op jit(solution)/shard_map/ppermute | solution.py:32
  197.1 1.9 collective-permute-start.9
  199.1 0.0 collective-permute-done.7
  199.1 1.7 collective-permute-done.8
  200.8 4.5 %collective-permute-done.9 = bf16[16,4,1024]{2,1,0:T(4,128)(2,1)S(1)} collective-permute-done((bf16[16,4,1024]{2,1,0:T(4,128)(2,1)S(1)}, bf16[16,4,1024]{2,1,0:T(4,128)(2,1)S(1)}, u32[]{:S(2)}, u32[]{:S(2)}) %collective-permute-start.9) | collective-permute-done | bytes 131104 | tf_op jit(solution)/shard_map/ppermute | solution.py:32
  205.2 0.3 select_bitcast_fusion.3
  205.5 0.4 pad_maximum_fusion
  205.9 0.9 reshape.28
  206.8 0.0 all-to-all-done.2
  206.8 1.9 convert_reduce_fusion
  208.7 0.6 fusion
  (5 shorter events, 0.2 us)
Async XLA Ops:
  0.6 0.7 copy-start
  1.3 0.7 copy-start.1
  3.3 50.7 %all-to-all-start = ((bf16[64,2,32,128]{3,2,1,0:T(8,128)(2,1)}), bf16[64,2,32,128]{3,2,1,0:T(8,128)(2,1)S(1)}, u32[]{:S(2)}, u32[]{:S(2)}) async-start(bf16[64,2,32,128]{3,2,1,0:T(8,128)(2,1)} %shard_map.94), calls=%async_computation | async-start | bytes 2097152 | tf_op jit(solution)/shard_map/all_to_all | solution.py:259
  21.5 32.4 %collective-permute-start = (bf16[2,512,128]{2,1,0:T(8,128)(2,1)S(1)}, bf16[2,512,128]{2,1,0:T(8,128)(2,1)S(1)}, u32[]{:S(2)}, u32[]{:S(2)}) collective-permute-start(bf16[2,512,128]{2,1,0:T(8,128)(2,1)S(1)} %pad_maximum_fusion.1.refs_0_.kv_ref), channel_id=1, source_target_pairs={{0,8},{8,16},{16,24},{24,0},{1,9},{9,17},{17,25},{25,1},{2,10},{10... | collective-permute-start | bytes 786440 | tf_op jit(solution)/shard_map/ppermute | solution.py:32
  23.9 30.1 %collective-permute-start.1 = (bf16[2,512,128]{2,1,0:T(8,128)(2,1)S(1)}, bf16[2,512,128]{2,1,0:T(8,128)(2,1)S(1)}, u32[]{:S(2)}, u32[]{:S(2)}) collective-permute-start(bf16[2,512,128]{2,1,0:T(8,128)(2,1)S(1)} %pad_maximum_fusion.1.refs_0_.kv_ref), channel_id=1, source_target_pairs={{0,16},{8,24},{16,0},{24,8},{1,17},{9,25},{17,1},{25,9},{2,18},{10... | collective-permute-start | bytes 786440 | tf_op jit(solution)/shard_map/ppermute | solution.py:32
  28.3 25.7 %collective-permute-start.2 = (bf16[2,512,128]{2,1,0:T(8,128)(2,1)S(1)}, bf16[2,512,128]{2,1,0:T(8,128)(2,1)S(1)}, u32[]{:S(2)}, u32[]{:S(2)}) collective-permute-start(bf16[2,512,128]{2,1,0:T(8,128)(2,1)S(1)} %pad_maximum_fusion.1.refs_0_.kv_ref), channel_id=1, source_target_pairs={{0,24},{8,0},{16,8},{24,16},{1,25},{9,1},{17,9},{25,17},{2,26},{10... | collective-permute-start | bytes 786440 | tf_op jit(solution)/shard_map/ppermute | solution.py:32
  31.0 5.3 %copy-start.2 = (s32[8]{0:T(128)S(1)}, s32[8]{0:T(128)}, u32[]{:S(2)}) copy-start(s32[8]{0:T(128)} %lengths_ref.1) | copy-start | bytes 100
  94.8 112.1 %all-to-all-start.2 = ((bf16[64,64,256]{2,1,0:T(8,128)(2,1)}), bf16[64,64,256]{2,1,0:T(8,128)(2,1)}, u32[]{:S(2)}, u32[]{:S(2)}) async-start(bf16[64,64,256]{2,1,0:T(8,128)(2,1)} %bitcast.30), calls=%async_computation.2 | async-start | bytes 4194304 | tf_op jit(solution)/shard_map/all_to_all | solution.py:316
  103.5 27.1 %collective-permute-start.3 = (f32[512,128]{1,0:T(8,128)S(1)}, f32[512,128]{1,0:T(8,128)S(1)}, u32[]{:S(2)}, u32[]{:S(2)}) collective-permute-start(f32[512,128]{1,0:T(8,128)S(1)} %shard_map.100), channel_id=1, source_target_pairs={{0,32},{32,0},{64,96},{96,64},{128,160},{160,128},{192,224},{224,1... | collective-permute-start | bytes 786440 | tf_op jit(solution)/shard_map/ppermute | solution.py:229
  130.7 31.2 %collective-permute-start.4 = (bf16[512,128]{1,0:T(8,128)(2,1)S(1)}, bf16[512,128]{1,0:T(8,128)(2,1)S(1)}, u32[]{:S(2)}, u32[]{:S(2)}) collective-permute-start(bf16[512,128]{1,0:T(8,128)(2,1)S(1)} %add_convert_fusion.3), channel_id=1, source_target_pairs={{0,64},{32,96},{64,0},{96,32},{128,192},{160,224},{192,128},{224,1... | collective-permute-start | bytes 393224 | tf_op jit(solution)/shard_map/ppermute | solution.py:229
  161.9 14.0 %collective-permute-start.5 = (bf16[512,128]{1,0:T(8,128)(2,1)S(1)}, bf16[512,128]{1,0:T(8,128)(2,1)S(1)}, u32[]{:S(2)}, u32[]{:S(2)}) collective-permute-start(bf16[512,128]{1,0:T(8,128)(2,1)S(1)} %add_convert_fusion.2), channel_id=1, source_target_pairs={{0,128},{32,160},{64,192},{96,224},{128,0},{160,32},{192,64},{224,... | collective-permute-start | bytes 393224 | tf_op jit(solution)/shard_map/ppermute | solution.py:229
  175.9 12.1 %collective-permute-start.6 = (bf16[512,128]{1,0:T(8,128)(2,1)S(1)}, bf16[512,128]{1,0:T(8,128)(2,1)S(1)}, u32[]{:S(2)}, u32[]{:S(2)}) collective-permute-start(bf16[512,128]{1,0:T(8,128)(2,1)S(1)} %add_convert_fusion.1), channel_id=1, source_target_pairs={{0,256},{256,0},{1,257},{257,1},{2,258},{258,2},{3,259},{259,3},{4... | collective-permute-start | bytes 393224 | tf_op jit(solution)/shard_map/ppermute | solution.py:229
  188.0 11.1 %collective-permute-start.7 = (bf16[16,4,1024]{2,1,0:T(4,128)(2,1)S(1)}, bf16[16,4,1024]{2,1,0:T(4,128)(2,1)S(1)}, u32[]{:S(2)}, u32[]{:S(2)}) collective-permute-start(bf16[16,4,1024]{2,1,0:T(4,128)(2,1)S(1)} %bitcast.31), channel_id=1, source_target_pairs={{0,8},{8,16},{16,24},{24,0},{1,9},{9,17},{17,25},{25,1},{2,10},{10... | collective-permute-start | bytes 393224 | tf_op jit(solution)/shard_map/ppermute | solution.py:32
  190.0 10.8 %collective-permute-start.8 = (bf16[16,4,1024]{2,1,0:T(4,128)(2,1)S(1)}, bf16[16,4,1024]{2,1,0:T(4,128)(2,1)S(1)}, u32[]{:S(2)}, u32[]{:S(2)}) collective-permute-start(bf16[16,4,1024]{2,1,0:T(4,128)(2,1)S(1)} %bitcast.32), channel_id=1, source_target_pairs={{0,16},{8,24},{16,0},{24,8},{1,17},{9,25},{17,1},{25,9},{2,18},{10... | collective-permute-start | bytes 393224 | tf_op jit(solution)/shard_map/ppermute | solution.py:32
  197.1 8.1 %collective-permute-start.9 = (bf16[16,4,1024]{2,1,0:T(4,128)(2,1)S(1)}, bf16[16,4,1024]{2,1,0:T(4,128)(2,1)S(1)}, u32[]{:S(2)}, u32[]{:S(2)}) collective-permute-start(bf16[16,4,1024]{2,1,0:T(4,128)(2,1)S(1)} %bitcast.33), channel_id=1, source_target_pairs={{0,24},{8,0},{16,8},{24,16},{1,25},{9,1},{17,9},{25,17},{2,26},{10... | collective-permute-start | bytes 393224 | tf_op jit(solution)/shard_map/ppermute | solution.py:32

commit v6 on v3

--- a/solution.py
+++ b/solution.py
@@ -98,20 +98,20 @@
 
 
 def join_kernel(stats_ref, out_ref):
-    lines = stats_ref.shape[2] // 3
-    for p in range(out_ref.shape[0]):
-        parts = [
-            [stats_ref[k, p, j * lines : (j + 1) * lines] for j in range(3)]
-            for k in range(stats_ref.shape[0])
-        ]
-        top, total, weighted = join(parts)
-        out_ref[p, :lines] = top + jnp.log2(total)
-        out_ref[p, lines:] = weighted / total
-
-
-def query_kernel(near_ref, text_ref, off_ref, all_norm_ref, *refs):
+    lines = stats_ref.shape[1] // 3
+    parts = [
+        [stats_ref[k, j * lines : (j + 1) * lines] for j in range(3)]
+        for k in range(stats_ref.shape[0])
+    ]
+    top, total, weighted = join(parts)
+    norm = jnp.concatenate((top + jnp.log2(total), weighted / total), axis=0)
+    for k in range(out_ref.shape[0]):
+        out_ref[k] = norm
+
+
+def query_kernel(text_ref, off_ref, copies_ref, *refs):
     kv_refs, dq_ref, ds_scr = refs[:-2], refs[-2], refs[-1]
-    norm_ref = all_norm_ref.at[near_ref[0]]
+    norm_ref = copies_ref.at[0]
     chunks = norm_ref.shape[0] // 2
     per = CHUNK // dq_ref.shape[1]
     for c in range(chunks):
@@ -135,8 +135,12 @@
     pieces = off_ref.shape[0]
     text_refs, out_refs = refs[:pieces], refs[pieces : 2 * pieces]
     p_scr, ds_scr, kv_scr, vision_ref, vision_sem = refs[2 * pieces :]
-    vision_copy = pltpu.make_async_copy(far_vision_ref, vision_ref, vision_sem)
-    vision_copy.start()
+    copies = [
+        pltpu.make_async_copy(far_vision_ref.at[p], vision_ref.at[p], vision_sem.at[p])
+        for p in range(pieces)
+    ]
+    for copy in copies:
+        copy.start()
     chunks = norm_ref.shape[1] // 2
     rows = kv_ref.shape[1] // FRAME_DEV
     key_sum = jnp.zeros(kv_ref.shape[1:], F32)
@@ -156,9 +160,9 @@
             key_sum += dot(ds_scr[...], q_c, NN)
     kv_scr[:, :HEAD_WIDTH] = (key_sum * SCALE).astype(BF16)
     kv_scr[:, HEAD_WIDTH:] = value_sum.astype(BF16)
-    vision_copy.wait()
     size = 512
     for p, out_ref in enumerate(out_refs):
+        copies[p].wait()
         for at in range(0, out_ref.shape[0], size):
             block = vision_ref[p, at : at + size]
             out_ref[at : at + size] = dot(block, kv_scr[...], NN).astype(BF16)
@@ -169,11 +173,12 @@
 
 
 def turn_kernel(near_ref, vision_ref, out_ref):
-    pieces, _, size, _ = out_ref.shape
-    turned = vision_ref[...].T
-    for p in range(pieces):
-        at = (p + pieces - near_ref[0]) % pieces
-        out_ref[at, 0] = turned[p * size : (p + 1) * size]
+    pieces, deep, size, _ = out_ref.shape
+    for d in range(deep):
+        turned = vision_ref[:, d * pieces * size : (d + 1) * pieces * size].T
+        for p in range(pieces):
+            at = lax.rem(p + pieces - near_ref[0], pieces)
+            out_ref[at, d] = turned[p * size : (p + 1) * size]
 
 
 def bases_from(at, peers):
@@ -239,9 +244,9 @@
     turned = pl.pallas_call(
         turn_kernel,
         out_shape=jax.ShapeDtypeStruct((near, far, part, kv_rows), BF16),
-        grid=(far,),
-        in_specs=[SCALARS, pl.BlockSpec((kv_rows, near * part), lambda i: (0, i))],
-        out_specs=pl.BlockSpec((near, 1, part, kv_rows), lambda i: (0, i, 0, 0)),
+        grid=(far // 4,),
+        in_specs=[SCALARS, pl.BlockSpec((kv_rows, 4 * near * part), lambda i: (0, i))],
+        out_specs=pl.BlockSpec((near, 4, part, kv_rows), lambda i: (0, i, 0, 0)),
         compiler_params=LARGER,
     )(near_id, vision)
     turned = turned.reshape(near, far * part, kv_rows)
@@ -249,29 +254,31 @@
 
     stats = pl.pallas_call(
         stats_kernel,
-        out_shape=jax.ShapeDtypeStruct((peers, 3 * chunks, CHUNK), F32),
+        out_shape=jax.ShapeDtypeStruct((far, 3 * chunks, CHUNK), F32),
         in_specs=[WHOLE] * (2 + near),
         out_specs=WHOLE,
         scratch_shapes=[pltpu.VMEM((3 * chunks, CHUNK), F32)],
         compiler_params=PARAMS,
     )(text, own_off, *all_kv)
-    stats = lax.all_to_all(stats, TOK, 0, 0, tiled=True)
-    all_norm = pl.pallas_call(
+    stats = lax.all_to_all(stats, FAR, 0, 0, tiled=True)
+    norms = pl.pallas_call(
         join_kernel,
         out_shape=jax.ShapeDtypeStruct((near, 2 * chunks, CHUNK), F32),
         in_specs=[WHOLE],
         out_specs=WHOLE,
         compiler_params=PARAMS,
-    )(stats.reshape(far, near, 3 * chunks, CHUNK))
+    )(stats)
+    all_norm = lax.all_to_all(norms, NEAR, 0, 0, tiled=True)
 
     dq = pl.pallas_call(
         query_kernel,
         out_shape=jax.ShapeDtypeStruct((far, lines, HEAD_WIDTH), F32),
-        in_specs=[SCALARS] + [WHOLE] * (3 + near),
+        in_specs=[WHOLE] * (3 + near),
         out_specs=WHOLE,
         scratch_shapes=[pltpu.VMEM((kv_rows, CHUNK), BF16)],
         compiler_params=PARAMS,
-    )(near_id, text, own_off, all_norm, *all_kv)
+    )(text, own_off, norms, *all_kv)
+    dq, all_norm = lax.optimization_barrier((dq, all_norm))
     dq = lax.all_to_all(dq, FAR, 0, 0, tiled=True)
 
     sums = pl.pallas_call(
@@ -284,7 +291,7 @@
             pltpu.VMEM((kv_rows, CHUNK), BF16),
             pltpu.VMEM((kv_rows, 2 * HEAD_WIDTH), BF16),
             pltpu.VMEM((near, far * part, kv_rows), BF16),
-            pltpu.SemaphoreType.DMA,
+            pltpu.SemaphoreType.DMA((near,)),
         ],
         compiler_params=LARGE,
         cost_estimate=HEAVY,

time: 159 us -> 151 us (0.950)
  waiting for transfers between devices: 34.9 us -> 28.9 us
  Pallas kernels: 22.9 us -> 17.8 us
  starting transfers between devices: 89.5 us -> 92.5 us
    all_to_all x1 -> x2, waiting for transfers between devices: 12.2 us -> 2.13 us  [the longest x1 2.13 us: shards(): stats = lax.all_to_all(stats, FAR, 0, 0, tiled=True)]
    all_to_all x1, starting transfers between devices: 3.53 us -> 9.42 us  [shards(): dq = lax.all_to_all(dq, FAR, 0, 0, tiled=True)]
    all_to_all x1, waiting for transfers between devices: 1.52 us -> 7.19 us  [shards(): text = lax.all_to_all(own_text, FAR, 0, 0, tiled=True)]
    pallas_call x1, Pallas kernels: 10.9 us -> 5.24 us  [shards(): pl.pallas_call(turn_kernel, out_shape=jax.ShapeDtypeStruct((near, far, pa...]
    ppermute x12, waiting for transfers between devices: 12.4 us -> 9.02 us  [shifted(): lax.ppermute(x, axis, [(i, (i + step) % peers) for i in range(peers)])]
    ppermute x12, starting transfers between devices: 35.1 us -> 38.1 us  [shifted(): lax.ppermute(x, axis, [(i, (i + step) % peers) for i in range(peers)])]
    all_to_all x1 -> x2, starting transfers between devices: 14.2 us -> 11.3 us  [the longest x1 6.46 us: shards(): all_norm = lax.all_to_all(norms, NEAR, 0, 0, tiled=True)]
    all_to_all x1, waiting for transfers between devices: 1.96 us -> 4.87 us  [from_everyone(): lax.all_to_all(jnp.broadcast_to(x[None], (peers, *x.shape)), axis, 0, 0,...]
  transfers between devices with their start and end apart: 17 -> 18, of which waited for: 8 -> 8; matrix products, arithmetic and copies ran while one was open for 4% -> 4% of each run, Pallas kernels for 13% -> 10%
where the time goes in v6:
time: 151 us; the launch traced here: 150 us
  starting transfers between devices  92.5 us (61%)
  waiting for transfers between devices  28.9 us (19%)
  Pallas kernels  17.8 us (12%)
  local copies, waits for them, and re-layouts  5.33 us (4%)
  other arithmetic  4.22 us (3%)
    ppermute x12, starting transfers between devices, shifted(): lax.ppermute(x, axis, [(i, (i + step) % peers) for i in range(peers)])  38.1 us
    all_to_all x1, starting transfers between devices, shards(): text = lax.all_to_all(own_text, FAR, 0, 0, tiled=True)  14.8 us
    all_to_all x1, starting transfers between devices, from_everyone(): lax.all_to_all(jnp.broadcast_to(x[None], (peers, *x.shape)), axis, 0, 0,...  12 us
    all_to_all x1, starting transfers between devices, shards(): dq = lax.all_to_all(dq, FAR, 0, 0, tiled=True)  9.42 us
    ppermute x12, waiting for transfers between devices, shifted(): lax.ppermute(x, axis, [(i, (i + step) % peers) for i in range(peers)])  9.02 us
    all_to_all x1, waiting for transfers between devices, shards(): text = lax.all_to_all(own_text, FAR, 0, 0, tiled=True)  7.19 us
    all_to_all x1, starting transfers between devices, shards(): lax.all_to_all(weights.reshape(far, part, 2 * HEAD_WIDTH), FAR, 0, 0, til...  6.88 us
    all_to_all x1, starting transfers between devices, shards(): all_norm = lax.all_to_all(norms, NEAR, 0, 0, tiled=True)  6.46 us
  transfers between devices with their start and end apart: 18, of which 8 were waited for; matrix products, arithmetic and copies ran while one was open for 4% of the time, Pallas kernels for 10%

profile of v6, /device:TPU:14, one launch (start us, length us, event | category | flops | bytes accessed | tf_op | source)
XLA Modules:
  0.0 149.7 jit_solution(12617106353971721739)
XLA Ops:
  0.6 0.7 stack_reshape.6
  1.3 0.7 stack_reshape.7
  2.1 0.8 broadcast_in_dim.32
  2.8 1.0 pad_maximum_fusion.1.refs_0_.kv_ref
  3.8 2.4 %collective-permute-start = (bf16[2,512,128]{2,1,0:T(8,128)(2,1)S(1)}, bf16[2,512,128]{2,1,0:T(8,128)(2,1)S(1)}, u32[]{:S(2)}, u32[]{:S(2)}) collective-permute-start(bf16[2,512,128]{2,1,0:T(8,128)(2,1)S(1)} %pad_maximum_fusion.1.refs_0_.kv_ref), channel_id=1, source_target_pairs={{0,8},{8,16},{16,24},{24,0},{1,9},{9,17},{17,25},{25,1},{2,10},{10... | collective-permute-start | bytes 786440 | tf_op jit(solution)/shard_map/ppermute | solution.py:38
  6.2 4.3 %collective-permute-start.1 = (bf16[2,512,128]{2,1,0:T(8,128)(2,1)S(1)}, bf16[2,512,128]{2,1,0:T(8,128)(2,1)S(1)}, u32[]{:S(2)}, u32[]{:S(2)}) collective-permute-start(bf16[2,512,128]{2,1,0:T(8,128)(2,1)S(1)} %pad_maximum_fusion.1.refs_0_.kv_ref), channel_id=1, source_target_pairs={{0,16},{8,24},{16,0},{24,8},{1,17},{9,25},{17,1},{25,9},{2,18},{10... | collective-permute-start | bytes 786440 | tf_op jit(solution)/shard_map/ppermute | solution.py:38
  10.5 1.9 %collective-permute-start.2 = (bf16[2,512,128]{2,1,0:T(8,128)(2,1)S(1)}, bf16[2,512,128]{2,1,0:T(8,128)(2,1)S(1)}, u32[]{:S(2)}, u32[]{:S(2)}) collective-permute-start(bf16[2,512,128]{2,1,0:T(8,128)(2,1)S(1)} %pad_maximum_fusion.1.refs_0_.kv_ref), channel_id=1, source_target_pairs={{0,24},{8,0},{16,8},{24,16},{1,25},{9,1},{17,9},{25,17},{2,26},{10... | collective-permute-start | bytes 786440 | tf_op jit(solution)/shard_map/ppermute | solution.py:38
  12.5 14.8 %all-to-all-start = ((bf16[16,2,32,128]{3,2,1,0:T(8,128)(2,1)}), bf16[16,2,32,128]{3,2,1,0:T(8,128)(2,1)S(1)}, u32[]{:S(2)}, u32[]{:S(2)}) async-start(bf16[16,2,32,128]{3,2,1,0:T(8,128)(2,1)} %broadcast_in_dim.32), calls=%async_computation | async-start | bytes 524288 | tf_op jit(solution)/shard_map/all_to_all | solution.py:222
  27.3 0.1 add_multiply_fusion
  27.4 0.8 slice_bitcast_fusion
  28.1 0.1 iota_add_fusion
  28.2 0.1 add_bitcast_fusion
  28.3 0.8 select_reduce_fusion.2
  29.1 0.1 convert_reduce_fusion.1
  29.2 0.1 select_reduce_fusion.1
  29.3 0.1 add.140
  29.4 5.2 %shard_map.94 = bf16[4,16,64,512]{3,2,1,0:T(8,128)(2,1)} custom-call(s32[1]{0:T(128)} %bitcast.near_ref, bf16[512,4096]{1,0:T(8,128)(2,1)} %vision_ref.1), custom_call_target="tpu_custom_call" | custom-call | tf_op jit(solution)/shard_map/pallas_call | solution.py:244
  34.6 0.1 and_select_fusion.off_ref
  34.7 7.2 %all-to-all-done.text_ref.refs_0_ = bf16[16,2,32,128]{3,2,1,0:T(8,128)(2,1)S(1)} async-done(((bf16[16,2,32,128]{3,2,1,0:T(8,128)(2,1)}), bf16[16,2,32,128]{3,2,1,0:T(8,128)(2,1)S(1)}, u32[]{:S(2)}, u32[]{:S(2)}) %all-to-all-start) | async-done | bytes 262176 | tf_op jit(solution)/shard_map/all_to_all | solution.py:222
  41.9 0.0 collective-permute-done.refs_1_
  41.9 0.0 collective-permute-done.1.refs_2_
  41.9 0.0 collective-permute-done.2.refs_3_
  41.9 2.5 %shard_map.95 = f32[16,6,256]{2,1,0:T(8,128)} custom-call(bf16[16,2,32,128]{3,2,1,0:T(8,128)(2,1)S(1)} %all-to-all-done.text_ref.refs_0_, f32[2,16,256]{2,1,0:T(8,128)S(1)} %and_select_fusion.off_ref, bf16[2,512,128]{2,1,0:T(8,128)(2,1)S(1)} %pad_maximum_fusion.1.refs_0_.kv_ref, bf16[2,512,128]{2,1,0:T(8,128)(2,1)S(1)} %collective-permute-done.refs_1_, ...), custom_call_target="tpu_custom_call" | custom-call | tf_op jit(solution)/shard_map/pallas_call | solution.py:255
  44.4 4.8 %all-to-all-start.1 = ((f32[16,6,256]{2,1,0:T(8,128)}), f32[16,6,256]{2,1,0:T(8,128)S(1)}, u32[]{:S(2)}, u32[]{:S(2)}) async-start(f32[16,6,256]{2,1,0:T(8,128)} %shard_map.95), calls=%async_computation.1 | async-start | bytes 262144 | tf_op jit(solution)/shard_map/all_to_all | solution.py:263
  49.2 5.1 %collective-permute-start.3 = (bf16[16,2,32,128]{3,2,1,0:T(8,128)(2,1)S(1)}, bf16[16,2,32,128]{3,2,1,0:T(8,128)(2,1)S(1)}, u32[]{:S(2)}, u32[]{:S(2)}) collective-permute-start(bf16[16,2,32,128]{3,2,1,0:T(8,128)(2,1)S(1)} %all-to-all-done.text_ref.refs_0_), channel_id=1, source_target_pairs={{0,8},{8,16},{16,24},{24,0},{1,9},{9,17},{17,25},{25,1},{2,10},{10... | collective-permute-start | bytes 786440 | tf_op jit(solution)/shard_map/ppermute | solution.py:38
  54.4 1.9 %collective-permute-start.4 = (bf16[16,2,32,128]{3,2,1,0:T(8,128)(2,1)S(1)}, bf16[16,2,32,128]{3,2,1,0:T(8,128)(2,1)S(1)}, u32[]{:S(2)}, u32[]{:S(2)}) collective-permute-start(bf16[16,2,32,128]{3,2,1,0:T(8,128)(2,1)S(1)} %all-to-all-done.text_ref.refs_0_), channel_id=1, source_target_pairs={{0,16},{8,24},{16,0},{24,8},{1,17},{9,25},{17,1},{25,9},{2,18},{10... | collective-permute-start | bytes 786440 | tf_op jit(solution)/shard_map/ppermute | solution.py:38
  56.3 3.3 %collective-permute-start.5 = (bf16[16,2,32,128]{3,2,1,0:T(8,128)(2,1)S(1)}, bf16[16,2,32,128]{3,2,1,0:T(8,128)(2,1)S(1)}, u32[]{:S(2)}, u32[]{:S(2)}) collective-permute-start(bf16[16,2,32,128]{3,2,1,0:T(8,128)(2,1)S(1)} %all-to-all-done.text_ref.refs_0_), channel_id=1, source_target_pairs={{0,24},{8,0},{16,8},{24,16},{1,25},{9,1},{17,9},{25,17},{2,26},{10... | collective-permute-start | bytes 786440 | tf_op jit(solution)/shard_map/ppermute | solution.py:38
  59.7 2.1 %all-to-all-done.1.stats_ref = f32[16,6,256]{2,1,0:T(8,128)S(1)} async-done(((f32[16,6,256]{2,1,0:T(8,128)}), f32[16,6,256]{2,1,0:T(8,128)S(1)}, u32[]{:S(2)}, u32[]{:S(2)}) %all-to-all-start.1) | async-done | bytes 98336 | tf_op jit(solution)/shard_map/all_to_all | solution.py:263
  61.9 0.7 shard_map.96.copies_ref
  62.5 6.5 %all-to-all-start.2 = ((f32[4,4,256]{2,1,0:T(4,128)}), f32[4,4,256]{2,1,0:T(4,128)S(1)}, u32[]{:S(2)}, u32[]{:S(2)}) async-start(f32[4,4,256]{2,1,0:T(4,128)} %shard_map.96.copies_ref), calls=%async_computation.2 | async-start | bytes 32768 | tf_op jit(solution)/shard_map/all_to_all | solution.py:271
  69.0 0.1 and_select_fusion.1.off_ref
  69.1 3.4 %shard_map.97 = f32[16,32,128]{2,1,0:T(8,128)} custom-call(bf16[16,2,32,128]{3,2,1,0:T(8,128)(2,1)S(1)} %all-to-all-done.text_ref.refs_0_, f32[2,16,256]{2,1,0:T(8,128)S(1)} %and_select_fusion.off_ref, f32[4,4,256]{2,1,0:T(4,128)} %shard_map.96.copies_ref, bf16[2,512,128]{2,1,0:T(8,128)(2,1)S(1)} %pad_maximum_fusion.1.refs_0_.kv_ref, ...), custom_call_target="tpu_custom_call" | custom-call | tf_op jit(solution)/shard_map/pallas_call | solution.py:273
  72.5 0.0 all-to-all-done.2.norm_ref
  72.5 9.4 %all-to-all-start.3 = ((f32[16,32,128]{2,1,0:T(8,128)}), f32[16,32,128]{2,1,0:T(8,128)S(1)}, u32[]{:S(2)}, u32[]{:S(2)}) async-start(f32[16,32,128]{2,1,0:T(8,128)} %shard_map.97), calls=%async_computation.3 | async-start | bytes 524288 | tf_op jit(solution)/shard_map/all_to_all | solution.py:282
  81.9 0.0 collective-permute-done.3.refs_1_
  81.9 0.0 collective-permute-done.4.refs_2_
  81.9 0.0 collective-permute-done.5.refs_3_
  82.0 6.0 %shard_map.98 = (bf16[1024,256]{1,0:T(8,128)(2,1)S(1)}, bf16[1024,256]{1,0:T(8,128)(2,1)}, bf16[1024,256]{1,0:T(8,128)(2,1)}, bf16[1024,256]{1,0:T(8,128)(2,1)}) custom-call(s32[1]{0:T(128)} %bitcast.near_ref, bf16[2,512,128]{2,1,0:T(8,128)(2,1)S(1)} %pad_maximum_fusion.1.refs_0_.kv_ref, f32[4,2,4,256]{3,2,1,0:T(4,128)S(1)} %and_select_fusion.1.off_ref, ...), custom_call_target="tpu_custom_call" | custom-call | flops 99999997952 | bytes 1048576 | tf_op jit(solution)/shard_map/pallas_call | solution.py:284
  88.0 3.8 %collective-permute-start.6 = (bf16[1024,256]{1,0:T(8,128)(2,1)}, bf16[1024,256]{1,0:T(8,128)(2,1)S(1)}, u32[]{:S(2)}, u32[]{:S(2)}) collective-permute-start(bf16[1024,256]{1,0:T(8,128)(2,1)} %get-tuple-element.23), channel_id=1, source_target_pairs={{0,8},{8,16},{16,24},{24,0},{1,9},{9,17},{17,25},{25,1},{2,10},{10... | collective-permute-start | bytes 1572872 | tf_op jit(solution)/shard_map/ppermute | solution.py:38
  91.7 3.0 %collective-permute-start.7 = (bf16[1024,256]{1,0:T(8,128)(2,1)}, bf16[1024,256]{1,0:T(8,128)(2,1)S(1)}, u32[]{:S(2)}, u32[]{:S(2)}) collective-permute-start(bf16[1024,256]{1,0:T(8,128)(2,1)} %get-tuple-element.24), channel_id=1, source_target_pairs={{0,16},{8,24},{16,0},{24,8},{1,17},{9,25},{17,1},{25,9},{2,18},{10... | collective-permute-start | bytes 1572872 | tf_op jit(solution)/shard_map/ppermute | solution.py:38
  94.7 2.3 %collective-permute-start.8 = (bf16[1024,256]{1,0:T(8,128)(2,1)}, bf16[1024,256]{1,0:T(8,128)(2,1)S(1)}, u32[]{:S(2)}, u32[]{:S(2)}) collective-permute-start(bf16[1024,256]{1,0:T(8,128)(2,1)} %get-tuple-element.25), channel_id=1, source_target_pairs={{0,24},{8,0},{16,8},{24,16},{1,25},{9,1},{17,9},{25,17},{2,26},{10... | collective-permute-start | bytes 1572872 | tf_op jit(solution)/shard_map/ppermute | solution.py:38
  97.0 0.0 all-to-all-done.3.parts_ref
  97.1 0.7 broadcast_in_dim.66
  97.8 12.0 %all-to-all-start.4 = ((bf16[16,4,1024]{2,1,0:T(4,128)(2,1)}), bf16[16,4,1024]{2,1,0:T(4,128)(2,1)S(1)}, u32[]{:S(2)}, u32[]{:S(2)}) async-start(bf16[16,4,1024]{2,1,0:T(4,128)(2,1)} %broadcast_in_dim.66), calls=%async_computation.4 | async-start | bytes 262144 | tf_op jit(solution)/shard_map/all_to_all | solution.py:33
  109.8 0.0 collective-permute-done.6
  109.8 0.4 collective-permute-done.7
  110.2 6.1 %collective-permute-done.8 = bf16[1024,256]{1,0:T(8,128)(2,1)S(1)} collective-permute-done((bf16[1024,256]{1,0:T(8,128)(2,1)}, bf16[1024,256]{1,0:T(8,128)(2,1)S(1)}, u32[]{:S(2)}, u32[]{:S(2)}) %collective-permute-start.8) | collective-permute-done | bytes 524320 | tf_op jit(solution)/shard_map/ppermute | solution.py:38
  116.3 1.1 add_convert_fusion
  117.4 4.9 %all-to-all-done.4 = bf16[16,4,1024]{2,1,0:T(4,128)(2,1)S(1)} async-done(((bf16[16,4,1024]{2,1,0:T(4,128)(2,1)}), bf16[16,4,1024]{2,1,0:T(4,128)(2,1)S(1)}, u32[]{:S(2)}, u32[]{:S(2)}) %all-to-all-start.4) | async-done | bytes 131104 | tf_op jit(solution)/shard_map/all_to_all | solution.py:33
  122.3 6.9 %all-to-all-start.5 = ((bf16[16,64,256]{2,1,0:T(8,128)(2,1)}), bf16[16,64,256]{2,1,0:T(8,128)(2,1)S(1)}, u32[]{:S(2)}, u32[]{:S(2)}) async-start(bf16[16,64,256]{2,1,0:T(8,128)(2,1)} %bitcast.18), calls=%async_computation.5 | async-start | bytes 1048576 | tf_op jit(solution)/shard_map/all_to_all | solution.py:314
  129.1 3.0 %collective-permute-start.10 = (bf16[16,4,1024]{2,1,0:T(4,128)(2,1)S(1)}, bf16[16,4,1024]{2,1,0:T(4,128)(2,1)S(1)}, u32[]{:S(2)}, u32[]{:S(2)}) collective-permute-start(bf16[16,4,1024]{2,1,0:T(4,128)(2,1)S(1)} %all-to-all-done.4), channel_id=1, source_target_pairs={{0,16},{8,24},{16,0},{24,8},{1,17},{9,25},{17,1},{25,9},{2,18},{10... | collective-permute-start | bytes 393224 | tf_op jit(solution)/shard_map/ppermute | solution.py:38
  132.1 2.3 %collective-permute-start.11 = (bf16[16,4,1024]{2,1,0:T(4,128)(2,1)S(1)}, bf16[16,4,1024]{2,1,0:T(4,128)(2,1)S(1)}, u32[]{:S(2)}, u32[]{:S(2)}) collective-permute-start(bf16[16,4,1024]{2,1,0:T(4,128)(2,1)S(1)} %all-to-all-done.4), channel_id=1, source_target_pairs={{0,24},{8,0},{16,8},{24,16},{1,25},{9,1},{17,9},{25,17},{2,26},{10... | collective-permute-start | bytes 393224 | tf_op jit(solution)/shard_map/ppermute | solution.py:38
  134.4 4.7 %collective-permute-start.9 = (bf16[16,4,1024]{2,1,0:T(4,128)(2,1)S(1)}, bf16[16,4,1024]{2,1,0:T(4,128)(2,1)S(1)}, u32[]{:S(2)}, u32[]{:S(2)}) collective-permute-start(bf16[16,4,1024]{2,1,0:T(4,128)(2,1)S(1)} %all-to-all-done.4), channel_id=1, source_target_pairs={{0,8},{8,16},{16,24},{24,0},{1,9},{9,17},{17,25},{25,1},{2,10},{10... | collective-permute-start | bytes 393224 | tf_op jit(solution)/shard_map/ppermute | solution.py:38
  139.2 0.0 collective-permute-done.10
  139.2 1.1 collective-permute-done.11
  140.3 1.4 collective-permute-done.9
  141.7 0.3 select_bitcast_fusion.3
  142.0 0.4 pad_maximum_fusion
  142.4 0.9 reshape.237
  143.3 5.7 %all-to-all-done.5 = bf16[16,64,256]{2,1,0:T(8,128)(2,1)S(1)} async-done(((bf16[16,64,256]{2,1,0:T(8,128)(2,1)}), bf16[16,64,256]{2,1,0:T(8,128)(2,1)S(1)}, u32[]{:S(2)}, u32[]{:S(2)}) %all-to-all-start.5) | async-done | bytes 524320 | tf_op jit(solution)/shard_map/all_to_all | solution.py:314
  149.0 0.1 convert_reduce_fusion
  149.1 0.6 fusion.10
  (13 shorter events, 0.1 us)
Async XLA Ops:
  3.8 38.1 %collective-permute-start = (bf16[2,512,128]{2,1,0:T(8,128)(2,1)S(1)}, bf16[2,512,128]{2,1,0:T(8,128)(2,1)S(1)}, u32[]{:S(2)}, u32[]{:S(2)}) collective-permute-start(bf16[2,512,128]{2,1,0:T(8,128)(2,1)S(1)} %pad_maximum_fusion.1.refs_0_.kv_ref), channel_id=1, source_target_pairs={{0,8},{8,16},{16,24},{24,0},{1,9},{9,17},{17,25},{25,1},{2,10},{10... | collective-permute-start | bytes 786440 | tf_op jit(solution)/shard_map/ppermute | solution.py:38
  6.2 35.7 %collective-permute-start.1 = (bf16[2,512,128]{2,1,0:T(8,128)(2,1)S(1)}, bf16[2,512,128]{2,1,0:T(8,128)(2,1)S(1)}, u32[]{:S(2)}, u32[]{:S(2)}) collective-permute-start(bf16[2,512,128]{2,1,0:T(8,128)(2,1)S(1)} %pad_maximum_fusion.1.refs_0_.kv_ref), channel_id=1, source_target_pairs={{0,16},{8,24},{16,0},{24,8},{1,17},{9,25},{17,1},{25,9},{2,18},{10... | collective-permute-start | bytes 786440 | tf_op jit(solution)/shard_map/ppermute | solution.py:38
  10.5 31.4 %collective-permute-start.2 = (bf16[2,512,128]{2,1,0:T(8,128)(2,1)S(1)}, bf16[2,512,128]{2,1,0:T(8,128)(2,1)S(1)}, u32[]{:S(2)}, u32[]{:S(2)}) collective-permute-start(bf16[2,512,128]{2,1,0:T(8,128)(2,1)S(1)} %pad_maximum_fusion.1.refs_0_.kv_ref), channel_id=1, source_target_pairs={{0,24},{8,0},{16,8},{24,16},{1,25},{9,1},{17,9},{25,17},{2,26},{10... | collective-permute-start | bytes 786440 | tf_op jit(solution)/shard_map/ppermute | solution.py:38
  12.5 29.4 %all-to-all-start = ((bf16[16,2,32,128]{3,2,1,0:T(8,128)(2,1)}), bf16[16,2,32,128]{3,2,1,0:T(8,128)(2,1)S(1)}, u32[]{:S(2)}, u32[]{:S(2)}) async-start(bf16[16,2,32,128]{3,2,1,0:T(8,128)(2,1)} %broadcast_in_dim.32), calls=%async_computation | async-start | bytes 524288 | tf_op jit(solution)/shard_map/all_to_all | solution.py:222
  44.4 17.5 %all-to-all-start.1 = ((f32[16,6,256]{2,1,0:T(8,128)}), f32[16,6,256]{2,1,0:T(8,128)S(1)}, u32[]{:S(2)}, u32[]{:S(2)}) async-start(f32[16,6,256]{2,1,0:T(8,128)} %shard_map.95), calls=%async_computation.1 | async-start | bytes 262144 | tf_op jit(solution)/shard_map/all_to_all | solution.py:263
  49.2 32.7 %collective-permute-start.3 = (bf16[16,2,32,128]{3,2,1,0:T(8,128)(2,1)S(1)}, bf16[16,2,32,128]{3,2,1,0:T(8,128)(2,1)S(1)}, u32[]{:S(2)}, u32[]{:S(2)}) collective-permute-start(bf16[16,2,32,128]{3,2,1,0:T(8,128)(2,1)S(1)} %all-to-all-done.text_ref.refs_0_), channel_id=1, source_target_pairs={{0,8},{8,16},{16,24},{24,0},{1,9},{9,17},{17,25},{25,1},{2,10},{10... | collective-permute-start | bytes 786440 | tf_op jit(solution)/shard_map/ppermute | solution.py:38
  54.4 27.6 %collective-permute-start.4 = (bf16[16,2,32,128]{3,2,1,0:T(8,128)(2,1)S(1)}, bf16[16,2,32,128]{3,2,1,0:T(8,128)(2,1)S(1)}, u32[]{:S(2)}, u32[]{:S(2)}) collective-permute-start(bf16[16,2,32,128]{3,2,1,0:T(8,128)(2,1)S(1)} %all-to-all-done.text_ref.refs_0_), channel_id=1, source_target_pairs={{0,16},{8,24},{16,0},{24,8},{1,17},{9,25},{17,1},{25,9},{2,18},{10... | collective-permute-start | bytes 786440 | tf_op jit(solution)/shard_map/ppermute | solution.py:38
  56.3 25.6 %collective-permute-start.5 = (bf16[16,2,32,128]{3,2,1,0:T(8,128)(2,1)S(1)}, bf16[16,2,32,128]{3,2,1,0:T(8,128)(2,1)S(1)}, u32[]{:S(2)}, u32[]{:S(2)}) collective-permute-start(bf16[16,2,32,128]{3,2,1,0:T(8,128)(2,1)S(1)} %all-to-all-done.text_ref.refs_0_), channel_id=1, source_target_pairs={{0,24},{8,0},{16,8},{24,16},{1,25},{9,1},{17,9},{25,17},{2,26},{10... | collective-permute-start | bytes 786440 | tf_op jit(solution)/shard_map/ppermute | solution.py:38
  62.5 10.0 %all-to-all-start.2 = ((f32[4,4,256]{2,1,0:T(4,128)}), f32[4,4,256]{2,1,0:T(4,128)S(1)}, u32[]{:S(2)}, u32[]{:S(2)}) async-start(f32[4,4,256]{2,1,0:T(4,128)} %shard_map.96.copies_ref), calls=%async_computation.2 | async-start | bytes 32768 | tf_op jit(solution)/shard_map/all_to_all | solution.py:271
  72.5 24.5 %all-to-all-start.3 = ((f32[16,32,128]{2,1,0:T(8,128)}), f32[16,32,128]{2,1,0:T(8,128)S(1)}, u32[]{:S(2)}, u32[]{:S(2)}) async-start(f32[16,32,128]{2,1,0:T(8,128)} %shard_map.97), calls=%async_computation.3 | async-start | bytes 524288 | tf_op jit(solution)/shard_map/all_to_all | solution.py:282
  88.0 21.8 %collective-permute-start.6 = (bf16[1024,256]{1,0:T(8,128)(2,1)}, bf16[1024,256]{1,0:T(8,128)(2,1)S(1)}, u32[]{:S(2)}, u32[]{:S(2)}) collective-permute-start(bf16[1024,256]{1,0:T(8,128)(2,1)} %get-tuple-element.23), channel_id=1, source_target_pairs={{0,8},{8,16},{16,24},{24,0},{1,9},{9,17},{17,25},{25,1},{2,10},{10... | collective-permute-start | bytes 1572872 | tf_op jit(solution)/shard_map/ppermute | solution.py:38
  91.7 18.5 %collective-permute-start.7 = (bf16[1024,256]{1,0:T(8,128)(2,1)}, bf16[1024,256]{1,0:T(8,128)(2,1)S(1)}, u32[]{:S(2)}, u32[]{:S(2)}) collective-permute-start(bf16[1024,256]{1,0:T(8,128)(2,1)} %get-tuple-element.24), channel_id=1, source_target_pairs={{0,16},{8,24},{16,0},{24,8},{1,17},{9,25},{17,1},{25,9},{2,18},{10... | collective-permute-start | bytes 1572872 | tf_op jit(solution)/shard_map/ppermute | solution.py:38
  94.7 21.6 %collective-permute-start.8 = (bf16[1024,256]{1,0:T(8,128)(2,1)}, bf16[1024,256]{1,0:T(8,128)(2,1)S(1)}, u32[]{:S(2)}, u32[]{:S(2)}) collective-permute-start(bf16[1024,256]{1,0:T(8,128)(2,1)} %get-tuple-element.25), channel_id=1, source_target_pairs={{0,24},{8,0},{16,8},{24,16},{1,25},{9,1},{17,9},{25,17},{2,26},{10... | collective-permute-start | bytes 1572872 | tf_op jit(solution)/shard_map/ppermute | solution.py:38
  97.8 24.5 %all-to-all-start.4 = ((bf16[16,4,1024]{2,1,0:T(4,128)(2,1)}), bf16[16,4,1024]{2,1,0:T(4,128)(2,1)S(1)}, u32[]{:S(2)}, u32[]{:S(2)}) async-start(bf16[16,4,1024]{2,1,0:T(4,128)(2,1)} %broadcast_in_dim.66), calls=%async_computation.4 | async-start | bytes 262144 | tf_op jit(solution)/shard_map/all_to_all | solution.py:33
  122.3 26.7 %all-to-all-start.5 = ((bf16[16,64,256]{2,1,0:T(8,128)(2,1)}), bf16[16,64,256]{2,1,0:T(8,128)(2,1)S(1)}, u32[]{:S(2)}, u32[]{:S(2)}) async-start(bf16[16,64,256]{2,1,0:T(8,128)(2,1)} %bitcast.18), calls=%async_computation.5 | async-start | bytes 1048576 | tf_op jit(solution)/shard_map/all_to_all | solution.py:314
  129.1 10.1 %collective-permute-start.10 = (bf16[16,4,1024]{2,1,0:T(4,128)(2,1)S(1)}, bf16[16,4,1024]{2,1,0:T(4,128)(2,1)S(1)}, u32[]{:S(2)}, u32[]{:S(2)}) collective-permute-start(bf16[16,4,1024]{2,1,0:T(4,128)(2,1)S(1)} %all-to-all-done.4), channel_id=1, source_target_pairs={{0,16},{8,24},{16,0},{24,8},{1,17},{9,25},{17,1},{25,9},{2,18},{10... | collective-permute-start | bytes 393224 | tf_op jit(solution)/shard_map/ppermute | solution.py:38
  132.1 8.2 %collective-permute-start.11 = (bf16[16,4,1024]{2,1,0:T(4,128)(2,1)S(1)}, bf16[16,4,1024]{2,1,0:T(4,128)(2,1)S(1)}, u32[]{:S(2)}, u32[]{:S(2)}) collective-permute-start(bf16[16,4,1024]{2,1,0:T(4,128)(2,1)S(1)} %all-to-all-done.4), channel_id=1, source_target_pairs={{0,24},{8,0},{16,8},{24,16},{1,25},{9,1},{17,9},{25,17},{2,26},{10... | collective-permute-start | bytes 393224 | tf_op jit(solution)/shard_map/ppermute | solution.py:38
  134.4 7.2 %collective-permute-start.9 = (bf16[16,4,1024]{2,1,0:T(4,128)(2,1)S(1)}, bf16[16,4,1024]{2,1,0:T(4,128)(2,1)S(1)}, u32[]{:S(2)}, u32[]{:S(2)}) collective-permute-start(bf16[16,4,1024]{2,1,0:T(4,128)(2,1)S(1)} %all-to-all-done.4), channel_id=1, source_target_pairs={{0,8},{8,16},{16,24},{24,0},{1,9},{9,17},{17,25},{25,1},{2,10},{10... | collective-permute-start | bytes 393224 | tf_op jit(solution)/shard_map/ppermute | solution.py:38

commit v7 on v6

--- a/solution.py
+++ b/solution.py
@@ -128,7 +128,8 @@
                 probs = jnp.exp2(scores[here] - (shift + off))
                 ds_scr[here] = (probs * (dprobs[here] - delta)).astype(BF16)
             dq += dot(kv_ref[0].T, ds_scr[...], NN)
-        dq_ref[c * per : (c + 1) * per] = (dq * SCALE).T.reshape(per, dq_ref.shape[1], HEAD_WIDTH)
+        dq = (dq * SCALE).T.reshape(per, dq_ref.shape[1], HEAD_WIDTH)
+        dq_ref[c * per : (c + 1) * per] = dq.astype(BF16)
 
 
 def token_kernel(near_ref, kv_ref, off_ref, norm_ref, far_vision_ref, *refs):
@@ -169,7 +170,7 @@
 
 
 def sum_kernel(parts_ref, out_ref):
-    out_ref[...] = jnp.sum(parts_ref[...], axis=0).astype(BF16)
+    out_ref[...] = jnp.sum(parts_ref[...].astype(F32), axis=0).astype(BF16)
 
 
 def turn_kernel(near_ref, vision_ref, out_ref):
@@ -272,14 +273,13 @@
 
     dq = pl.pallas_call(
         query_kernel,
-        out_shape=jax.ShapeDtypeStruct((far, lines, HEAD_WIDTH), F32),
+        out_shape=jax.ShapeDtypeStruct((far, lines, HEAD_WIDTH), BF16),
         in_specs=[WHOLE] * (3 + near),
         out_specs=WHOLE,
         scratch_shapes=[pltpu.VMEM((kv_rows, CHUNK), BF16)],
         compiler_params=PARAMS,
     )(text, own_off, norms, *all_kv)
     dq, all_norm = lax.optimization_barrier((dq, all_norm))
-    dq = lax.all_to_all(dq, FAR, 0, 0, tiled=True)
 
     sums = pl.pallas_call(
         token_kernel,
@@ -297,6 +297,8 @@
         cost_estimate=HEAVY,
     )(near_id, own_kv, all_off, all_norm, turned, *all_text)
 
+    sums, dq = lax.optimization_barrier((sums, dq))
+    dq = lax.all_to_all(dq, FAR, 0, 0, tiled=True)
     got = [sums[0]] + [shifted(sums[k], NEAR, k) for k in range(1, near)]
 
     dq = pl.pallas_call(

time: 151 us -> 151 us (level)
  waiting for transfers between devices: 28.9 us -> 32.5 us
  starting transfers between devices: 92.5 us -> 88.9 us
    all_to_all x1, waiting for transfers between devices: 0.01 us -> 3.57 us  [shards(): dq = lax.all_to_all(dq, FAR, 0, 0, tiled=True)]
    all_to_all x1, starting transfers between devices: 12 us -> 8.46 us  [from_everyone(): lax.all_to_all(jnp.broadcast_to(x[None], (peers, *x.shape)), axis, 0, 0,...]
  transfers between devices with their start and end apart: 18 -> 18, of which waited for: 8 -> 9; matrix products, arithmetic and copies ran while one was open for 4% -> 4% of each run, Pallas kernels for 10% -> 6%
where the time goes in v7:
time: 151 us; the launch traced here: 150 us
  starting transfers between devices  88.9 us (59%)
  waiting for transfers between devices  32.5 us (22%)
  Pallas kernels  17.8 us (12%)
  local copies, waits for them, and re-layouts  5.33 us (4%)
  other arithmetic  4.22 us (3%)
    ppermute x12, starting transfers between devices, shifted(): lax.ppermute(x, axis, [(i, (i + step) % peers) for i in range(peers)])  38.1 us
    all_to_all x1, starting transfers between devices, shards(): text = lax.all_to_all(own_text, FAR, 0, 0, tiled=True)  14.8 us
    all_to_all x1, starting transfers between devices, shards(): dq = lax.all_to_all(dq, FAR, 0, 0, tiled=True)  9.43 us
    ppermute x12, waiting for transfers between devices, shifted(): lax.ppermute(x, axis, [(i, (i + step) % peers) for i in range(peers)])  9.02 us
    all_to_all x1, starting transfers between devices, from_everyone(): lax.all_to_all(jnp.broadcast_to(x[None], (peers, *x.shape)), axis, 0, 0,...  8.46 us
    all_to_all x1, waiting for transfers between devices, shards(): text = lax.all_to_all(own_text, FAR, 0, 0, tiled=True)  7.19 us
    all_to_all x1, starting transfers between devices, shards(): lax.all_to_all(weights.reshape(far, part, 2 * HEAD_WIDTH), FAR, 0, 0, til...  6.87 us
    all_to_all x1, starting transfers between devices, shards(): all_norm = lax.all_to_all(norms, NEAR, 0, 0, tiled=True)  6.46 us
  transfers between devices with their start and end apart: 18, of which 9 were waited for; matrix products, arithmetic and copies ran while one was open for 4% of the time, Pallas kernels for 6%

profile of v7, /device:TPU:14, one launch (start us, length us, event | category | flops | bytes accessed | tf_op | source)
XLA Modules:
  0.0 149.7 jit_solution(12803426765879561817)
XLA Ops:
  0.6 0.7 stack_reshape.6
  1.3 0.7 stack_reshape.7
  2.1 0.8 broadcast_in_dim.32
  2.8 1.0 pad_maximum_fusion.1.refs_0_.kv_ref
  3.8 2.4 %collective-permute-start = (bf16[2,512,128]{2,1,0:T(8,128)(2,1)S(1)}, bf16[2,512,128]{2,1,0:T(8,128)(2,1)S(1)}, u32[]{:S(2)}, u32[]{:S(2)}) collective-permute-start(bf16[2,512,128]{2,1,0:T(8,128)(2,1)S(1)} %pad_maximum_fusion.1.refs_0_.kv_ref), channel_id=1, source_target_pairs={{0,8},{8,16},{16,24},{24,0},{1,9},{9,17},{17,25},{25,1},{2,10},{10... | collective-permute-start | bytes 786440 | tf_op jit(solution)/shard_map/ppermute | solution.py:38
  6.2 4.3 %collective-permute-start.1 = (bf16[2,512,128]{2,1,0:T(8,128)(2,1)S(1)}, bf16[2,512,128]{2,1,0:T(8,128)(2,1)S(1)}, u32[]{:S(2)}, u32[]{:S(2)}) collective-permute-start(bf16[2,512,128]{2,1,0:T(8,128)(2,1)S(1)} %pad_maximum_fusion.1.refs_0_.kv_ref), channel_id=1, source_target_pairs={{0,16},{8,24},{16,0},{24,8},{1,17},{9,25},{17,1},{25,9},{2,18},{10... | collective-permute-start | bytes 786440 | tf_op jit(solution)/shard_map/ppermute | solution.py:38
  10.5 1.9 %collective-permute-start.2 = (bf16[2,512,128]{2,1,0:T(8,128)(2,1)S(1)}, bf16[2,512,128]{2,1,0:T(8,128)(2,1)S(1)}, u32[]{:S(2)}, u32[]{:S(2)}) collective-permute-start(bf16[2,512,128]{2,1,0:T(8,128)(2,1)S(1)} %pad_maximum_fusion.1.refs_0_.kv_ref), channel_id=1, source_target_pairs={{0,24},{8,0},{16,8},{24,16},{1,25},{9,1},{17,9},{25,17},{2,26},{10... | collective-permute-start | bytes 786440 | tf_op jit(solution)/shard_map/ppermute | solution.py:38
  12.5 14.8 %all-to-all-start = ((bf16[16,2,32,128]{3,2,1,0:T(8,128)(2,1)}), bf16[16,2,32,128]{3,2,1,0:T(8,128)(2,1)S(1)}, u32[]{:S(2)}, u32[]{:S(2)}) async-start(bf16[16,2,32,128]{3,2,1,0:T(8,128)(2,1)} %broadcast_in_dim.32), calls=%async_computation | async-start | bytes 524288 | tf_op jit(solution)/shard_map/all_to_all | solution.py:223
  27.3 0.1 add_multiply_fusion
  27.4 0.8 slice_bitcast_fusion
  28.1 0.1 iota_add_fusion
  28.2 0.1 add_bitcast_fusion
  28.3 0.8 select_reduce_fusion.2
  29.1 0.1 convert_reduce_fusion.1
  29.2 0.1 select_reduce_fusion.1
  29.3 0.1 add.140
  29.4 5.2 %shard_map.94 = bf16[4,16,64,512]{3,2,1,0:T(8,128)(2,1)} custom-call(s32[1]{0:T(128)} %bitcast.near_ref, bf16[512,4096]{1,0:T(8,128)(2,1)} %vision_ref.1), custom_call_target="tpu_custom_call" | custom-call | tf_op jit(solution)/shard_map/pallas_call | solution.py:245
  34.6 0.1 and_select_fusion.off_ref
  34.7 7.2 %all-to-all-done.text_ref.refs_0_ = bf16[16,2,32,128]{3,2,1,0:T(8,128)(2,1)S(1)} async-done(((bf16[16,2,32,128]{3,2,1,0:T(8,128)(2,1)}), bf16[16,2,32,128]{3,2,1,0:T(8,128)(2,1)S(1)}, u32[]{:S(2)}, u32[]{:S(2)}) %all-to-all-start) | async-done | bytes 262176 | tf_op jit(solution)/shard_map/all_to_all | solution.py:223
  41.9 0.0 collective-permute-done.refs_1_
  41.9 0.0 collective-permute-done.1.refs_2_
  41.9 0.0 collective-permute-done.2.refs_3_
  41.9 2.5 %shard_map.95 = f32[16,6,256]{2,1,0:T(8,128)} custom-call(bf16[16,2,32,128]{3,2,1,0:T(8,128)(2,1)S(1)} %all-to-all-done.text_ref.refs_0_, f32[2,16,256]{2,1,0:T(8,128)S(1)} %and_select_fusion.off_ref, bf16[2,512,128]{2,1,0:T(8,128)(2,1)S(1)} %pad_maximum_fusion.1.refs_0_.kv_ref, bf16[2,512,128]{2,1,0:T(8,128)(2,1)S(1)} %collective-permute-done.refs_1_, ...), custom_call_target="tpu_custom_call" | custom-call | tf_op jit(solution)/shard_map/pallas_call | solution.py:256
  44.4 4.8 %all-to-all-start.1 = ((f32[16,6,256]{2,1,0:T(8,128)}), f32[16,6,256]{2,1,0:T(8,128)S(1)}, u32[]{:S(2)}, u32[]{:S(2)}) async-start(f32[16,6,256]{2,1,0:T(8,128)} %shard_map.95), calls=%async_computation.1 | async-start | bytes 262144 | tf_op jit(solution)/shard_map/all_to_all | solution.py:264
  49.2 5.1 %collective-permute-start.3 = (bf16[16,2,32,128]{3,2,1,0:T(8,128)(2,1)S(1)}, bf16[16,2,32,128]{3,2,1,0:T(8,128)(2,1)S(1)}, u32[]{:S(2)}, u32[]{:S(2)}) collective-permute-start(bf16[16,2,32,128]{3,2,1,0:T(8,128)(2,1)S(1)} %all-to-all-done.text_ref.refs_0_), channel_id=1, source_target_pairs={{0,8},{8,16},{16,24},{24,0},{1,9},{9,17},{17,25},{25,1},{2,10},{10... | collective-permute-start | bytes 786440 | tf_op jit(solution)/shard_map/ppermute | solution.py:38
  54.4 1.9 %collective-permute-start.4 = (bf16[16,2,32,128]{3,2,1,0:T(8,128)(2,1)S(1)}, bf16[16,2,32,128]{3,2,1,0:T(8,128)(2,1)S(1)}, u32[]{:S(2)}, u32[]{:S(2)}) collective-permute-start(bf16[16,2,32,128]{3,2,1,0:T(8,128)(2,1)S(1)} %all-to-all-done.text_ref.refs_0_), channel_id=1, source_target_pairs={{0,16},{8,24},{16,0},{24,8},{1,17},{9,25},{17,1},{25,9},{2,18},{10... | collective-permute-start | bytes 786440 | tf_op jit(solution)/shard_map/ppermute | solution.py:38
  56.3 3.3 %collective-permute-start.5 = (bf16[16,2,32,128]{3,2,1,0:T(8,128)(2,1)S(1)}, bf16[16,2,32,128]{3,2,1,0:T(8,128)(2,1)S(1)}, u32[]{:S(2)}, u32[]{:S(2)}) collective-permute-start(bf16[16,2,32,128]{3,2,1,0:T(8,128)(2,1)S(1)} %all-to-all-done.text_ref.refs_0_), channel_id=1, source_target_pairs={{0,24},{8,0},{16,8},{24,16},{1,25},{9,1},{17,9},{25,17},{2,26},{10... | collective-permute-start | bytes 786440 | tf_op jit(solution)/shard_map/ppermute | solution.py:38
  59.7 2.1 %all-to-all-done.1.stats_ref = f32[16,6,256]{2,1,0:T(8,128)S(1)} async-done(((f32[16,6,256]{2,1,0:T(8,128)}), f32[16,6,256]{2,1,0:T(8,128)S(1)}, u32[]{:S(2)}, u32[]{:S(2)}) %all-to-all-start.1) | async-done | bytes 98336 | tf_op jit(solution)/shard_map/all_to_all | solution.py:264
  61.9 0.7 shard_map.96.copies_ref
  62.5 6.5 %all-to-all-start.2 = ((f32[4,4,256]{2,1,0:T(4,128)}), f32[4,4,256]{2,1,0:T(4,128)S(1)}, u32[]{:S(2)}, u32[]{:S(2)}) async-start(f32[4,4,256]{2,1,0:T(4,128)} %shard_map.96.copies_ref), calls=%async_computation.2 | async-start | bytes 32768 | tf_op jit(solution)/shard_map/all_to_all | solution.py:272
  69.0 0.1 and_select_fusion.1.off_ref
  69.1 3.4 %shard_map.97 = bf16[16,32,128]{2,1,0:T(8,128)(2,1)} custom-call(bf16[16,2,32,128]{3,2,1,0:T(8,128)(2,1)S(1)} %all-to-all-done.text_ref.refs_0_, f32[2,16,256]{2,1,0:T(8,128)S(1)} %and_select_fusion.off_ref, f32[4,4,256]{2,1,0:T(4,128)} %shard_map.96.copies_ref, bf16[2,512,128]{2,1,0:T(8,128)(2,1)S(1)} %pad_maximum_fusion.1.refs_0_.kv_ref, ...), custom_call_target="tpu_custom_call" | custom-call | tf_op jit(solution)/shard_map/pallas_call | solution.py:274
  72.5 0.0 all-to-all-done.2.norm_ref
  72.5 0.0 collective-permute-done.3.refs_1_
  72.5 0.0 collective-permute-done.4.refs_2_
  72.5 0.0 collective-permute-done.5.refs_3_
  72.5 6.0 %shard_map.98 = (bf16[1024,256]{1,0:T(8,128)(2,1)S(1)}, bf16[1024,256]{1,0:T(8,128)(2,1)}, bf16[1024,256]{1,0:T(8,128)(2,1)}, bf16[1024,256]{1,0:T(8,128)(2,1)}) custom-call(s32[1]{0:T(128)} %bitcast.near_ref, bf16[2,512,128]{2,1,0:T(8,128)(2,1)S(1)} %pad_maximum_fusion.1.refs_0_.kv_ref, f32[4,2,4,256]{3,2,1,0:T(4,128)S(1)} %and_select_fusion.1.off_ref, ...), custom_call_target="tpu_custom_call" | custom-call | flops 99999997952 | bytes 1048576 | tf_op jit(solution)/shard_map/pallas_call | solution.py:284
  78.5 9.4 %all-to-all-start.3 = ((bf16[16,32,128]{2,1,0:T(8,128)(2,1)}), bf16[16,32,128]{2,1,0:T(8,128)(2,1)S(1)}, u32[]{:S(2)}, u32[]{:S(2)}) async-start(bf16[16,32,128]{2,1,0:T(8,128)(2,1)} %shard_map.97), calls=%async_computation.3 | async-start | bytes 262144 | tf_op jit(solution)/shard_map/all_to_all | solution.py:301
  87.9 3.8 %collective-permute-start.6 = (bf16[1024,256]{1,0:T(8,128)(2,1)}, bf16[1024,256]{1,0:T(8,128)(2,1)S(1)}, u32[]{:S(2)}, u32[]{:S(2)}) collective-permute-start(bf16[1024,256]{1,0:T(8,128)(2,1)} %get-tuple-element.33), channel_id=1, source_target_pairs={{0,8},{8,16},{16,24},{24,0},{1,9},{9,17},{17,25},{25,1},{2,10},{10... | collective-permute-start | bytes 1572872 | tf_op jit(solution)/shard_map/ppermute | solution.py:38
  91.7 2.9 %collective-permute-start.7 = (bf16[1024,256]{1,0:T(8,128)(2,1)}, bf16[1024,256]{1,0:T(8,128)(2,1)S(1)}, u32[]{:S(2)}, u32[]{:S(2)}) collective-permute-start(bf16[1024,256]{1,0:T(8,128)(2,1)} %get-tuple-element.34), channel_id=1, source_target_pairs={{0,16},{8,24},{16,0},{24,8},{1,17},{9,25},{17,1},{25,9},{2,18},{10... | collective-permute-start | bytes 1572872 | tf_op jit(solution)/shard_map/ppermute | solution.py:38
  94.7 2.3 %collective-permute-start.8 = (bf16[1024,256]{1,0:T(8,128)(2,1)}, bf16[1024,256]{1,0:T(8,128)(2,1)S(1)}, u32[]{:S(2)}, u32[]{:S(2)}) collective-permute-start(bf16[1024,256]{1,0:T(8,128)(2,1)} %get-tuple-element.35), channel_id=1, source_target_pairs={{0,24},{8,0},{16,8},{24,16},{1,25},{9,1},{17,9},{25,17},{2,26},{10... | collective-permute-start | bytes 1572872 | tf_op jit(solution)/shard_map/ppermute | solution.py:38
  97.0 3.6 %all-to-all-done.3.parts_ref = bf16[16,32,128]{2,1,0:T(8,128)(2,1)S(1)} async-done(((bf16[16,32,128]{2,1,0:T(8,128)(2,1)}), bf16[16,32,128]{2,1,0:T(8,128)(2,1)S(1)}, u32[]{:S(2)}, u32[]{:S(2)}) %all-to-all-start.3) | async-done | bytes 131104 | tf_op jit(solution)/shard_map/all_to_all | solution.py:301
  100.6 0.7 broadcast_in_dim.66
  101.3 8.5 %all-to-all-start.4 = ((bf16[16,4,1024]{2,1,0:T(4,128)(2,1)}), bf16[16,4,1024]{2,1,0:T(4,128)(2,1)S(1)}, u32[]{:S(2)}, u32[]{:S(2)}) async-start(bf16[16,4,1024]{2,1,0:T(4,128)(2,1)} %broadcast_in_dim.66), calls=%async_computation.4 | async-start | bytes 262144 | tf_op jit(solution)/shard_map/all_to_all | solution.py:33
  109.8 0.0 collective-permute-done.6
  109.8 0.4 collective-permute-done.7
  110.2 6.1 %collective-permute-done.8 = bf16[1024,256]{1,0:T(8,128)(2,1)S(1)} collective-permute-done((bf16[1024,256]{1,0:T(8,128)(2,1)}, bf16[1024,256]{1,0:T(8,128)(2,1)S(1)}, u32[]{:S(2)}, u32[]{:S(2)}) %collective-permute-start.8) | collective-permute-done | bytes 524320 | tf_op jit(solution)/shard_map/ppermute | solution.py:38
  116.3 1.1 add_convert_fusion
  117.4 4.9 %all-to-all-done.4 = bf16[16,4,1024]{2,1,0:T(4,128)(2,1)S(1)} async-done(((bf16[16,4,1024]{2,1,0:T(4,128)(2,1)}), bf16[16,4,1024]{2,1,0:T(4,128)(2,1)S(1)}, u32[]{:S(2)}, u32[]{:S(2)}) %all-to-all-start.4) | async-done | bytes 131104 | tf_op jit(solution)/shard_map/all_to_all | solution.py:33
  122.2 6.9 %all-to-all-start.5 = ((bf16[16,64,256]{2,1,0:T(8,128)(2,1)}), bf16[16,64,256]{2,1,0:T(8,128)(2,1)S(1)}, u32[]{:S(2)}, u32[]{:S(2)}) async-start(bf16[16,64,256]{2,1,0:T(8,128)(2,1)} %bitcast.18), calls=%async_computation.5 | async-start | bytes 1048576 | tf_op jit(solution)/shard_map/all_to_all | solution.py:316
  129.1 2.9 %collective-permute-start.10 = (bf16[16,4,1024]{2,1,0:T(4,128)(2,1)S(1)}, bf16[16,4,1024]{2,1,0:T(4,128)(2,1)S(1)}, u32[]{:S(2)}, u32[]{:S(2)}) collective-permute-start(bf16[16,4,1024]{2,1,0:T(4,128)(2,1)S(1)} %all-to-all-done.4), channel_id=1, source_target_pairs={{0,16},{8,24},{16,0},{24,8},{1,17},{9,25},{17,1},{25,9},{2,18},{10... | collective-permute-start | bytes 393224 | tf_op jit(solution)/shard_map/ppermute | solution.py:38
  132.1 2.3 %collective-permute-start.11 = (bf16[16,4,1024]{2,1,0:T(4,128)(2,1)S(1)}, bf16[16,4,1024]{2,1,0:T(4,128)(2,1)S(1)}, u32[]{:S(2)}, u32[]{:S(2)}) collective-permute-start(bf16[16,4,1024]{2,1,0:T(4,128)(2,1)S(1)} %all-to-all-done.4), channel_id=1, source_target_pairs={{0,24},{8,0},{16,8},{24,16},{1,25},{9,1},{17,9},{25,17},{2,26},{10... | collective-permute-start | bytes 393224 | tf_op jit(solution)/shard_map/ppermute | solution.py:38
  134.4 4.7 %collective-permute-start.9 = (bf16[16,4,1024]{2,1,0:T(4,128)(2,1)S(1)}, bf16[16,4,1024]{2,1,0:T(4,128)(2,1)S(1)}, u32[]{:S(2)}, u32[]{:S(2)}) collective-permute-start(bf16[16,4,1024]{2,1,0:T(4,128)(2,1)S(1)} %all-to-all-done.4), channel_id=1, source_target_pairs={{0,8},{8,16},{16,24},{24,0},{1,9},{9,17},{17,25},{25,1},{2,10},{10... | collective-permute-start | bytes 393224 | tf_op jit(solution)/shard_map/ppermute | solution.py:38
  139.2 0.0 collective-permute-done.10
  139.2 1.1 collective-permute-done.11
  140.3 1.4 collective-permute-done.9
  141.6 0.3 select_bitcast_fusion.3
  141.9 0.4 pad_maximum_fusion
  142.4 0.9 reshape.237
  143.3 5.7 %all-to-all-done.5 = bf16[16,64,256]{2,1,0:T(8,128)(2,1)S(1)} async-done(((bf16[16,64,256]{2,1,0:T(8,128)(2,1)}), bf16[16,64,256]{2,1,0:T(8,128)(2,1)S(1)}, u32[]{:S(2)}, u32[]{:S(2)}) %all-to-all-start.5) | async-done | bytes 524320 | tf_op jit(solution)/shard_map/all_to_all | solution.py:316
  149.0 0.1 convert_reduce_fusion
  149.0 0.6 fusion.10
  (13 shorter events, 0.1 us)
Async XLA Ops:
  3.8 38.1 %collective-permute-start = (bf16[2,512,128]{2,1,0:T(8,128)(2,1)S(1)}, bf16[2,512,128]{2,1,0:T(8,128)(2,1)S(1)}, u32[]{:S(2)}, u32[]{:S(2)}) collective-permute-start(bf16[2,512,128]{2,1,0:T(8,128)(2,1)S(1)} %pad_maximum_fusion.1.refs_0_.kv_ref), channel_id=1, source_target_pairs={{0,8},{8,16},{16,24},{24,0},{1,9},{9,17},{17,25},{25,1},{2,10},{10... | collective-permute-start | bytes 786440 | tf_op jit(solution)/shard_map/ppermute | solution.py:38
  6.2 35.7 %collective-permute-start.1 = (bf16[2,512,128]{2,1,0:T(8,128)(2,1)S(1)}, bf16[2,512,128]{2,1,0:T(8,128)(2,1)S(1)}, u32[]{:S(2)}, u32[]{:S(2)}) collective-permute-start(bf16[2,512,128]{2,1,0:T(8,128)(2,1)S(1)} %pad_maximum_fusion.1.refs_0_.kv_ref), channel_id=1, source_target_pairs={{0,16},{8,24},{16,0},{24,8},{1,17},{9,25},{17,1},{25,9},{2,18},{10... | collective-permute-start | bytes 786440 | tf_op jit(solution)/shard_map/ppermute | solution.py:38
  10.5 31.4 %collective-permute-start.2 = (bf16[2,512,128]{2,1,0:T(8,128)(2,1)S(1)}, bf16[2,512,128]{2,1,0:T(8,128)(2,1)S(1)}, u32[]{:S(2)}, u32[]{:S(2)}) collective-permute-start(bf16[2,512,128]{2,1,0:T(8,128)(2,1)S(1)} %pad_maximum_fusion.1.refs_0_.kv_ref), channel_id=1, source_target_pairs={{0,24},{8,0},{16,8},{24,16},{1,25},{9,1},{17,9},{25,17},{2,26},{10... | collective-permute-start | bytes 786440 | tf_op jit(solution)/shard_map/ppermute | solution.py:38
  12.5 29.4 %all-to-all-start = ((bf16[16,2,32,128]{3,2,1,0:T(8,128)(2,1)}), bf16[16,2,32,128]{3,2,1,0:T(8,128)(2,1)S(1)}, u32[]{:S(2)}, u32[]{:S(2)}) async-start(bf16[16,2,32,128]{3,2,1,0:T(8,128)(2,1)} %broadcast_in_dim.32), calls=%async_computation | async-start | bytes 524288 | tf_op jit(solution)/shard_map/all_to_all | solution.py:223
  44.4 17.5 %all-to-all-start.1 = ((f32[16,6,256]{2,1,0:T(8,128)}), f32[16,6,256]{2,1,0:T(8,128)S(1)}, u32[]{:S(2)}, u32[]{:S(2)}) async-start(f32[16,6,256]{2,1,0:T(8,128)} %shard_map.95), calls=%async_computation.1 | async-start | bytes 262144 | tf_op jit(solution)/shard_map/all_to_all | solution.py:264
  49.2 23.2 %collective-permute-start.3 = (bf16[16,2,32,128]{3,2,1,0:T(8,128)(2,1)S(1)}, bf16[16,2,32,128]{3,2,1,0:T(8,128)(2,1)S(1)}, u32[]{:S(2)}, u32[]{:S(2)}) collective-permute-start(bf16[16,2,32,128]{3,2,1,0:T(8,128)(2,1)S(1)} %all-to-all-done.text_ref.refs_0_), channel_id=1, source_target_pairs={{0,8},{8,16},{16,24},{24,0},{1,9},{9,17},{17,25},{25,1},{2,10},{10... | collective-permute-start | bytes 786440 | tf_op jit(solution)/shard_map/ppermute | solution.py:38
  54.4 18.1 %collective-permute-start.4 = (bf16[16,2,32,128]{3,2,1,0:T(8,128)(2,1)S(1)}, bf16[16,2,32,128]{3,2,1,0:T(8,128)(2,1)S(1)}, u32[]{:S(2)}, u32[]{:S(2)}) collective-permute-start(bf16[16,2,32,128]{3,2,1,0:T(8,128)(2,1)S(1)} %all-to-all-done.text_ref.refs_0_), channel_id=1, source_target_pairs={{0,16},{8,24},{16,0},{24,8},{1,17},{9,25},{17,1},{25,9},{2,18},{10... | collective-permute-start | bytes 786440 | tf_op jit(solution)/shard_map/ppermute | solution.py:38
  56.3 16.2 %collective-permute-start.5 = (bf16[16,2,32,128]{3,2,1,0:T(8,128)(2,1)S(1)}, bf16[16,2,32,128]{3,2,1,0:T(8,128)(2,1)S(1)}, u32[]{:S(2)}, u32[]{:S(2)}) collective-permute-start(bf16[16,2,32,128]{3,2,1,0:T(8,128)(2,1)S(1)} %all-to-all-done.text_ref.refs_0_), channel_id=1, source_target_pairs={{0,24},{8,0},{16,8},{24,16},{1,25},{9,1},{17,9},{25,17},{2,26},{10... | collective-permute-start | bytes 786440 | tf_op jit(solution)/shard_map/ppermute | solution.py:38
  62.5 9.9 %all-to-all-start.2 = ((f32[4,4,256]{2,1,0:T(4,128)}), f32[4,4,256]{2,1,0:T(4,128)S(1)}, u32[]{:S(2)}, u32[]{:S(2)}) async-start(f32[4,4,256]{2,1,0:T(4,128)} %shard_map.96.copies_ref), calls=%async_computation.2 | async-start | bytes 32768 | tf_op jit(solution)/shard_map/all_to_all | solution.py:272
  78.5 22.1 %all-to-all-start.3 = ((bf16[16,32,128]{2,1,0:T(8,128)(2,1)}), bf16[16,32,128]{2,1,0:T(8,128)(2,1)S(1)}, u32[]{:S(2)}, u32[]{:S(2)}) async-start(bf16[16,32,128]{2,1,0:T(8,128)(2,1)} %shard_map.97), calls=%async_computation.3 | async-start | bytes 262144 | tf_op jit(solution)/shard_map/all_to_all | solution.py:301
  87.9 21.8 %collective-permute-start.6 = (bf16[1024,256]{1,0:T(8,128)(2,1)}, bf16[1024,256]{1,0:T(8,128)(2,1)S(1)}, u32[]{:S(2)}, u32[]{:S(2)}) collective-permute-start(bf16[1024,256]{1,0:T(8,128)(2,1)} %get-tuple-element.33), channel_id=1, source_target_pairs={{0,8},{8,16},{16,24},{24,0},{1,9},{9,17},{17,25},{25,1},{2,10},{10... | collective-permute-start | bytes 1572872 | tf_op jit(solution)/shard_map/ppermute | solution.py:38
  91.7 18.5 %collective-permute-start.7 = (bf16[1024,256]{1,0:T(8,128)(2,1)}, bf16[1024,256]{1,0:T(8,128)(2,1)S(1)}, u32[]{:S(2)}, u32[]{:S(2)}) collective-permute-start(bf16[1024,256]{1,0:T(8,128)(2,1)} %get-tuple-element.34), channel_id=1, source_target_pairs={{0,16},{8,24},{16,0},{24,8},{1,17},{9,25},{17,1},{25,9},{2,18},{10... | collective-permute-start | bytes 1572872 | tf_op jit(solution)/shard_map/ppermute | solution.py:38
  94.7 21.6 %collective-permute-start.8 = (bf16[1024,256]{1,0:T(8,128)(2,1)}, bf16[1024,256]{1,0:T(8,128)(2,1)S(1)}, u32[]{:S(2)}, u32[]{:S(2)}) collective-permute-start(bf16[1024,256]{1,0:T(8,128)(2,1)} %get-tuple-element.35), channel_id=1, source_target_pairs={{0,24},{8,0},{16,8},{24,16},{1,25},{9,1},{17,9},{25,17},{2,26},{10... | collective-permute-start | bytes 1572872 | tf_op jit(solution)/shard_map/ppermute | solution.py:38
  101.3 20.9 %all-to-all-start.4 = ((bf16[16,4,1024]{2,1,0:T(4,128)(2,1)}), bf16[16,4,1024]{2,1,0:T(4,128)(2,1)S(1)}, u32[]{:S(2)}, u32[]{:S(2)}) async-start(bf16[16,4,1024]{2,1,0:T(4,128)(2,1)} %broadcast_in_dim.66), calls=%async_computation.4 | async-start | bytes 262144 | tf_op jit(solution)/shard_map/all_to_all | solution.py:33
  122.2 26.7 %all-to-all-start.5 = ((bf16[16,64,256]{2,1,0:T(8,128)(2,1)}), bf16[16,64,256]{2,1,0:T(8,128)(2,1)S(1)}, u32[]{:S(2)}, u32[]{:S(2)}) async-start(bf16[16,64,256]{2,1,0:T(8,128)(2,1)} %bitcast.18), calls=%async_computation.5 | async-start | bytes 1048576 | tf_op jit(solution)/shard_map/all_to_all | solution.py:316
  129.1 10.0 %collective-permute-start.10 = (bf16[16,4,1024]{2,1,0:T(4,128)(2,1)S(1)}, bf16[16,4,1024]{2,1,0:T(4,128)(2,1)S(1)}, u32[]{:S(2)}, u32[]{:S(2)}) collective-permute-start(bf16[16,4,1024]{2,1,0:T(4,128)(2,1)S(1)} %all-to-all-done.4), channel_id=1, source_target_pairs={{0,16},{8,24},{16,0},{24,8},{1,17},{9,25},{17,1},{25,9},{2,18},{10... | collective-permute-start | bytes 393224 | tf_op jit(solution)/shard_map/ppermute | solution.py:38
  132.1 8.2 %collective-permute-start.11 = (bf16[16,4,1024]{2,1,0:T(4,128)(2,1)S(1)}, bf16[16,4,1024]{2,1,0:T(4,128)(2,1)S(1)}, u32[]{:S(2)}, u32[]{:S(2)}) collective-permute-start(bf16[16,4,1024]{2,1,0:T(4,128)(2,1)S(1)} %all-to-all-done.4), channel_id=1, source_target_pairs={{0,24},{8,0},{16,8},{24,16},{1,25},{9,1},{17,9},{25,17},{2,26},{10... | collective-permute-start | bytes 393224 | tf_op jit(solution)/shard_map/ppermute | solution.py:38
  134.4 7.2 %collective-permute-start.9 = (bf16[16,4,1024]{2,1,0:T(4,128)(2,1)S(1)}, bf16[16,4,1024]{2,1,0:T(4,128)(2,1)S(1)}, u32[]{:S(2)}, u32[]{:S(2)}) collective-permute-start(bf16[16,4,1024]{2,1,0:T(4,128)(2,1)S(1)} %all-to-all-done.4), channel_id=1, source_target_pairs={{0,8},{8,16},{16,24},{24,0},{1,9},{9,17},{17,25},{25,1},{2,10},{10... | collective-permute-start | bytes 393224 | tf_op jit(solution)/shard_map/ppermute | solution.py:38

commit v8 on v6

--- a/solution.py
+++ b/solution.py
@@ -36,6 +36,13 @@
 def shifted(x, axis, step):
     peers = lax.axis_size(axis)
     return lax.ppermute(x, axis, [(i, (i + step) % peers) for i in range(peers)])
+
+
+def from_ring(xs, axis):
+    peers = lax.axis_size(axis)
+    order = sorted(range(1, peers), key=lambda k: -min(k, peers - k))
+    got = {k: shifted(xs[k], axis, k) for k in order}
+    return [xs[0]] + [got[k] for k in range(1, peers)]
 
 
 def dot(a, b, dims):
@@ -172,6 +179,12 @@
     out_ref[...] = jnp.sum(parts_ref[...], axis=0).astype(BF16)
 
 
+def total_kernel(parts_ref, key_ref, value_ref):
+    total = jnp.sum(parts_ref[...].astype(F32), axis=0)
+    key_ref[...] = total[:, :HEAD_WIDTH]
+    value_ref[...] = total[:, HEAD_WIDTH:]
+
+
 def turn_kernel(near_ref, vision_ref, out_ref):
     pieces, deep, size, _ = out_ref.shape
     for d in range(deep):
@@ -221,8 +234,8 @@
     )
     text = lax.all_to_all(own_text, FAR, 0, 0, tiled=True)
     own_kv = jnp.stack((vision_keys, video_value_rows))
-    all_kv = [own_kv] + [shifted(own_kv, NEAR, k) for k in range(1, near)]
-    all_text = [text] + [shifted(text, NEAR, k) for k in range(1, near)]
+    all_kv = from_ring([own_kv] * near, NEAR)
+    all_text = from_ring([text] * near, NEAR)
 
     line_ids = jnp.arange(far * lines, dtype=jnp.int32)
     sources = jnp.stack(bases_from(my_near, near))
@@ -297,7 +310,7 @@
         cost_estimate=HEAVY,
     )(near_id, own_kv, all_off, all_norm, turned, *all_text)
 
-    got = [sums[0]] + [shifted(sums[k], NEAR, k) for k in range(1, near)]
+    got = from_ring(sums, NEAR)
 
     dq = pl.pallas_call(
         sum_kernel,
@@ -314,11 +327,17 @@
     weights = lax.all_to_all(
         weights.reshape(far, part, 2 * HEAD_WIDTH), FAR, 0, 0, tiled=True
     )
-    all_dq = [dq] + [shifted(dq, NEAR, k) for k in range(1, near)]
+    all_dq = from_ring([dq] * near, NEAR)
     query_grad = jnp.stack([lax.select_n(base, *all_dq) for base in bases_from(my_near, near)], 1)
     query_grad = query_grad.reshape(peers * own_rows, -1)
-    weights = jnp.sum(weights.astype(F32), axis=0)
-    return query_grad, weights[:, :HEAD_WIDTH], weights[:, HEAD_WIDTH:]
+    key_weights, value_weights = pl.pallas_call(
+        total_kernel,
+        out_shape=[jax.ShapeDtypeStruct((part, HEAD_WIDTH), F32)] * 2,
+        in_specs=[WHOLE],
+        out_specs=[WHOLE] * 2,
+        compiler_params=PARAMS,
+    )(weights)
+    return query_grad, key_weights, value_weights
 
 
 def solution(mesh):

time: 151 us -> 151 us (level)
  no operation moved by 1% of the time
where the time goes in v8:
time: 151 us; the launch traced here: 150 us
  starting transfers between devices  92.5 us (61%)
  waiting for transfers between devices  28.9 us (19%)
  Pallas kernels  18.5 us (12%)
  local copies, waits for them, and re-layouts  4.68 us (3%)
  other arithmetic  4.15 us (3%)
    ppermute x12, starting transfers between devices, shifted(): lax.ppermute(x, axis, [(i, (i + step) % peers) for i in range(peers)])  38.1 us
    all_to_all x1, starting transfers between devices, shards(): text = lax.all_to_all(own_text, FAR, 0, 0, tiled=True)  14.8 us
    all_to_all x1, starting transfers between devices, from_everyone(): lax.all_to_all(jnp.broadcast_to(x[None], (peers, *x.shape)), axis, 0, 0,...  12 us
    all_to_all x1, starting transfers between devices, shards(): dq = lax.all_to_all(dq, FAR, 0, 0, tiled=True)  9.42 us
    ppermute x12, waiting for transfers between devices, shifted(): lax.ppermute(x, axis, [(i, (i + step) % peers) for i in range(peers)])  9.04 us
    all_to_all x1, waiting for transfers between devices, shards(): text = lax.all_to_all(own_text, FAR, 0, 0, tiled=True)  7.21 us
    all_to_all x1, starting transfers between devices, shards(): lax.all_to_all(weights.reshape(far, part, 2 * HEAD_WIDTH), FAR, 0, 0, til...  6.91 us
    all_to_all x1, starting transfers between devices, shards(): all_norm = lax.all_to_all(norms, NEAR, 0, 0, tiled=True)  6.45 us
  transfers between devices with their start and end apart: 18, of which 8 were waited for; matrix products, arithmetic and copies ran while one was open for 4% of the time, Pallas kernels for 10%

profile of v8, /device:TPU:14, one launch (start us, length us, event | category | flops | bytes accessed | tf_op | source)
XLA Modules:
  0.0 149.7 jit_solution(6628327413775138869)
XLA Ops:
  0.6 0.7 stack_reshape.6
  1.3 0.7 stack_reshape.7
  2.1 0.8 broadcast_in_dim.32
  2.8 1.0 pad_maximum_fusion.1.refs_0_.kv_ref
  3.8 2.4 %collective-permute-start = (bf16[2,512,128]{2,1,0:T(8,128)(2,1)S(1)}, bf16[2,512,128]{2,1,0:T(8,128)(2,1)S(1)}, u32[]{:S(2)}, u32[]{:S(2)}) collective-permute-start(bf16[2,512,128]{2,1,0:T(8,128)(2,1)S(1)} %pad_maximum_fusion.1.refs_0_.kv_ref), channel_id=1, source_target_pairs={{0,8},{8,16},{16,24},{24,0},{1,9},{9,17},{17,25},{25,1},{2,10},{10... | collective-permute-start | bytes 786440 | tf_op jit(solution)/shard_map/ppermute | solution.py:38
  6.2 4.3 %collective-permute-start.1 = (bf16[2,512,128]{2,1,0:T(8,128)(2,1)S(1)}, bf16[2,512,128]{2,1,0:T(8,128)(2,1)S(1)}, u32[]{:S(2)}, u32[]{:S(2)}) collective-permute-start(bf16[2,512,128]{2,1,0:T(8,128)(2,1)S(1)} %pad_maximum_fusion.1.refs_0_.kv_ref), channel_id=1, source_target_pairs={{0,16},{8,24},{16,0},{24,8},{1,17},{9,25},{17,1},{25,9},{2,18},{10... | collective-permute-start | bytes 786440 | tf_op jit(solution)/shard_map/ppermute | solution.py:38
  10.5 1.9 %collective-permute-start.2 = (bf16[2,512,128]{2,1,0:T(8,128)(2,1)S(1)}, bf16[2,512,128]{2,1,0:T(8,128)(2,1)S(1)}, u32[]{:S(2)}, u32[]{:S(2)}) collective-permute-start(bf16[2,512,128]{2,1,0:T(8,128)(2,1)S(1)} %pad_maximum_fusion.1.refs_0_.kv_ref), channel_id=1, source_target_pairs={{0,24},{8,0},{16,8},{24,16},{1,25},{9,1},{17,9},{25,17},{2,26},{10... | collective-permute-start | bytes 786440 | tf_op jit(solution)/shard_map/ppermute | solution.py:38
  12.5 14.8 %all-to-all-start = ((bf16[16,2,32,128]{3,2,1,0:T(8,128)(2,1)}), bf16[16,2,32,128]{3,2,1,0:T(8,128)(2,1)S(1)}, u32[]{:S(2)}, u32[]{:S(2)}) async-start(bf16[16,2,32,128]{3,2,1,0:T(8,128)(2,1)} %broadcast_in_dim.32), calls=%async_computation | async-start | bytes 524288 | tf_op jit(solution)/shard_map/all_to_all | solution.py:235
  27.3 0.1 add_multiply_fusion
  27.4 0.8 slice_bitcast_fusion
  28.1 0.1 iota_add_fusion
  28.2 0.1 add_bitcast_fusion
  28.3 0.8 select_reduce_fusion.2
  29.1 0.1 convert_reduce_fusion
  29.2 0.1 select_reduce_fusion.1
  29.3 0.1 add.140
  29.4 5.2 %shard_map.94 = bf16[4,16,64,512]{3,2,1,0:T(8,128)(2,1)} custom-call(s32[1]{0:T(128)} %bitcast.near_ref, bf16[512,4096]{1,0:T(8,128)(2,1)} %vision_ref.1), custom_call_target="tpu_custom_call" | custom-call | tf_op jit(solution)/shard_map/pallas_call | solution.py:257
  34.6 0.1 and_select_fusion.off_ref
  34.7 7.2 %all-to-all-done.text_ref.refs_0_ = bf16[16,2,32,128]{3,2,1,0:T(8,128)(2,1)S(1)} async-done(((bf16[16,2,32,128]{3,2,1,0:T(8,128)(2,1)}), bf16[16,2,32,128]{3,2,1,0:T(8,128)(2,1)S(1)}, u32[]{:S(2)}, u32[]{:S(2)}) %all-to-all-start) | async-done | bytes 262176 | tf_op jit(solution)/shard_map/all_to_all | solution.py:235
  41.9 0.0 collective-permute-done.refs_1_
  41.9 0.0 collective-permute-done.1.refs_2_
  41.9 0.0 collective-permute-done.2.refs_3_
  41.9 2.5 %shard_map.95 = f32[16,6,256]{2,1,0:T(8,128)} custom-call(bf16[16,2,32,128]{3,2,1,0:T(8,128)(2,1)S(1)} %all-to-all-done.text_ref.refs_0_, f32[2,16,256]{2,1,0:T(8,128)S(1)} %and_select_fusion.off_ref, bf16[2,512,128]{2,1,0:T(8,128)(2,1)S(1)} %pad_maximum_fusion.1.refs_0_.kv_ref, bf16[2,512,128]{2,1,0:T(8,128)(2,1)S(1)} %collective-permute-done.refs_1_, ...), custom_call_target="tpu_custom_call" | custom-call | tf_op jit(solution)/shard_map/pallas_call | solution.py:268
  44.4 4.8 %all-to-all-start.1 = ((f32[16,6,256]{2,1,0:T(8,128)}), f32[16,6,256]{2,1,0:T(8,128)S(1)}, u32[]{:S(2)}, u32[]{:S(2)}) async-start(f32[16,6,256]{2,1,0:T(8,128)} %shard_map.95), calls=%async_computation.1 | async-start | bytes 262144 | tf_op jit(solution)/shard_map/all_to_all | solution.py:276
  49.2 5.1 %collective-permute-start.3 = (bf16[16,2,32,128]{3,2,1,0:T(8,128)(2,1)S(1)}, bf16[16,2,32,128]{3,2,1,0:T(8,128)(2,1)S(1)}, u32[]{:S(2)}, u32[]{:S(2)}) collective-permute-start(bf16[16,2,32,128]{3,2,1,0:T(8,128)(2,1)S(1)} %all-to-all-done.text_ref.refs_0_), channel_id=1, source_target_pairs={{0,8},{8,16},{16,24},{24,0},{1,9},{9,17},{17,25},{25,1},{2,10},{10... | collective-permute-start | bytes 786440 | tf_op jit(solution)/shard_map/ppermute | solution.py:38
  54.4 2.0 %collective-permute-start.4 = (bf16[16,2,32,128]{3,2,1,0:T(8,128)(2,1)S(1)}, bf16[16,2,32,128]{3,2,1,0:T(8,128)(2,1)S(1)}, u32[]{:S(2)}, u32[]{:S(2)}) collective-permute-start(bf16[16,2,32,128]{3,2,1,0:T(8,128)(2,1)S(1)} %all-to-all-done.text_ref.refs_0_), channel_id=1, source_target_pairs={{0,16},{8,24},{16,0},{24,8},{1,17},{9,25},{17,1},{25,9},{2,18},{10... | collective-permute-start | bytes 786440 | tf_op jit(solution)/shard_map/ppermute | solution.py:38
  56.3 3.3 %collective-permute-start.5 = (bf16[16,2,32,128]{3,2,1,0:T(8,128)(2,1)S(1)}, bf16[16,2,32,128]{3,2,1,0:T(8,128)(2,1)S(1)}, u32[]{:S(2)}, u32[]{:S(2)}) collective-permute-start(bf16[16,2,32,128]{3,2,1,0:T(8,128)(2,1)S(1)} %all-to-all-done.text_ref.refs_0_), channel_id=1, source_target_pairs={{0,24},{8,0},{16,8},{24,16},{1,25},{9,1},{17,9},{25,17},{2,26},{10... | collective-permute-start | bytes 786440 | tf_op jit(solution)/shard_map/ppermute | solution.py:38
  59.7 2.1 %all-to-all-done.1.stats_ref = f32[16,6,256]{2,1,0:T(8,128)S(1)} async-done(((f32[16,6,256]{2,1,0:T(8,128)}), f32[16,6,256]{2,1,0:T(8,128)S(1)}, u32[]{:S(2)}, u32[]{:S(2)}) %all-to-all-start.1) | async-done | bytes 98336 | tf_op jit(solution)/shard_map/all_to_all | solution.py:276
  61.9 0.7 shard_map.96.copies_ref
  62.5 6.5 %all-to-all-start.2 = ((f32[4,4,256]{2,1,0:T(4,128)}), f32[4,4,256]{2,1,0:T(4,128)S(1)}, u32[]{:S(2)}, u32[]{:S(2)}) async-start(f32[4,4,256]{2,1,0:T(4,128)} %shard_map.96.copies_ref), calls=%async_computation.2 | async-start | bytes 32768 | tf_op jit(solution)/shard_map/all_to_all | solution.py:284
  69.0 0.1 and_select_fusion.1.off_ref
  69.1 3.4 %shard_map.97 = f32[16,32,128]{2,1,0:T(8,128)} custom-call(bf16[16,2,32,128]{3,2,1,0:T(8,128)(2,1)S(1)} %all-to-all-done.text_ref.refs_0_, f32[2,16,256]{2,1,0:T(8,128)S(1)} %and_select_fusion.off_ref, f32[4,4,256]{2,1,0:T(4,128)} %shard_map.96.copies_ref, bf16[2,512,128]{2,1,0:T(8,128)(2,1)S(1)} %pad_maximum_fusion.1.refs_0_.kv_ref, ...), custom_call_target="tpu_custom_call" | custom-call | tf_op jit(solution)/shard_map/pallas_call | solution.py:286
  72.5 0.0 all-to-all-done.2.norm_ref
  72.5 9.4 %all-to-all-start.3 = ((f32[16,32,128]{2,1,0:T(8,128)}), f32[16,32,128]{2,1,0:T(8,128)S(1)}, u32[]{:S(2)}, u32[]{:S(2)}) async-start(f32[16,32,128]{2,1,0:T(8,128)} %shard_map.97), calls=%async_computation.3 | async-start | bytes 524288 | tf_op jit(solution)/shard_map/all_to_all | solution.py:295
  81.9 0.0 collective-permute-done.3.refs_1_
  81.9 0.0 collective-permute-done.4.refs_2_
  81.9 0.0 collective-permute-done.5.refs_3_
  81.9 6.0 %shard_map.98 = (bf16[1024,256]{1,0:T(8,128)(2,1)S(1)}, bf16[1024,256]{1,0:T(8,128)(2,1)}, bf16[1024,256]{1,0:T(8,128)(2,1)}, bf16[1024,256]{1,0:T(8,128)(2,1)}) custom-call(s32[1]{0:T(128)} %bitcast.near_ref, bf16[2,512,128]{2,1,0:T(8,128)(2,1)S(1)} %pad_maximum_fusion.1.refs_0_.kv_ref, f32[4,2,4,256]{3,2,1,0:T(4,128)S(1)} %and_select_fusion.1.off_ref, ...), custom_call_target="tpu_custom_call" | custom-call | flops 99999997952 | bytes 1048576 | tf_op jit(solution)/shard_map/pallas_call | solution.py:297
  88.0 3.8 %collective-permute-start.6 = (bf16[1024,256]{1,0:T(8,128)(2,1)}, bf16[1024,256]{1,0:T(8,128)(2,1)S(1)}, u32[]{:S(2)}, u32[]{:S(2)}) collective-permute-start(bf16[1024,256]{1,0:T(8,128)(2,1)} %get-tuple-element.25), channel_id=1, source_target_pairs={{0,8},{8,16},{16,24},{24,0},{1,9},{9,17},{17,25},{25,1},{2,10},{10... | collective-permute-start | bytes 1572872 | tf_op jit(solution)/shard_map/ppermute | solution.py:38
  91.7 3.0 %collective-permute-start.7 = (bf16[1024,256]{1,0:T(8,128)(2,1)}, bf16[1024,256]{1,0:T(8,128)(2,1)S(1)}, u32[]{:S(2)}, u32[]{:S(2)}) collective-permute-start(bf16[1024,256]{1,0:T(8,128)(2,1)} %get-tuple-element.26), channel_id=1, source_target_pairs={{0,16},{8,24},{16,0},{24,8},{1,17},{9,25},{17,1},{25,9},{2,18},{10... | collective-permute-start | bytes 1572872 | tf_op jit(solution)/shard_map/ppermute | solution.py:38
  94.7 2.3 %collective-permute-start.8 = (bf16[1024,256]{1,0:T(8,128)(2,1)}, bf16[1024,256]{1,0:T(8,128)(2,1)S(1)}, u32[]{:S(2)}, u32[]{:S(2)}) collective-permute-start(bf16[1024,256]{1,0:T(8,128)(2,1)} %get-tuple-element.27), channel_id=1, source_target_pairs={{0,24},{8,0},{16,8},{24,16},{1,25},{9,1},{17,9},{25,17},{2,26},{10... | collective-permute-start | bytes 1572872 | tf_op jit(solution)/shard_map/ppermute | solution.py:38
  97.0 0.0 all-to-all-done.3.parts_ref
  97.0 0.7 broadcast_in_dim.66
  97.7 12.0 %all-to-all-start.4 = ((bf16[16,4,1024]{2,1,0:T(4,128)(2,1)}), bf16[16,4,1024]{2,1,0:T(4,128)(2,1)S(1)}, u32[]{:S(2)}, u32[]{:S(2)}) async-start(bf16[16,4,1024]{2,1,0:T(4,128)(2,1)} %broadcast_in_dim.66), calls=%async_computation.4 | async-start | bytes 262144 | tf_op jit(solution)/shard_map/all_to_all | solution.py:33
  109.8 0.0 collective-permute-done.6
  109.8 0.4 collective-permute-done.7
  110.2 6.1 %collective-permute-done.8 = bf16[1024,256]{1,0:T(8,128)(2,1)S(1)} collective-permute-done((bf16[1024,256]{1,0:T(8,128)(2,1)}, bf16[1024,256]{1,0:T(8,128)(2,1)S(1)}, u32[]{:S(2)}, u32[]{:S(2)}) %collective-permute-start.8) | collective-permute-done | bytes 524320 | tf_op jit(solution)/shard_map/ppermute | solution.py:38
  116.3 1.1 add_convert_fusion
  117.4 4.8 %all-to-all-done.4 = bf16[16,4,1024]{2,1,0:T(4,128)(2,1)S(1)} async-done(((bf16[16,4,1024]{2,1,0:T(4,128)(2,1)}), bf16[16,4,1024]{2,1,0:T(4,128)(2,1)S(1)}, u32[]{:S(2)}, u32[]{:S(2)}) %all-to-all-start.4) | async-done | bytes 131104 | tf_op jit(solution)/shard_map/all_to_all | solution.py:33
  122.2 6.9 %all-to-all-start.5 = ((bf16[16,64,256]{2,1,0:T(8,128)(2,1)}), bf16[16,64,256]{2,1,0:T(8,128)(2,1)S(1)}, u32[]{:S(2)}, u32[]{:S(2)}) async-start(bf16[16,64,256]{2,1,0:T(8,128)(2,1)} %bitcast.18), calls=%async_computation.5 | async-start | bytes 1048576 | tf_op jit(solution)/shard_map/all_to_all | solution.py:327
  129.1 3.0 %collective-permute-start.10 = (bf16[16,4,1024]{2,1,0:T(4,128)(2,1)S(1)}, bf16[16,4,1024]{2,1,0:T(4,128)(2,1)S(1)}, u32[]{:S(2)}, u32[]{:S(2)}) collective-permute-start(bf16[16,4,1024]{2,1,0:T(4,128)(2,1)S(1)} %all-to-all-done.4), channel_id=1, source_target_pairs={{0,16},{8,24},{16,0},{24,8},{1,17},{9,25},{17,1},{25,9},{2,18},{10... | collective-permute-start | bytes 393224 | tf_op jit(solution)/shard_map/ppermute | solution.py:38
  132.1 2.3 %collective-permute-start.11 = (bf16[16,4,1024]{2,1,0:T(4,128)(2,1)S(1)}, bf16[16,4,1024]{2,1,0:T(4,128)(2,1)S(1)}, u32[]{:S(2)}, u32[]{:S(2)}) collective-permute-start(bf16[16,4,1024]{2,1,0:T(4,128)(2,1)S(1)} %all-to-all-done.4), channel_id=1, source_target_pairs={{0,24},{8,0},{16,8},{24,16},{1,25},{9,1},{17,9},{25,17},{2,26},{10... | collective-permute-start | bytes 393224 | tf_op jit(solution)/shard_map/ppermute | solution.py:38
  134.4 4.7 %collective-permute-start.9 = (bf16[16,4,1024]{2,1,0:T(4,128)(2,1)S(1)}, bf16[16,4,1024]{2,1,0:T(4,128)(2,1)S(1)}, u32[]{:S(2)}, u32[]{:S(2)}) collective-permute-start(bf16[16,4,1024]{2,1,0:T(4,128)(2,1)S(1)} %all-to-all-done.4), channel_id=1, source_target_pairs={{0,8},{8,16},{16,24},{24,0},{1,9},{9,17},{17,25},{25,1},{2,10},{10... | collective-permute-start | bytes 393224 | tf_op jit(solution)/shard_map/ppermute | solution.py:38
  139.2 0.0 collective-permute-done.10
  139.2 1.1 collective-permute-done.11
  140.3 1.4 collective-permute-done.9
  141.7 0.3 select_bitcast_fusion.3
  142.0 0.4 pad_maximum_fusion
  142.4 0.9 reshape.237
  143.3 5.7 %all-to-all-done.5.parts_ref = bf16[16,64,256]{2,1,0:T(8,128)(2,1)S(1)} async-done(((bf16[16,64,256]{2,1,0:T(8,128)(2,1)}), bf16[16,64,256]{2,1,0:T(8,128)(2,1)S(1)}, u32[]{:S(2)}, u32[]{:S(2)}) %all-to-all-start.5) | async-done | bytes 524320 | tf_op jit(solution)/shard_map/all_to_all | solution.py:327
  149.0 0.7 shard_map.100
  (13 shorter events, 0.1 us)
Async XLA Ops:
  3.8 38.1 %collective-permute-start = (bf16[2,512,128]{2,1,0:T(8,128)(2,1)S(1)}, bf16[2,512,128]{2,1,0:T(8,128)(2,1)S(1)}, u32[]{:S(2)}, u32[]{:S(2)}) collective-permute-start(bf16[2,512,128]{2,1,0:T(8,128)(2,1)S(1)} %pad_maximum_fusion.1.refs_0_.kv_ref), channel_id=1, source_target_pairs={{0,8},{8,16},{16,24},{24,0},{1,9},{9,17},{17,25},{25,1},{2,10},{10... | collective-permute-start | bytes 786440 | tf_op jit(solution)/shard_map/ppermute | solution.py:38
  6.2 35.7 %collective-permute-start.1 = (bf16[2,512,128]{2,1,0:T(8,128)(2,1)S(1)}, bf16[2,512,128]{2,1,0:T(8,128)(2,1)S(1)}, u32[]{:S(2)}, u32[]{:S(2)}) collective-permute-start(bf16[2,512,128]{2,1,0:T(8,128)(2,1)S(1)} %pad_maximum_fusion.1.refs_0_.kv_ref), channel_id=1, source_target_pairs={{0,16},{8,24},{16,0},{24,8},{1,17},{9,25},{17,1},{25,9},{2,18},{10... | collective-permute-start | bytes 786440 | tf_op jit(solution)/shard_map/ppermute | solution.py:38
  10.5 31.4 %collective-permute-start.2 = (bf16[2,512,128]{2,1,0:T(8,128)(2,1)S(1)}, bf16[2,512,128]{2,1,0:T(8,128)(2,1)S(1)}, u32[]{:S(2)}, u32[]{:S(2)}) collective-permute-start(bf16[2,512,128]{2,1,0:T(8,128)(2,1)S(1)} %pad_maximum_fusion.1.refs_0_.kv_ref), channel_id=1, source_target_pairs={{0,24},{8,0},{16,8},{24,16},{1,25},{9,1},{17,9},{25,17},{2,26},{10... | collective-permute-start | bytes 786440 | tf_op jit(solution)/shard_map/ppermute | solution.py:38
  12.5 29.4 %all-to-all-start = ((bf16[16,2,32,128]{3,2,1,0:T(8,128)(2,1)}), bf16[16,2,32,128]{3,2,1,0:T(8,128)(2,1)S(1)}, u32[]{:S(2)}, u32[]{:S(2)}) async-start(bf16[16,2,32,128]{3,2,1,0:T(8,128)(2,1)} %broadcast_in_dim.32), calls=%async_computation | async-start | bytes 524288 | tf_op jit(solution)/shard_map/all_to_all | solution.py:235
  44.4 17.5 %all-to-all-start.1 = ((f32[16,6,256]{2,1,0:T(8,128)}), f32[16,6,256]{2,1,0:T(8,128)S(1)}, u32[]{:S(2)}, u32[]{:S(2)}) async-start(f32[16,6,256]{2,1,0:T(8,128)} %shard_map.95), calls=%async_computation.1 | async-start | bytes 262144 | tf_op jit(solution)/shard_map/all_to_all | solution.py:276
  49.2 32.7 %collective-permute-start.3 = (bf16[16,2,32,128]{3,2,1,0:T(8,128)(2,1)S(1)}, bf16[16,2,32,128]{3,2,1,0:T(8,128)(2,1)S(1)}, u32[]{:S(2)}, u32[]{:S(2)}) collective-permute-start(bf16[16,2,32,128]{3,2,1,0:T(8,128)(2,1)S(1)} %all-to-all-done.text_ref.refs_0_), channel_id=1, source_target_pairs={{0,8},{8,16},{16,24},{24,0},{1,9},{9,17},{17,25},{25,1},{2,10},{10... | collective-permute-start | bytes 786440 | tf_op jit(solution)/shard_map/ppermute | solution.py:38
  54.4 27.6 %collective-permute-start.4 = (bf16[16,2,32,128]{3,2,1,0:T(8,128)(2,1)S(1)}, bf16[16,2,32,128]{3,2,1,0:T(8,128)(2,1)S(1)}, u32[]{:S(2)}, u32[]{:S(2)}) collective-permute-start(bf16[16,2,32,128]{3,2,1,0:T(8,128)(2,1)S(1)} %all-to-all-done.text_ref.refs_0_), channel_id=1, source_target_pairs={{0,16},{8,24},{16,0},{24,8},{1,17},{9,25},{17,1},{25,9},{2,18},{10... | collective-permute-start | bytes 786440 | tf_op jit(solution)/shard_map/ppermute | solution.py:38
  56.3 25.6 %collective-permute-start.5 = (bf16[16,2,32,128]{3,2,1,0:T(8,128)(2,1)S(1)}, bf16[16,2,32,128]{3,2,1,0:T(8,128)(2,1)S(1)}, u32[]{:S(2)}, u32[]{:S(2)}) collective-permute-start(bf16[16,2,32,128]{3,2,1,0:T(8,128)(2,1)S(1)} %all-to-all-done.text_ref.refs_0_), channel_id=1, source_target_pairs={{0,24},{8,0},{16,8},{24,16},{1,25},{9,1},{17,9},{25,17},{2,26},{10... | collective-permute-start | bytes 786440 | tf_op jit(solution)/shard_map/ppermute | solution.py:38
  62.5 10.0 %all-to-all-start.2 = ((f32[4,4,256]{2,1,0:T(4,128)}), f32[4,4,256]{2,1,0:T(4,128)S(1)}, u32[]{:S(2)}, u32[]{:S(2)}) async-start(f32[4,4,256]{2,1,0:T(4,128)} %shard_map.96.copies_ref), calls=%async_computation.2 | async-start | bytes 32768 | tf_op jit(solution)/shard_map/all_to_all | solution.py:284
  72.5 24.5 %all-to-all-start.3 = ((f32[16,32,128]{2,1,0:T(8,128)}), f32[16,32,128]{2,1,0:T(8,128)S(1)}, u32[]{:S(2)}, u32[]{:S(2)}) async-start(f32[16,32,128]{2,1,0:T(8,128)} %shard_map.97), calls=%async_computation.3 | async-start | bytes 524288 | tf_op jit(solution)/shard_map/all_to_all | solution.py:295
  88.0 21.8 %collective-permute-start.6 = (bf16[1024,256]{1,0:T(8,128)(2,1)}, bf16[1024,256]{1,0:T(8,128)(2,1)S(1)}, u32[]{:S(2)}, u32[]{:S(2)}) collective-permute-start(bf16[1024,256]{1,0:T(8,128)(2,1)} %get-tuple-element.25), channel_id=1, source_target_pairs={{0,8},{8,16},{16,24},{24,0},{1,9},{9,17},{17,25},{25,1},{2,10},{10... | collective-permute-start | bytes 1572872 | tf_op jit(solution)/shard_map/ppermute | solution.py:38
  91.7 18.5 %collective-permute-start.7 = (bf16[1024,256]{1,0:T(8,128)(2,1)}, bf16[1024,256]{1,0:T(8,128)(2,1)S(1)}, u32[]{:S(2)}, u32[]{:S(2)}) collective-permute-start(bf16[1024,256]{1,0:T(8,128)(2,1)} %get-tuple-element.26), channel_id=1, source_target_pairs={{0,16},{8,24},{16,0},{24,8},{1,17},{9,25},{17,1},{25,9},{2,18},{10... | collective-permute-start | bytes 1572872 | tf_op jit(solution)/shard_map/ppermute | solution.py:38
  94.7 21.6 %collective-permute-start.8 = (bf16[1024,256]{1,0:T(8,128)(2,1)}, bf16[1024,256]{1,0:T(8,128)(2,1)S(1)}, u32[]{:S(2)}, u32[]{:S(2)}) collective-permute-start(bf16[1024,256]{1,0:T(8,128)(2,1)} %get-tuple-element.27), channel_id=1, source_target_pairs={{0,24},{8,0},{16,8},{24,16},{1,25},{9,1},{17,9},{25,17},{2,26},{10... | collective-permute-start | bytes 1572872 | tf_op jit(solution)/shard_map/ppermute | solution.py:38
  97.7 24.5 %all-to-all-start.4 = ((bf16[16,4,1024]{2,1,0:T(4,128)(2,1)}), bf16[16,4,1024]{2,1,0:T(4,128)(2,1)S(1)}, u32[]{:S(2)}, u32[]{:S(2)}) async-start(bf16[16,4,1024]{2,1,0:T(4,128)(2,1)} %broadcast_in_dim.66), calls=%async_computation.4 | async-start | bytes 262144 | tf_op jit(solution)/shard_map/all_to_all | solution.py:33
  122.2 26.7 %all-to-all-start.5 = ((bf16[16,64,256]{2,1,0:T(8,128)(2,1)}), bf16[16,64,256]{2,1,0:T(8,128)(2,1)S(1)}, u32[]{:S(2)}, u32[]{:S(2)}) async-start(bf16[16,64,256]{2,1,0:T(8,128)(2,1)} %bitcast.18), calls=%async_computation.5 | async-start | bytes 1048576 | tf_op jit(solution)/shard_map/all_to_all | solution.py:327
  129.1 10.1 %collective-permute-start.10 = (bf16[16,4,1024]{2,1,0:T(4,128)(2,1)S(1)}, bf16[16,4,1024]{2,1,0:T(4,128)(2,1)S(1)}, u32[]{:S(2)}, u32[]{:S(2)}) collective-permute-start(bf16[16,4,1024]{2,1,0:T(4,128)(2,1)S(1)} %all-to-all-done.4), channel_id=1, source_target_pairs={{0,16},{8,24},{16,0},{24,8},{1,17},{9,25},{17,1},{25,9},{2,18},{10... | collective-permute-start | bytes 393224 | tf_op jit(solution)/shard_map/ppermute | solution.py:38
  132.1 8.2 %collective-permute-start.11 = (bf16[16,4,1024]{2,1,0:T(4,128)(2,1)S(1)}, bf16[16,4,1024]{2,1,0:T(4,128)(2,1)S(1)}, u32[]{:S(2)}, u32[]{:S(2)}) collective-permute-start(bf16[16,4,1024]{2,1,0:T(4,128)(2,1)S(1)} %all-to-all-done.4), channel_id=1, source_target_pairs={{0,24},{8,0},{16,8},{24,16},{1,25},{9,1},{17,9},{25,17},{2,26},{10... | collective-permute-start | bytes 393224 | tf_op jit(solution)/shard_map/ppermute | solution.py:38
  134.4 7.2 %collective-permute-start.9 = (bf16[16,4,1024]{2,1,0:T(4,128)(2,1)S(1)}, bf16[16,4,1024]{2,1,0:T(4,128)(2,1)S(1)}, u32[]{:S(2)}, u32[]{:S(2)}) collective-permute-start(bf16[16,4,1024]{2,1,0:T(4,128)(2,1)S(1)} %all-to-all-done.4), channel_id=1, source_target_pairs={{0,8},{8,16},{16,24},{24,0},{1,9},{9,17},{17,25},{25,1},{2,10},{10... | collective-permute-start | bytes 393224 | tf_op jit(solution)/shard_map/ppermute | solution.py:38

commit v9 on v8

--- a/solution.py
+++ b/solution.py
@@ -8,9 +8,11 @@
 
 HEAD_WIDTH = 128
 FRAME_DEV = 4
-TOK = ("tok_0", "tok_1", "tok_2")
-FAR = ("tok_0", "tok_1")
-NEAR = "tok_2"
+TOK = ("tok_0", "tok_1", "tok_2", "tok_3")
+FAR = ("tok_0", "tok_1", "tok_2")
+NEAR = "tok_3"
+PLANE = ("tok_0", "tok_1")
+LINE = ("tok_2", "tok_3")
 CHUNK = 256
 SCALE = HEAD_WIDTH**-0.5
 LOG2E = 1.4426950408889634
@@ -21,7 +23,7 @@
 NT = (((1,), (1,)), ((), ()))
 NN = (((1,), (0,)), ((), ()))
 PARAMS = pltpu.CompilerParams(vmem_limit_bytes=32 * 2**20)
-LARGE = pltpu.CompilerParams(vmem_limit_bytes=52 * 2**20)
+LARGE = pltpu.CompilerParams(vmem_limit_bytes=49 * 2**20)
 LARGER = pltpu.CompilerParams(vmem_limit_bytes=58 * 2**20)
 HEAVY = pl.CostEstimate(flops=10**11, bytes_accessed=2**20, transcendentals=0)
 WHOLE = pl.BlockSpec(memory_space=pltpu.VMEM)
@@ -140,11 +142,13 @@
 
 def token_kernel(near_ref, kv_ref, off_ref, norm_ref, far_vision_ref, *refs):
     pieces = off_ref.shape[0]
-    text_refs, out_refs = refs[:pieces], refs[pieces : 2 * pieces]
-    p_scr, ds_scr, kv_scr, vision_ref, vision_sem = refs[2 * pieces :]
+    out_count = far_vision_ref.shape[0]
+    text_refs, refs = refs[:pieces], refs[pieces:]
+    out_refs = refs[:out_count]
+    p_scr, ds_scr, kv_scr, vision_ref, vision_sem = refs[out_count:]
     copies = [
         pltpu.make_async_copy(far_vision_ref.at[p], vision_ref.at[p], vision_sem.at[p])
-        for p in range(pieces)
+        for p in range(out_count)
     ]
     for copy in copies:
         copy.start()
@@ -223,6 +227,8 @@
     lines = own_rows * members
     kv_rows = vision_keys.shape[0]
     features = vision.shape[1]
+    plane, line = lax.axis_size(PLANE), lax.axis_size(LINE)
+    line_id = lax.axis_index(LINE).reshape(1).astype(jnp.int32)
     near_id = my_near.reshape(1).astype(jnp.int32)
 
     own_text = jnp.stack(
@@ -256,13 +262,13 @@
     part = features // peers
     turned = pl.pallas_call(
         turn_kernel,
-        out_shape=jax.ShapeDtypeStruct((near, far, part, kv_rows), BF16),
-        grid=(far // 4,),
-        in_specs=[SCALARS, pl.BlockSpec((kv_rows, 4 * near * part), lambda i: (0, i))],
-        out_specs=pl.BlockSpec((near, 4, part, kv_rows), lambda i: (0, i, 0, 0)),
+        out_shape=jax.ShapeDtypeStruct((line, plane, part, kv_rows), BF16),
+        grid=(plane // 4,),
+        in_specs=[SCALARS, pl.BlockSpec((kv_rows, 4 * line * part), lambda i: (0, i))],
+        out_specs=pl.BlockSpec((line, 4, part, kv_rows), lambda i: (0, i, 0, 0)),
         compiler_params=LARGER,
-    )(near_id, vision)
-    turned = turned.reshape(near, far * part, kv_rows)
+    )(line_id, vision)
+    turned = turned.reshape(line, plane * part, kv_rows)
     text, turned = lax.optimization_barrier((text, turned))
 
     stats = pl.pallas_call(
@@ -296,21 +302,21 @@
 
     sums = pl.pallas_call(
         token_kernel,
-        out_shape=[jax.ShapeDtypeStruct((far * part, 2 * HEAD_WIDTH), BF16)] * near,
+        out_shape=[jax.ShapeDtypeStruct((plane * part, 2 * HEAD_WIDTH), BF16)] * line,
         in_specs=[SCALARS] + [WHOLE] * 3 + [pl.BlockSpec(memory_space=pltpu.HBM)] + [WHOLE] * near,
-        out_specs=[WHOLE] * near,
+        out_specs=[WHOLE] * line,
         scratch_shapes=[
             pltpu.VMEM((kv_rows, CHUNK), BF16),
             pltpu.VMEM((kv_rows, CHUNK), BF16),
             pltpu.VMEM((kv_rows, 2 * HEAD_WIDTH), BF16),
-            pltpu.VMEM((near, far * part, kv_rows), BF16),
-            pltpu.SemaphoreType.DMA((near,)),
+            pltpu.VMEM((line, plane * part, kv_rows), BF16),
+            pltpu.SemaphoreType.DMA((line,)),
         ],
         compiler_params=LARGE,
         cost_estimate=HEAVY,
     )(near_id, own_kv, all_off, all_norm, turned, *all_text)
 
-    got = from_ring(sums, NEAR)
+    got = from_ring(sums, LINE)
 
     dq = pl.pallas_call(
         sum_kernel,
@@ -325,7 +331,7 @@
     weights = sum(one.astype(F32) for one in got).astype(BF16)
     weights, dq = lax.optimization_barrier((weights, dq))
     weights = lax.all_to_all(
-        weights.reshape(far, part, 2 * HEAD_WIDTH), FAR, 0, 0, tiled=True
+        weights.reshape(plane, part, 2 * HEAD_WIDTH), PLANE, 0, 0, tiled=True
     )
     all_dq = from_ring([dq] * near, NEAR)
     query_grad = jnp.stack([lax.select_n(base, *all_dq) for base in bases_from(my_near, near)], 1)
@@ -342,7 +348,8 @@
 
 def solution(mesh):
     finer = Mesh(
-        mesh.devices.reshape(2, 8, 4, mesh.shape["head"]), ("tok_0", "tok_1", "tok_2", "head")
+        mesh.devices.reshape(2, 8, 2, 2, mesh.shape["head"]),
+        ("tok_0", "tok_1", "tok_2", "tok_3", "head"),
     )
     return jax.shard_map(
         shards,

time: 151 us -> 161 us (1.066)
  the two profiles are of different devices: /device:TPU:14 before, /device:TPU:18 now
where the time goes in v9:
time: 161 us; the launch traced here: 160 us
  waiting for transfers between devices  66.3 us (41%)
  starting transfers between devices  64 us (40%)
  Pallas kernels  18.7 us (12%)
  other arithmetic  5.21 us (3%)
  local copies, waits for them, and re-layouts  4.92 us (3%)
    ppermute x6, starting transfers between devices, shifted(): lax.ppermute(x, axis, [(i, (i + step) % peers) for i in range(peers)])  20.4 us
    all_to_all x1, waiting for transfers between devices, shards(): stats = lax.all_to_all(stats, FAR, 0, 0, tiled=True)  18.4 us
    ppermute x6, waiting for transfers between devices, shifted(): lax.ppermute(x, axis, [(i, (i + step) % peers) for i in range(peers)])  17.8 us
    all_to_all x1, starting transfers between devices, shards(): text = lax.all_to_all(own_text, FAR, 0, 0, tiled=True)  15.7 us
    all_to_all x1, waiting for transfers between devices, shards(): text = lax.all_to_all(own_text, FAR, 0, 0, tiled=True)  11.4 us
    all_to_all x1, waiting for transfers between devices, shards(): lax.all_to_all(weights.reshape(plane, part, 2 * HEAD_WIDTH), PLANE, 0, 0,...  9.63 us
    all_to_all x1, starting transfers between devices, shards(): lax.all_to_all(weights.reshape(plane, part, 2 * HEAD_WIDTH), PLANE, 0, 0,...  7.97 us
    all_to_all x1, starting transfers between devices, from_everyone(): lax.all_to_all(jnp.broadcast_to(x[None], (peers, *x.shape)), axis, 0, 0,...  6.14 us
  transfers between devices with their start and end apart: 12, of which 7 were waited for; matrix products, arithmetic and copies ran while one was open for 5% of the time, Pallas kernels for 10%

profile of v9, /device:TPU:18, one launch (start us, length us, event | category | flops | bytes accessed | tf_op | source)
XLA Modules:
  0.0 160.0 jit_solution(15788838305982044387)
XLA Ops:
  0.6 0.7 stack_reshape.6
  1.3 0.7 stack_reshape.7
  2.1 0.9 broadcast_in_dim.32
  3.0 15.7 %all-to-all-start = ((bf16[32,2,32,128]{3,2,1,0:T(8,128)(2,1)}), bf16[32,2,32,128]{3,2,1,0:T(8,128)(2,1)S(1)}, u32[]{:S(2)}, u32[]{:S(2)}) async-start(bf16[32,2,32,128]{3,2,1,0:T(8,128)(2,1)} %broadcast_in_dim.32), calls=%async_computation | async-start | bytes 1048576 | tf_op jit(solution)/shard_map/all_to_all | solution.py:241
  18.7 1.0 pad_maximum_fusion.1.refs_0_.kv_ref
  19.7 3.3 %collective-permute-start = (bf16[2,512,128]{2,1,0:T(8,128)(2,1)S(1)}, bf16[2,512,128]{2,1,0:T(8,128)(2,1)S(1)}, u32[]{:S(2)}, u32[]{:S(2)}) collective-permute-start(bf16[2,512,128]{2,1,0:T(8,128)(2,1)S(1)} %pad_maximum_fusion.1.refs_0_.kv_ref), channel_id=1, source_target_pairs={{0,8},{8,0},{1,9},{9,1},{2,10},{10,2},{3,11},{11,3},{4,12},{12,4},... | collective-permute-start | bytes 786440 | tf_op jit(solution)/shard_map/ppermute | solution.py:40
  23.1 0.1 add_multiply_fusion
  23.2 0.1 add_bitcast_fusion
  23.3 0.8 select_reduce_fusion.2
  24.0 0.1 convert_reduce_fusion
  24.1 0.1 iota_add_fusion
  24.2 0.8 slice_bitcast_fusion
  24.9 0.1 select_reduce_fusion.1
  25.1 0.1 add.138
  25.2 5.2 %shard_map.94 = bf16[4,16,64,512]{3,2,1,0:T(8,128)(2,1)} custom-call(s32[1]{0:T(128)} %bitcast.8.near_ref, bf16[512,4096]{1,0:T(8,128)(2,1)} %vision_ref.1), custom_call_target="tpu_custom_call" | custom-call | tf_op jit(solution)/shard_map/pallas_call | solution.py:263
  30.4 0.1 and_select_fusion.off_ref
  30.5 11.4 %all-to-all-done.text_ref.refs_0_ = bf16[32,2,32,128]{3,2,1,0:T(8,128)(2,1)S(1)} async-done(((bf16[32,2,32,128]{3,2,1,0:T(8,128)(2,1)}), bf16[32,2,32,128]{3,2,1,0:T(8,128)(2,1)S(1)}, u32[]{:S(2)}, u32[]{:S(2)}) %all-to-all-start) | async-done | bytes 524320 | tf_op jit(solution)/shard_map/all_to_all | solution.py:241
  41.9 0.0 collective-permute-done.refs_1_
  41.9 2.7 %shard_map.95 = f32[32,12,256]{2,1,0:T(8,128)} custom-call(bf16[32,2,32,128]{3,2,1,0:T(8,128)(2,1)S(1)} %all-to-all-done.text_ref.refs_0_, f32[4,8,256]{2,1,0:T(8,128)S(1)} %and_select_fusion.off_ref, bf16[2,512,128]{2,1,0:T(8,128)(2,1)S(1)} %pad_maximum_fusion.1.refs_0_.kv_ref, bf16[2,512,128]{2,1,0:T(8,128)(2,1)S(1)} %collective-permute-done.refs_1_), custom_call_target="tpu_custom_call" | custom-call | tf_op jit(solution)/shard_map/pallas_call | solution.py:274
  44.6 5.1 %all-to-all-start.1 = ((f32[32,12,256]{2,1,0:T(8,128)}), f32[32,12,256]{2,1,0:T(8,128)S(1)}, u32[]{:S(2)}, u32[]{:S(2)}) async-start(f32[32,12,256]{2,1,0:T(8,128)} %shard_map.95), calls=%async_computation.1 | async-start | bytes 1048576 | tf_op jit(solution)/shard_map/all_to_all | solution.py:282
  49.7 3.5 %collective-permute-start.1 = (bf16[32,2,32,128]{3,2,1,0:T(8,128)(2,1)S(1)}, bf16[32,2,32,128]{3,2,1,0:T(8,128)(2,1)S(1)}, u32[]{:S(2)}, u32[]{:S(2)}) collective-permute-start(bf16[32,2,32,128]{3,2,1,0:T(8,128)(2,1)S(1)} %all-to-all-done.text_ref.refs_0_), channel_id=1, source_target_pairs={{0,8},{8,0},{1,9},{9,1},{2,10},{10,2},{3,11},{11,3},{4,12},{12,4},... | collective-permute-start | bytes 1572872 | tf_op jit(solution)/shard_map/ppermute | solution.py:40
  53.2 18.4 %all-to-all-done.1.stats_ref = f32[32,12,256]{2,1,0:T(8,128)S(1)} async-done(((f32[32,12,256]{2,1,0:T(8,128)}), f32[32,12,256]{2,1,0:T(8,128)S(1)}, u32[]{:S(2)}, u32[]{:S(2)}) %all-to-all-start.1) | async-done | bytes 393248 | tf_op jit(solution)/shard_map/all_to_all | solution.py:282
  71.6 0.7 shard_map.96.copies_ref
  72.3 3.3 %all-to-all-start.2 = ((f32[2,8,256]{2,1,0:T(8,128)}), f32[2,8,256]{2,1,0:T(8,128)S(1)}, u32[]{:S(2)}, u32[]{:S(2)}) async-start(f32[2,8,256]{2,1,0:T(8,128)} %shard_map.96.copies_ref), calls=%async_computation.2 | async-start | bytes 32768 | tf_op jit(solution)/shard_map/all_to_all | solution.py:290
  75.6 0.1 and_select_fusion.1.off_ref
  75.7 3.8 %shard_map.97 = f32[32,32,128]{2,1,0:T(8,128)} custom-call(bf16[32,2,32,128]{3,2,1,0:T(8,128)(2,1)S(1)} %all-to-all-done.text_ref.refs_0_, f32[4,8,256]{2,1,0:T(8,128)S(1)} %and_select_fusion.off_ref, f32[2,8,256]{2,1,0:T(8,128)} %shard_map.96.copies_ref, bf16[2,512,128]{2,1,0:T(8,128)(2,1)S(1)} %pad_maximum_fusion.1.refs_0_.kv_ref, ...), custom_call_target="tpu_custom_call" | custom-call | tf_op jit(solution)/shard_map/pallas_call | solution.py:292
  79.5 0.0 all-to-all-done.2.norm_ref
  79.5 5.3 %all-to-all-start.3 = ((f32[32,32,128]{2,1,0:T(8,128)}), f32[32,32,128]{2,1,0:T(8,128)S(1)}, u32[]{:S(2)}, u32[]{:S(2)}) async-start(f32[32,32,128]{2,1,0:T(8,128)} %shard_map.97), calls=%async_computation.3 | async-start | bytes 1048576 | tf_op jit(solution)/shard_map/all_to_all | solution.py:301
  84.8 0.0 collective-permute-done.1.refs_1_
  84.8 5.6 %shard_map.98 = (bf16[1024,256]{1,0:T(8,128)(2,1)S(1)}, bf16[1024,256]{1,0:T(8,128)(2,1)}, bf16[1024,256]{1,0:T(8,128)(2,1)S(1)}, bf16[1024,256]{1,0:T(8,128)(2,1)S(1)}) custom-call(s32[1]{0:T(128)} %bitcast.near_ref, bf16[2,512,128]{2,1,0:T(8,128)(2,1)S(1)} %pad_maximum_fusion.1.refs_0_.kv_ref, f32[2,4,4,256]{3,2,1,0:T(4,128)S(1)} %and_select_fusion.1.off_ref, ...), custom_call_target="tpu_custom_call" | custom-call | flops 99999997952 | bytes 1048576 | tf_op jit(solution)/shard_map/pallas_call | solution.py:303
  90.4 3.2 %collective-permute-start.2 = (bf16[1024,256]{1,0:T(8,128)(2,1)}, bf16[1024,256]{1,0:T(8,128)(2,1)S(1)}, u32[]{:S(2)}, u32[]{:S(2)}) collective-permute-start(bf16[1024,256]{1,0:T(8,128)(2,1)} %get-tuple-element.25), channel_id=1, source_target_pairs={{0,8},{8,16},{16,24},{24,0},{1,9},{9,17},{17,25},{25,1},{2,10},{10... | collective-permute-start | bytes 1572872 | tf_op jit(solution)/shard_map/ppermute | solution.py:40
  93.6 4.0 %collective-permute-start.3 = (bf16[1024,256]{1,0:T(8,128)(2,1)S(1)}, bf16[1024,256]{1,0:T(8,128)(2,1)}, u32[]{:S(2)}, u32[]{:S(2)}) collective-permute-start(bf16[1024,256]{1,0:T(8,128)(2,1)S(1)} %get-tuple-element.26), channel_id=1, source_target_pairs={{0,16},{8,24},{16,0},{24,8},{1,17},{9,25},{17,1},{25,9},{2,18},{10... | collective-permute-start | bytes 1572872 | tf_op jit(solution)/shard_map/ppermute | solution.py:40
  97.5 4.5 %collective-permute-start.4 = (bf16[1024,256]{1,0:T(8,128)(2,1)S(1)}, bf16[1024,256]{1,0:T(8,128)(2,1)}, u32[]{:S(2)}, u32[]{:S(2)}) collective-permute-start(bf16[1024,256]{1,0:T(8,128)(2,1)S(1)} %get-tuple-element.27), channel_id=1, source_target_pairs={{0,24},{8,0},{16,8},{24,16},{1,25},{9,1},{17,9},{25,17},{2,26},{10... | collective-permute-start | bytes 1572872 | tf_op jit(solution)/shard_map/ppermute | solution.py:40
  102.1 5.8 %all-to-all-done.3.parts_ref = f32[32,32,128]{2,1,0:T(8,128)S(1)} async-done(((f32[32,32,128]{2,1,0:T(8,128)}), f32[32,32,128]{2,1,0:T(8,128)S(1)}, u32[]{:S(2)}, u32[]{:S(2)}) %all-to-all-start.3) | async-done | bytes 524320 | tf_op jit(solution)/shard_map/all_to_all | solution.py:301
  107.9 0.8 broadcast_in_dim.66
  108.7 6.1 %all-to-all-start.4 = ((bf16[32,4,1024]{2,1,0:T(4,128)(2,1)}), bf16[32,4,1024]{2,1,0:T(4,128)(2,1)S(1)}, u32[]{:S(2)}, u32[]{:S(2)}) async-start(bf16[32,4,1024]{2,1,0:T(4,128)(2,1)} %broadcast_in_dim.66), calls=%async_computation.4 | async-start | bytes 524288 | tf_op jit(solution)/shard_map/all_to_all | solution.py:35
  114.8 0.0 collective-permute-done.2
  114.8 0.0 collective-permute-done.3
  114.8 9.9 %collective-permute-done.4 = bf16[1024,256]{1,0:T(8,128)(2,1)} collective-permute-done((bf16[1024,256]{1,0:T(8,128)(2,1)S(1)}, bf16[1024,256]{1,0:T(8,128)(2,1)}, u32[]{:S(2)}, u32[]{:S(2)}) %collective-permute-start.4) | collective-permute-done | bytes 524320 | tf_op jit(solution)/shard_map/ppermute | solution.py:40
  124.8 2.3 %add_convert_fusion = bf16[1024,256]{1,0:T(8,128)(2,1)} fusion(bf16[1024,256]{1,0:T(8,128)(2,1)} %collective-permute-done.4, bf16[1024,256]{1,0:T(8,128)(2,1)} %collective-permute-done.3, bf16[1024,256]{1,0:T(8,128)(2,1)S(1)} %collective-permute-done.2, bf16[1024,256]{1,0:T(8,128)(2,1)S(1)} %get-tuple-element.24), kind=kLoop, calls=%fused_computation | loop fusion | flops 2097152 | bytes 2621440 | tf_op jit(solution)/shard_map/convert_element_type | solution.py:331
  127.0 3.3 %all-to-all-done.4 = bf16[32,4,1024]{2,1,0:T(4,128)(2,1)S(1)} async-done(((bf16[32,4,1024]{2,1,0:T(4,128)(2,1)}), bf16[32,4,1024]{2,1,0:T(4,128)(2,1)S(1)}, u32[]{:S(2)}, u32[]{:S(2)}) %all-to-all-start.4) | async-done | bytes 262176 | tf_op jit(solution)/shard_map/all_to_all | solution.py:35
  130.3 8.0 %all-to-all-start.5 = ((bf16[16,64,256]{2,1,0:T(8,128)(2,1)}), bf16[16,64,256]{2,1,0:T(8,128)(2,1)S(1)}, u32[]{:S(2)}, u32[]{:S(2)}) async-start(bf16[16,64,256]{2,1,0:T(8,128)(2,1)} %bitcast.13), calls=%async_computation.5 | async-start | bytes 1048576 | tf_op jit(solution)/shard_map/all_to_all | solution.py:333
  138.3 2.0 %collective-permute-start.5 = (bf16[32,4,1024]{2,1,0:T(4,128)(2,1)S(1)}, bf16[32,4,1024]{2,1,0:T(4,128)(2,1)S(1)}, u32[]{:S(2)}, u32[]{:S(2)}) collective-permute-start(bf16[32,4,1024]{2,1,0:T(4,128)(2,1)S(1)} %all-to-all-done.4), channel_id=1, source_target_pairs={{0,8},{8,0},{1,9},{9,1},{2,10},{10,2},{3,11},{11,3},{4,12},{12,4},... | collective-permute-start | bytes 786440 | tf_op jit(solution)/shard_map/ppermute | solution.py:40
  140.3 7.8 %collective-permute-done.5 = bf16[32,4,1024]{2,1,0:T(4,128)(2,1)S(1)} collective-permute-done((bf16[32,4,1024]{2,1,0:T(4,128)(2,1)S(1)}, bf16[32,4,1024]{2,1,0:T(4,128)(2,1)S(1)}, u32[]{:S(2)}, u32[]{:S(2)}) %collective-permute-start.5) | collective-permute-done | bytes 262176 | tf_op jit(solution)/shard_map/ppermute | solution.py:40
  148.1 0.2 select_bitcast_fusion.1
  148.4 0.3 pad_maximum_fusion
  148.7 0.9 reshape.209
  149.6 9.6 %all-to-all-done.5.parts_ref = bf16[16,64,256]{2,1,0:T(8,128)(2,1)S(1)} async-done(((bf16[16,64,256]{2,1,0:T(8,128)(2,1)}), bf16[16,64,256]{2,1,0:T(8,128)(2,1)S(1)}, u32[]{:S(2)}, u32[]{:S(2)}) %all-to-all-start.5) | async-done | bytes 524320 | tf_op jit(solution)/shard_map/all_to_all | solution.py:333
  159.3 0.7 shard_map.100
  (12 shorter events, 0.2 us)
Async XLA Ops:
  3.0 38.9 %all-to-all-start = ((bf16[32,2,32,128]{3,2,1,0:T(8,128)(2,1)}), bf16[32,2,32,128]{3,2,1,0:T(8,128)(2,1)S(1)}, u32[]{:S(2)}, u32[]{:S(2)}) async-start(bf16[32,2,32,128]{3,2,1,0:T(8,128)(2,1)} %broadcast_in_dim.32), calls=%async_computation | async-start | bytes 1048576 | tf_op jit(solution)/shard_map/all_to_all | solution.py:241
  19.7 22.2 %collective-permute-start = (bf16[2,512,128]{2,1,0:T(8,128)(2,1)S(1)}, bf16[2,512,128]{2,1,0:T(8,128)(2,1)S(1)}, u32[]{:S(2)}, u32[]{:S(2)}) collective-permute-start(bf16[2,512,128]{2,1,0:T(8,128)(2,1)S(1)} %pad_maximum_fusion.1.refs_0_.kv_ref), channel_id=1, source_target_pairs={{0,8},{8,0},{1,9},{9,1},{2,10},{10,2},{3,11},{11,3},{4,12},{12,4},... | collective-permute-start | bytes 786440 | tf_op jit(solution)/shard_map/ppermute | solution.py:40
  44.6 27.0 %all-to-all-start.1 = ((f32[32,12,256]{2,1,0:T(8,128)}), f32[32,12,256]{2,1,0:T(8,128)S(1)}, u32[]{:S(2)}, u32[]{:S(2)}) async-start(f32[32,12,256]{2,1,0:T(8,128)} %shard_map.95), calls=%async_computation.1 | async-start | bytes 1048576 | tf_op jit(solution)/shard_map/all_to_all | solution.py:282
  49.7 35.1 %collective-permute-start.1 = (bf16[32,2,32,128]{3,2,1,0:T(8,128)(2,1)S(1)}, bf16[32,2,32,128]{3,2,1,0:T(8,128)(2,1)S(1)}, u32[]{:S(2)}, u32[]{:S(2)}) collective-permute-start(bf16[32,2,32,128]{3,2,1,0:T(8,128)(2,1)S(1)} %all-to-all-done.text_ref.refs_0_), channel_id=1, source_target_pairs={{0,8},{8,0},{1,9},{9,1},{2,10},{10,2},{3,11},{11,3},{4,12},{12,4},... | collective-permute-start | bytes 1572872 | tf_op jit(solution)/shard_map/ppermute | solution.py:40
  72.3 7.2 %all-to-all-start.2 = ((f32[2,8,256]{2,1,0:T(8,128)}), f32[2,8,256]{2,1,0:T(8,128)S(1)}, u32[]{:S(2)}, u32[]{:S(2)}) async-start(f32[2,8,256]{2,1,0:T(8,128)} %shard_map.96.copies_ref), calls=%async_computation.2 | async-start | bytes 32768 | tf_op jit(solution)/shard_map/all_to_all | solution.py:290
  79.5 28.3 %all-to-all-start.3 = ((f32[32,32,128]{2,1,0:T(8,128)}), f32[32,32,128]{2,1,0:T(8,128)S(1)}, u32[]{:S(2)}, u32[]{:S(2)}) async-start(f32[32,32,128]{2,1,0:T(8,128)} %shard_map.97), calls=%async_computation.3 | async-start | bytes 1048576 | tf_op jit(solution)/shard_map/all_to_all | solution.py:301
  90.4 24.4 %collective-permute-start.2 = (bf16[1024,256]{1,0:T(8,128)(2,1)}, bf16[1024,256]{1,0:T(8,128)(2,1)S(1)}, u32[]{:S(2)}, u32[]{:S(2)}) collective-permute-start(bf16[1024,256]{1,0:T(8,128)(2,1)} %get-tuple-element.25), channel_id=1, source_target_pairs={{0,8},{8,16},{16,24},{24,0},{1,9},{9,17},{17,25},{25,1},{2,10},{10... | collective-permute-start | bytes 1572872 | tf_op jit(solution)/shard_map/ppermute | solution.py:40
  93.6 21.3 %collective-permute-start.3 = (bf16[1024,256]{1,0:T(8,128)(2,1)S(1)}, bf16[1024,256]{1,0:T(8,128)(2,1)}, u32[]{:S(2)}, u32[]{:S(2)}) collective-permute-start(bf16[1024,256]{1,0:T(8,128)(2,1)S(1)} %get-tuple-element.26), channel_id=1, source_target_pairs={{0,16},{8,24},{16,0},{24,8},{1,17},{9,25},{17,1},{25,9},{2,18},{10... | collective-permute-start | bytes 1572872 | tf_op jit(solution)/shard_map/ppermute | solution.py:40
  97.5 27.2 %collective-permute-start.4 = (bf16[1024,256]{1,0:T(8,128)(2,1)S(1)}, bf16[1024,256]{1,0:T(8,128)(2,1)}, u32[]{:S(2)}, u32[]{:S(2)}) collective-permute-start(bf16[1024,256]{1,0:T(8,128)(2,1)S(1)} %get-tuple-element.27), channel_id=1, source_target_pairs={{0,24},{8,0},{16,8},{24,16},{1,25},{9,1},{17,9},{25,17},{2,26},{10... | collective-permute-start | bytes 1572872 | tf_op jit(solution)/shard_map/ppermute | solution.py:40
  108.7 21.7 %all-to-all-start.4 = ((bf16[32,4,1024]{2,1,0:T(4,128)(2,1)}), bf16[32,4,1024]{2,1,0:T(4,128)(2,1)S(1)}, u32[]{:S(2)}, u32[]{:S(2)}) async-start(bf16[32,4,1024]{2,1,0:T(4,128)(2,1)} %broadcast_in_dim.66), calls=%async_computation.4 | async-start | bytes 524288 | tf_op jit(solution)/shard_map/all_to_all | solution.py:35
  130.3 29.0 %all-to-all-start.5 = ((bf16[16,64,256]{2,1,0:T(8,128)(2,1)}), bf16[16,64,256]{2,1,0:T(8,128)(2,1)S(1)}, u32[]{:S(2)}, u32[]{:S(2)}) async-start(bf16[16,64,256]{2,1,0:T(8,128)(2,1)} %bitcast.13), calls=%async_computation.5 | async-start | bytes 1048576 | tf_op jit(solution)/shard_map/all_to_all | solution.py:333
  138.3 9.8 %collective-permute-start.5 = (bf16[32,4,1024]{2,1,0:T(4,128)(2,1)S(1)}, bf16[32,4,1024]{2,1,0:T(4,128)(2,1)S(1)}, u32[]{:S(2)}, u32[]{:S(2)}) collective-permute-start(bf16[32,4,1024]{2,1,0:T(4,128)(2,1)S(1)} %all-to-all-done.4), channel_id=1, source_target_pairs={{0,8},{8,0},{1,9},{9,1},{2,10},{10,2},{3,11},{11,3},{4,12},{12,4},... | collective-permute-start | bytes 786440 | tf_op jit(solution)/shard_map/ppermute | solution.py:40

commit v10 on v8

--- a/solution.py
+++ b/solution.py
@@ -144,7 +144,7 @@
     p_scr, ds_scr, kv_scr, vision_ref, vision_sem = refs[2 * pieces :]
     copies = [
         pltpu.make_async_copy(far_vision_ref.at[p], vision_ref.at[p], vision_sem.at[p])
-        for p in range(pieces)
+        for p in range(1, pieces)
     ]
     for copy in copies:
         copy.start()
@@ -168,11 +168,16 @@
     kv_scr[:, :HEAD_WIDTH] = (key_sum * SCALE).astype(BF16)
     kv_scr[:, HEAD_WIDTH:] = value_sum.astype(BF16)
     size = 512
-    for p, out_ref in enumerate(out_refs):
-        copies[p].wait()
+    out_refs[0][...] = kv_scr[...]
+    for p, out_ref in list(enumerate(out_refs))[1:]:
+        copies[p - 1].wait()
         for at in range(0, out_ref.shape[0], size):
             block = vision_ref[p, at : at + size]
             out_ref[at : at + size] = dot(block, kv_scr[...], NN).astype(BF16)
+
+
+def own_kernel(vision_ref, kv_ref, out_ref):
+    out_ref[...] = dot(vision_ref[0], kv_ref[...], NN).astype(BF16)
 
 
 def sum_kernel(parts_ref, out_ref):
@@ -296,7 +301,8 @@
 
     sums = pl.pallas_call(
         token_kernel,
-        out_shape=[jax.ShapeDtypeStruct((far * part, 2 * HEAD_WIDTH), BF16)] * near,
+        out_shape=[jax.ShapeDtypeStruct((kv_rows, 2 * HEAD_WIDTH), BF16)]
+        + [jax.ShapeDtypeStruct((far * part, 2 * HEAD_WIDTH), BF16)] * (near - 1),
         in_specs=[SCALARS] + [WHOLE] * 3 + [pl.BlockSpec(memory_space=pltpu.HBM)] + [WHOLE] * near,
         out_specs=[WHOLE] * near,
         scratch_shapes=[
@@ -311,6 +317,17 @@
     )(near_id, own_kv, all_off, all_norm, turned, *all_text)
 
     got = from_ring(sums, NEAR)
+    got[0] = pl.pallas_call(
+        own_kernel,
+        out_shape=jax.ShapeDtypeStruct((far * part, 2 * HEAD_WIDTH), BF16),
+        grid=(1,),
+        in_specs=[
+            pl.BlockSpec((1, far * part, kv_rows), lambda i: (0, 0, 0)),
+            pl.BlockSpec((kv_rows, 2 * HEAD_WIDTH), lambda i: (0, 0)),
+        ],
+        out_specs=pl.BlockSpec((far * part, 2 * HEAD_WIDTH), lambda i: (0, 0)),
+        compiler_params=LARGE,
+    )(turned, sums[0])
 
     dq = pl.pallas_call(
         sum_kernel,

time: 151 us -> 152 us (level)
    all_to_all x1, starting transfers between devices: 6.45 us -> 4.5 us  [shards(): all_norm = lax.all_to_all(norms, NEAR, 0, 0, tiled=True)]
    ppermute x12, waiting for transfers between devices: 9.04 us -> 10.7 us  [shifted(): lax.ppermute(x, axis, [(i, (i + step) % peers) for i in range(peers)])]
    pallas_call x1 -> x2, Pallas kernels: 6 us -> 6.82 us  [the longest x1 5.08 us: shards(): pl.pallas_call(token_kernel, out_shape=[jax.ShapeDtypeStruct((kv_rows, 2...]
  transfers between devices with their start and end apart: 18 -> 18, of which waited for: 8 -> 8; matrix products, arithmetic and copies ran while one was open for 4% -> 4% of each run, Pallas kernels for 10% -> 11%
where the time goes in v10:
time: 152 us; the launch traced here: 151 us
  starting transfers between devices  92.4 us (61%)
  waiting for transfers between devices  29.5 us (19%)
  Pallas kernels  19.3 us (13%)
  local copies, waits for them, and re-layouts  4.7 us (3%)
  other arithmetic  4.2 us (3%)
    ppermute x12, starting transfers between devices, shifted(): lax.ppermute(x, axis, [(i, (i + step) % peers) for i in range(peers)])  38.8 us
    all_to_all x1, starting transfers between devices, shards(): text = lax.all_to_all(own_text, FAR, 0, 0, tiled=True)  14.8 us
    all_to_all x1, starting transfers between devices, from_everyone(): lax.all_to_all(jnp.broadcast_to(x[None], (peers, *x.shape)), axis, 0, 0,...  12 us
    ppermute x12, waiting for transfers between devices, shifted(): lax.ppermute(x, axis, [(i, (i + step) % peers) for i in range(peers)])  10.7 us
    all_to_all x1, starting transfers between devices, shards(): dq = lax.all_to_all(dq, FAR, 0, 0, tiled=True)  9.99 us
    all_to_all x1, starting transfers between devices, shards(): lax.all_to_all(weights.reshape(far, part, 2 * HEAD_WIDTH), FAR, 0, 0, til...  7.18 us
    all_to_all x1, waiting for transfers between devices, shards(): text = lax.all_to_all(own_text, FAR, 0, 0, tiled=True)  6.93 us
    pallas_call x1, Pallas kernels, shards(): pl.pallas_call(turn_kernel, out_shape=jax.ShapeDtypeStruct((near, far, pa...  5.23 us
  transfers between devices with their start and end apart: 18, of which 8 were waited for; matrix products, arithmetic and copies ran while one was open for 4% of the time, Pallas kernels for 11%

profile of v10, /device:TPU:14, one launch (start us, length us, event | category | flops | bytes accessed | tf_op | source)
XLA Modules:
  0.0 151.0 jit_solution(3388492243886068146)
XLA Ops:
  0.6 0.7 stack_reshape.6
  1.3 0.7 stack_reshape.7
  2.1 0.8 broadcast_in_dim.32
  2.8 1.0 pad_maximum_fusion.1.refs_0_.kv_ref
  3.8 2.7 %collective-permute-start.2 = (bf16[2,512,128]{2,1,0:T(8,128)(2,1)S(1)}, bf16[2,512,128]{2,1,0:T(8,128)(2,1)S(1)}, u32[]{:S(2)}, u32[]{:S(2)}) collective-permute-start(bf16[2,512,128]{2,1,0:T(8,128)(2,1)S(1)} %pad_maximum_fusion.1.refs_0_.kv_ref), channel_id=1, source_target_pairs={{0,24},{8,0},{16,8},{24,16},{1,25},{9,1},{17,9},{25,17},{2,26},{10... | collective-permute-start | bytes 786440 | tf_op jit(solution)/shard_map/ppermute | solution.py:38
  6.5 3.0 %collective-permute-start.1 = (bf16[2,512,128]{2,1,0:T(8,128)(2,1)S(1)}, bf16[2,512,128]{2,1,0:T(8,128)(2,1)S(1)}, u32[]{:S(2)}, u32[]{:S(2)}) collective-permute-start(bf16[2,512,128]{2,1,0:T(8,128)(2,1)S(1)} %pad_maximum_fusion.1.refs_0_.kv_ref), channel_id=1, source_target_pairs={{0,16},{8,24},{16,0},{24,8},{1,17},{9,25},{17,1},{25,9},{2,18},{10... | collective-permute-start | bytes 786440 | tf_op jit(solution)/shard_map/ppermute | solution.py:38
  9.6 4.0 %collective-permute-start = (bf16[2,512,128]{2,1,0:T(8,128)(2,1)S(1)}, bf16[2,512,128]{2,1,0:T(8,128)(2,1)S(1)}, u32[]{:S(2)}, u32[]{:S(2)}) collective-permute-start(bf16[2,512,128]{2,1,0:T(8,128)(2,1)S(1)} %pad_maximum_fusion.1.refs_0_.kv_ref), channel_id=1, source_target_pairs={{0,8},{8,16},{16,24},{24,0},{1,9},{9,17},{17,25},{25,1},{2,10},{10... | collective-permute-start | bytes 786440 | tf_op jit(solution)/shard_map/ppermute | solution.py:38
  13.6 14.8 %all-to-all-start = ((bf16[16,2,32,128]{3,2,1,0:T(8,128)(2,1)}), bf16[16,2,32,128]{3,2,1,0:T(8,128)(2,1)S(1)}, u32[]{:S(2)}, u32[]{:S(2)}) async-start(bf16[16,2,32,128]{3,2,1,0:T(8,128)(2,1)} %broadcast_in_dim.32), calls=%async_computation | async-start | bytes 524288 | tf_op jit(solution)/shard_map/all_to_all | solution.py:240
  28.4 0.1 add_multiply_fusion
  28.5 0.8 slice_bitcast_fusion
  29.3 0.1 iota_add_fusion
  29.3 0.1 add_bitcast_fusion
  29.4 0.8 select_reduce_fusion.2
  30.2 0.1 convert_reduce_fusion
  30.3 0.1 select_reduce_fusion.1
  30.4 0.1 add.140
  30.5 5.2 %shard_map.94 = bf16[4,16,64,512]{3,2,1,0:T(8,128)(2,1)} custom-call(s32[1]{0:T(128)} %bitcast.near_ref, bf16[512,4096]{1,0:T(8,128)(2,1)} %vision_ref.1), custom_call_target="tpu_custom_call" | custom-call | tf_op jit(solution)/shard_map/pallas_call | solution.py:262
  35.8 0.1 and_select_fusion.off_ref
  35.8 6.9 %all-to-all-done.text_ref.refs_0_ = bf16[16,2,32,128]{3,2,1,0:T(8,128)(2,1)S(1)} async-done(((bf16[16,2,32,128]{3,2,1,0:T(8,128)(2,1)}), bf16[16,2,32,128]{3,2,1,0:T(8,128)(2,1)S(1)}, u32[]{:S(2)}, u32[]{:S(2)}) %all-to-all-start) | async-done | bytes 262176 | tf_op jit(solution)/shard_map/all_to_all | solution.py:240
  42.8 0.0 collective-permute-done.2.refs_3_
  42.8 0.0 collective-permute-done.1.refs_2_
  42.8 0.0 collective-permute-done.refs_1_
  42.8 2.5 %shard_map.95 = f32[16,6,256]{2,1,0:T(8,128)} custom-call(bf16[16,2,32,128]{3,2,1,0:T(8,128)(2,1)S(1)} %all-to-all-done.text_ref.refs_0_, f32[2,16,256]{2,1,0:T(8,128)S(1)} %and_select_fusion.off_ref, bf16[2,512,128]{2,1,0:T(8,128)(2,1)S(1)} %pad_maximum_fusion.1.refs_0_.kv_ref, bf16[2,512,128]{2,1,0:T(8,128)(2,1)S(1)} %collective-permute-done.refs_1_, ...), custom_call_target="tpu_custom_call" | custom-call | tf_op jit(solution)/shard_map/pallas_call | solution.py:273
  45.2 5.1 %all-to-all-start.1 = ((f32[16,6,256]{2,1,0:T(8,128)}), f32[16,6,256]{2,1,0:T(8,128)S(1)}, u32[]{:S(2)}, u32[]{:S(2)}) async-start(f32[16,6,256]{2,1,0:T(8,128)} %shard_map.95), calls=%async_computation.1 | async-start | bytes 262144 | tf_op jit(solution)/shard_map/all_to_all | solution.py:281
  50.4 2.0 %collective-permute-start.5 = (bf16[16,2,32,128]{3,2,1,0:T(8,128)(2,1)S(1)}, bf16[16,2,32,128]{3,2,1,0:T(8,128)(2,1)S(1)}, u32[]{:S(2)}, u32[]{:S(2)}) collective-permute-start(bf16[16,2,32,128]{3,2,1,0:T(8,128)(2,1)S(1)} %all-to-all-done.text_ref.refs_0_), channel_id=1, source_target_pairs={{0,24},{8,0},{16,8},{24,16},{1,25},{9,1},{17,9},{25,17},{2,26},{10... | collective-permute-start | bytes 786440 | tf_op jit(solution)/shard_map/ppermute | solution.py:38
  52.3 4.2 %collective-permute-start.4 = (bf16[16,2,32,128]{3,2,1,0:T(8,128)(2,1)S(1)}, bf16[16,2,32,128]{3,2,1,0:T(8,128)(2,1)S(1)}, u32[]{:S(2)}, u32[]{:S(2)}) collective-permute-start(bf16[16,2,32,128]{3,2,1,0:T(8,128)(2,1)S(1)} %all-to-all-done.text_ref.refs_0_), channel_id=1, source_target_pairs={{0,16},{8,24},{16,0},{24,8},{1,17},{9,25},{17,1},{25,9},{2,18},{10... | collective-permute-start | bytes 786440 | tf_op jit(solution)/shard_map/ppermute | solution.py:38
  56.5 4.3 %collective-permute-start.3 = (bf16[16,2,32,128]{3,2,1,0:T(8,128)(2,1)S(1)}, bf16[16,2,32,128]{3,2,1,0:T(8,128)(2,1)S(1)}, u32[]{:S(2)}, u32[]{:S(2)}) collective-permute-start(bf16[16,2,32,128]{3,2,1,0:T(8,128)(2,1)S(1)} %all-to-all-done.text_ref.refs_0_), channel_id=1, source_target_pairs={{0,8},{8,16},{16,24},{24,0},{1,9},{9,17},{17,25},{25,1},{2,10},{10... | collective-permute-start | bytes 786440 | tf_op jit(solution)/shard_map/ppermute | solution.py:38
  60.9 2.0 %all-to-all-done.1.stats_ref = f32[16,6,256]{2,1,0:T(8,128)S(1)} async-done(((f32[16,6,256]{2,1,0:T(8,128)}), f32[16,6,256]{2,1,0:T(8,128)S(1)}, u32[]{:S(2)}, u32[]{:S(2)}) %all-to-all-start.1) | async-done | bytes 98336 | tf_op jit(solution)/shard_map/all_to_all | solution.py:281
  63.0 0.7 shard_map.96.copies_ref
  63.7 4.5 %all-to-all-start.2 = ((f32[4,4,256]{2,1,0:T(4,128)}), f32[4,4,256]{2,1,0:T(4,128)S(1)}, u32[]{:S(2)}, u32[]{:S(2)}) async-start(f32[4,4,256]{2,1,0:T(4,128)} %shard_map.96.copies_ref), calls=%async_computation.2 | async-start | bytes 32768 | tf_op jit(solution)/shard_map/all_to_all | solution.py:289
  68.2 0.1 and_select_fusion.1.off_ref
  68.2 3.4 %shard_map.97 = f32[16,32,128]{2,1,0:T(8,128)} custom-call(bf16[16,2,32,128]{3,2,1,0:T(8,128)(2,1)S(1)} %all-to-all-done.text_ref.refs_0_, f32[2,16,256]{2,1,0:T(8,128)S(1)} %and_select_fusion.off_ref, f32[4,4,256]{2,1,0:T(4,128)} %shard_map.96.copies_ref, bf16[2,512,128]{2,1,0:T(8,128)(2,1)S(1)} %pad_maximum_fusion.1.refs_0_.kv_ref, ...), custom_call_target="tpu_custom_call" | custom-call | tf_op jit(solution)/shard_map/pallas_call | solution.py:291
  71.6 0.0 all-to-all-done.2.norm_ref
  71.6 10.0 %all-to-all-start.3 = ((f32[16,32,128]{2,1,0:T(8,128)}), f32[16,32,128]{2,1,0:T(8,128)S(1)}, u32[]{:S(2)}, u32[]{:S(2)}) async-start(f32[16,32,128]{2,1,0:T(8,128)} %shard_map.97), calls=%async_computation.3 | async-start | bytes 524288 | tf_op jit(solution)/shard_map/all_to_all | solution.py:300
  81.6 0.0 collective-permute-done.5.refs_3_
  81.6 0.0 collective-permute-done.4.refs_2_
  81.7 0.0 collective-permute-done.3.refs_1_
  81.7 5.1 %shard_map.98 = (bf16[512,256]{1,0:T(8,128)(2,1)S(1)}, bf16[1024,256]{1,0:T(8,128)(2,1)}, bf16[1024,256]{1,0:T(8,128)(2,1)}, bf16[1024,256]{1,0:T(8,128)(2,1)}) custom-call(s32[1]{0:T(128)} %bitcast.near_ref, bf16[2,512,128]{2,1,0:T(8,128)(2,1)S(1)} %pad_maximum_fusion.1.refs_0_.kv_ref, f32[4,2,4,256]{3,2,1,0:T(4,128)S(1)} %and_select_fusion.1.off_ref, ...), custom_call_target="tpu_custom_call" | custom-call | flops 99999997952 | bytes 1048576 | tf_op jit(solution)/shard_map/pallas_call | solution.py:302
  86.8 0.0 copy-start.1
  86.8 0.0 copy-start
  86.8 1.7 %shard_map.99 = bf16[1024,256]{1,0:T(8,128)(2,1)S(1)} custom-call(bf16[4,1024,512]{2,1,0:T(8,128)(2,1)} %bitcast.33, bf16[512,256]{1,0:T(8,128)(2,1)S(1)} %get-tuple-element.24.kv_ref), custom_call_target="tpu_custom_call" | custom-call | tf_op jit(solution)/shard_map/pallas_call | solution.py:320
  88.5 3.8 %collective-permute-start.6 = (bf16[1024,256]{1,0:T(8,128)(2,1)}, bf16[1024,256]{1,0:T(8,128)(2,1)S(1)}, u32[]{:S(2)}, u32[]{:S(2)}) collective-permute-start(bf16[1024,256]{1,0:T(8,128)(2,1)} %get-tuple-element.25), channel_id=1, source_target_pairs={{0,8},{8,16},{16,24},{24,0},{1,9},{9,17},{17,25},{25,1},{2,10},{10... | collective-permute-start | bytes 1572872 | tf_op jit(solution)/shard_map/ppermute | solution.py:38
  92.3 2.9 %collective-permute-start.7 = (bf16[1024,256]{1,0:T(8,128)(2,1)S(1)}, bf16[1024,256]{1,0:T(8,128)(2,1)S(1)}, u32[]{:S(2)}, u32[]{:S(2)}) collective-permute-start(bf16[1024,256]{1,0:T(8,128)(2,1)S(1)} %copy-done.1), channel_id=1, source_target_pairs={{0,16},{8,24},{16,0},{24,8},{1,17},{9,25},{17,1},{25,9},{2,18},{10... | collective-permute-start | bytes 1572872 | tf_op jit(solution)/shard_map/ppermute | solution.py:38
  95.3 2.3 %collective-permute-start.8 = (bf16[1024,256]{1,0:T(8,128)(2,1)S(1)}, bf16[1024,256]{1,0:T(8,128)(2,1)S(1)}, u32[]{:S(2)}, u32[]{:S(2)}) collective-permute-start(bf16[1024,256]{1,0:T(8,128)(2,1)S(1)} %copy-done), channel_id=1, source_target_pairs={{0,24},{8,0},{16,8},{24,16},{1,25},{9,1},{17,9},{25,17},{2,26},{10... | collective-permute-start | bytes 1572872 | tf_op jit(solution)/shard_map/ppermute | solution.py:38
  97.6 0.0 all-to-all-done.3.parts_ref
  97.6 0.7 broadcast_in_dim.66
  98.3 12.0 %all-to-all-start.4 = ((bf16[16,4,1024]{2,1,0:T(4,128)(2,1)}), bf16[16,4,1024]{2,1,0:T(4,128)(2,1)S(1)}, u32[]{:S(2)}, u32[]{:S(2)}) async-start(bf16[16,4,1024]{2,1,0:T(4,128)(2,1)} %broadcast_in_dim.66), calls=%async_computation.4 | async-start | bytes 262144 | tf_op jit(solution)/shard_map/all_to_all | solution.py:33
  110.4 1.5 %collective-permute-done.6 = bf16[1024,256]{1,0:T(8,128)(2,1)S(1)} collective-permute-done((bf16[1024,256]{1,0:T(8,128)(2,1)}, bf16[1024,256]{1,0:T(8,128)(2,1)S(1)}, u32[]{:S(2)}, u32[]{:S(2)}) %collective-permute-start.6) | collective-permute-done | bytes 524320 | tf_op jit(solution)/shard_map/ppermute | solution.py:38
  111.9 0.0 collective-permute-done.7
  111.9 5.3 %collective-permute-done.8 = bf16[1024,256]{1,0:T(8,128)(2,1)S(1)} collective-permute-done((bf16[1024,256]{1,0:T(8,128)(2,1)S(1)}, bf16[1024,256]{1,0:T(8,128)(2,1)S(1)}, u32[]{:S(2)}, u32[]{:S(2)}) %collective-permute-start.8) | collective-permute-done | bytes 524320 | tf_op jit(solution)/shard_map/ppermute | solution.py:38
  117.2 1.1 add_convert_fusion
  118.3 4.6 %all-to-all-done.4 = bf16[16,4,1024]{2,1,0:T(4,128)(2,1)S(1)} async-done(((bf16[16,4,1024]{2,1,0:T(4,128)(2,1)}), bf16[16,4,1024]{2,1,0:T(4,128)(2,1)S(1)}, u32[]{:S(2)}, u32[]{:S(2)}) %all-to-all-start.4) | async-done | bytes 131104 | tf_op jit(solution)/shard_map/all_to_all | solution.py:33
  122.8 7.2 %all-to-all-start.5 = ((bf16[16,64,256]{2,1,0:T(8,128)(2,1)}), bf16[16,64,256]{2,1,0:T(8,128)(2,1)S(1)}, u32[]{:S(2)}, u32[]{:S(2)}) async-start(bf16[16,64,256]{2,1,0:T(8,128)(2,1)} %bitcast.18), calls=%async_computation.5 | async-start | bytes 1048576 | tf_op jit(solution)/shard_map/all_to_all | solution.py:344
  130.0 1.9 %collective-permute-start.11 = (bf16[16,4,1024]{2,1,0:T(4,128)(2,1)S(1)}, bf16[16,4,1024]{2,1,0:T(4,128)(2,1)S(1)}, u32[]{:S(2)}, u32[]{:S(2)}) collective-permute-start(bf16[16,4,1024]{2,1,0:T(4,128)(2,1)S(1)} %all-to-all-done.4), channel_id=1, source_target_pairs={{0,24},{8,0},{16,8},{24,16},{1,25},{9,1},{17,9},{25,17},{2,26},{10... | collective-permute-start | bytes 393224 | tf_op jit(solution)/shard_map/ppermute | solution.py:38
  132.0 4.0 %collective-permute-start.10 = (bf16[16,4,1024]{2,1,0:T(4,128)(2,1)S(1)}, bf16[16,4,1024]{2,1,0:T(4,128)(2,1)S(1)}, u32[]{:S(2)}, u32[]{:S(2)}) collective-permute-start(bf16[16,4,1024]{2,1,0:T(4,128)(2,1)S(1)} %all-to-all-done.4), channel_id=1, source_target_pairs={{0,16},{8,24},{16,0},{24,8},{1,17},{9,25},{17,1},{25,9},{2,18},{10... | collective-permute-start | bytes 393224 | tf_op jit(solution)/shard_map/ppermute | solution.py:38
  135.9 3.6 %collective-permute-start.9 = (bf16[16,4,1024]{2,1,0:T(4,128)(2,1)S(1)}, bf16[16,4,1024]{2,1,0:T(4,128)(2,1)S(1)}, u32[]{:S(2)}, u32[]{:S(2)}) collective-permute-start(bf16[16,4,1024]{2,1,0:T(4,128)(2,1)S(1)} %all-to-all-done.4), channel_id=1, source_target_pairs={{0,8},{8,16},{16,24},{24,0},{1,9},{9,17},{17,25},{25,1},{2,10},{10... | collective-permute-start | bytes 393224 | tf_op jit(solution)/shard_map/ppermute | solution.py:38
  139.6 1.3 collective-permute-done.11
  140.9 0.0 collective-permute-done.10
  140.9 2.6 %collective-permute-done.9 = bf16[16,4,1024]{2,1,0:T(4,128)(2,1)S(1)} collective-permute-done((bf16[16,4,1024]{2,1,0:T(4,128)(2,1)S(1)}, bf16[16,4,1024]{2,1,0:T(4,128)(2,1)S(1)}, u32[]{:S(2)}, u32[]{:S(2)}) %collective-permute-start.9) | collective-permute-done | bytes 131104 | tf_op jit(solution)/shard_map/ppermute | solution.py:38
  143.5 0.3 select_bitcast_fusion.3
  143.8 0.4 pad_maximum_fusion
  144.2 0.9 reshape.237
  145.1 5.2 %all-to-all-done.5.parts_ref = bf16[16,64,256]{2,1,0:T(8,128)(2,1)S(1)} async-done(((bf16[16,64,256]{2,1,0:T(8,128)(2,1)}), bf16[16,64,256]{2,1,0:T(8,128)(2,1)S(1)}, u32[]{:S(2)}, u32[]{:S(2)}) %all-to-all-start.5) | async-done | bytes 524320 | tf_op jit(solution)/shard_map/all_to_all | solution.py:344
  150.3 0.7 shard_map.101
  (15 shorter events, 0.2 us)
Async XLA Ops:
  3.8 39.0 %collective-permute-start.2 = (bf16[2,512,128]{2,1,0:T(8,128)(2,1)S(1)}, bf16[2,512,128]{2,1,0:T(8,128)(2,1)S(1)}, u32[]{:S(2)}, u32[]{:S(2)}) collective-permute-start(bf16[2,512,128]{2,1,0:T(8,128)(2,1)S(1)} %pad_maximum_fusion.1.refs_0_.kv_ref), channel_id=1, source_target_pairs={{0,24},{8,0},{16,8},{24,16},{1,25},{9,1},{17,9},{25,17},{2,26},{10... | collective-permute-start | bytes 786440 | tf_op jit(solution)/shard_map/ppermute | solution.py:38
  6.5 36.2 %collective-permute-start.1 = (bf16[2,512,128]{2,1,0:T(8,128)(2,1)S(1)}, bf16[2,512,128]{2,1,0:T(8,128)(2,1)S(1)}, u32[]{:S(2)}, u32[]{:S(2)}) collective-permute-start(bf16[2,512,128]{2,1,0:T(8,128)(2,1)S(1)} %pad_maximum_fusion.1.refs_0_.kv_ref), channel_id=1, source_target_pairs={{0,16},{8,24},{16,0},{24,8},{1,17},{9,25},{17,1},{25,9},{2,18},{10... | collective-permute-start | bytes 786440 | tf_op jit(solution)/shard_map/ppermute | solution.py:38
  9.6 33.2 %collective-permute-start = (bf16[2,512,128]{2,1,0:T(8,128)(2,1)S(1)}, bf16[2,512,128]{2,1,0:T(8,128)(2,1)S(1)}, u32[]{:S(2)}, u32[]{:S(2)}) collective-permute-start(bf16[2,512,128]{2,1,0:T(8,128)(2,1)S(1)} %pad_maximum_fusion.1.refs_0_.kv_ref), channel_id=1, source_target_pairs={{0,8},{8,16},{16,24},{24,0},{1,9},{9,17},{17,25},{25,1},{2,10},{10... | collective-permute-start | bytes 786440 | tf_op jit(solution)/shard_map/ppermute | solution.py:38
  13.6 29.2 %all-to-all-start = ((bf16[16,2,32,128]{3,2,1,0:T(8,128)(2,1)}), bf16[16,2,32,128]{3,2,1,0:T(8,128)(2,1)S(1)}, u32[]{:S(2)}, u32[]{:S(2)}) async-start(bf16[16,2,32,128]{3,2,1,0:T(8,128)(2,1)} %broadcast_in_dim.32), calls=%async_computation | async-start | bytes 524288 | tf_op jit(solution)/shard_map/all_to_all | solution.py:240
  45.2 17.7 %all-to-all-start.1 = ((f32[16,6,256]{2,1,0:T(8,128)}), f32[16,6,256]{2,1,0:T(8,128)S(1)}, u32[]{:S(2)}, u32[]{:S(2)}) async-start(f32[16,6,256]{2,1,0:T(8,128)} %shard_map.95), calls=%async_computation.1 | async-start | bytes 262144 | tf_op jit(solution)/shard_map/all_to_all | solution.py:281
  50.4 31.3 %collective-permute-start.5 = (bf16[16,2,32,128]{3,2,1,0:T(8,128)(2,1)S(1)}, bf16[16,2,32,128]{3,2,1,0:T(8,128)(2,1)S(1)}, u32[]{:S(2)}, u32[]{:S(2)}) collective-permute-start(bf16[16,2,32,128]{3,2,1,0:T(8,128)(2,1)S(1)} %all-to-all-done.text_ref.refs_0_), channel_id=1, source_target_pairs={{0,24},{8,0},{16,8},{24,16},{1,25},{9,1},{17,9},{25,17},{2,26},{10... | collective-permute-start | bytes 786440 | tf_op jit(solution)/shard_map/ppermute | solution.py:38
  52.3 29.3 %collective-permute-start.4 = (bf16[16,2,32,128]{3,2,1,0:T(8,128)(2,1)S(1)}, bf16[16,2,32,128]{3,2,1,0:T(8,128)(2,1)S(1)}, u32[]{:S(2)}, u32[]{:S(2)}) collective-permute-start(bf16[16,2,32,128]{3,2,1,0:T(8,128)(2,1)S(1)} %all-to-all-done.text_ref.refs_0_), channel_id=1, source_target_pairs={{0,16},{8,24},{16,0},{24,8},{1,17},{9,25},{17,1},{25,9},{2,18},{10... | collective-permute-start | bytes 786440 | tf_op jit(solution)/shard_map/ppermute | solution.py:38
  56.5 25.1 %collective-permute-start.3 = (bf16[16,2,32,128]{3,2,1,0:T(8,128)(2,1)S(1)}, bf16[16,2,32,128]{3,2,1,0:T(8,128)(2,1)S(1)}, u32[]{:S(2)}, u32[]{:S(2)}) collective-permute-start(bf16[16,2,32,128]{3,2,1,0:T(8,128)(2,1)S(1)} %all-to-all-done.text_ref.refs_0_), channel_id=1, source_target_pairs={{0,8},{8,16},{16,24},{24,0},{1,9},{9,17},{17,25},{25,1},{2,10},{10... | collective-permute-start | bytes 786440 | tf_op jit(solution)/shard_map/ppermute | solution.py:38
  63.7 8.0 %all-to-all-start.2 = ((f32[4,4,256]{2,1,0:T(4,128)}), f32[4,4,256]{2,1,0:T(4,128)S(1)}, u32[]{:S(2)}, u32[]{:S(2)}) async-start(f32[4,4,256]{2,1,0:T(4,128)} %shard_map.96.copies_ref), calls=%async_computation.2 | async-start | bytes 32768 | tf_op jit(solution)/shard_map/all_to_all | solution.py:289
  71.6 26.0 %all-to-all-start.3 = ((f32[16,32,128]{2,1,0:T(8,128)}), f32[16,32,128]{2,1,0:T(8,128)S(1)}, u32[]{:S(2)}, u32[]{:S(2)}) async-start(f32[16,32,128]{2,1,0:T(8,128)} %shard_map.97), calls=%async_computation.3 | async-start | bytes 524288 | tf_op jit(solution)/shard_map/all_to_all | solution.py:300
  86.8 5.6 %copy-start.1 = (bf16[1024,256]{1,0:T(8,128)(2,1)S(1)}, bf16[1024,256]{1,0:T(8,128)(2,1)}, u32[]{:S(2)}) copy-start(bf16[1024,256]{1,0:T(8,128)(2,1)} %get-tuple-element.26) | copy-start | bytes 1572868
  86.8 8.5 %copy-start = (bf16[1024,256]{1,0:T(8,128)(2,1)S(1)}, bf16[1024,256]{1,0:T(8,128)(2,1)}, u32[]{:S(2)}) copy-start(bf16[1024,256]{1,0:T(8,128)(2,1)} %get-tuple-element.27) | copy-start | bytes 1572868
  88.5 23.4 %collective-permute-start.6 = (bf16[1024,256]{1,0:T(8,128)(2,1)}, bf16[1024,256]{1,0:T(8,128)(2,1)S(1)}, u32[]{:S(2)}, u32[]{:S(2)}) collective-permute-start(bf16[1024,256]{1,0:T(8,128)(2,1)} %get-tuple-element.25), channel_id=1, source_target_pairs={{0,8},{8,16},{16,24},{24,0},{1,9},{9,17},{17,25},{25,1},{2,10},{10... | collective-permute-start | bytes 1572872 | tf_op jit(solution)/shard_map/ppermute | solution.py:38
  92.3 19.6 %collective-permute-start.7 = (bf16[1024,256]{1,0:T(8,128)(2,1)S(1)}, bf16[1024,256]{1,0:T(8,128)(2,1)S(1)}, u32[]{:S(2)}, u32[]{:S(2)}) collective-permute-start(bf16[1024,256]{1,0:T(8,128)(2,1)S(1)} %copy-done.1), channel_id=1, source_target_pairs={{0,16},{8,24},{16,0},{24,8},{1,17},{9,25},{17,1},{25,9},{2,18},{10... | collective-permute-start | bytes 1572872 | tf_op jit(solution)/shard_map/ppermute | solution.py:38
  95.3 21.9 %collective-permute-start.8 = (bf16[1024,256]{1,0:T(8,128)(2,1)S(1)}, bf16[1024,256]{1,0:T(8,128)(2,1)S(1)}, u32[]{:S(2)}, u32[]{:S(2)}) collective-permute-start(bf16[1024,256]{1,0:T(8,128)(2,1)S(1)} %copy-done), channel_id=1, source_target_pairs={{0,24},{8,0},{16,8},{24,16},{1,25},{9,1},{17,9},{25,17},{2,26},{10... | collective-permute-start | bytes 1572872 | tf_op jit(solution)/shard_map/ppermute | solution.py:38
  98.3 24.5 %all-to-all-start.4 = ((bf16[16,4,1024]{2,1,0:T(4,128)(2,1)}), bf16[16,4,1024]{2,1,0:T(4,128)(2,1)S(1)}, u32[]{:S(2)}, u32[]{:S(2)}) async-start(bf16[16,4,1024]{2,1,0:T(4,128)(2,1)} %broadcast_in_dim.66), calls=%async_computation.4 | async-start | bytes 262144 | tf_op jit(solution)/shard_map/all_to_all | solution.py:33
  122.8 27.5 %all-to-all-start.5 = ((bf16[16,64,256]{2,1,0:T(8,128)(2,1)}), bf16[16,64,256]{2,1,0:T(8,128)(2,1)S(1)}, u32[]{:S(2)}, u32[]{:S(2)}) async-start(bf16[16,64,256]{2,1,0:T(8,128)(2,1)} %bitcast.18), calls=%async_computation.5 | async-start | bytes 1048576 | tf_op jit(solution)/shard_map/all_to_all | solution.py:344
  130.0 10.9 %collective-permute-start.11 = (bf16[16,4,1024]{2,1,0:T(4,128)(2,1)S(1)}, bf16[16,4,1024]{2,1,0:T(4,128)(2,1)S(1)}, u32[]{:S(2)}, u32[]{:S(2)}) collective-permute-start(bf16[16,4,1024]{2,1,0:T(4,128)(2,1)S(1)} %all-to-all-done.4), channel_id=1, source_target_pairs={{0,24},{8,0},{16,8},{24,16},{1,25},{9,1},{17,9},{25,17},{2,26},{10... | collective-permute-start | bytes 393224 | tf_op jit(solution)/shard_map/ppermute | solution.py:38
  132.0 9.0 %collective-permute-start.10 = (bf16[16,4,1024]{2,1,0:T(4,128)(2,1)S(1)}, bf16[16,4,1024]{2,1,0:T(4,128)(2,1)S(1)}, u32[]{:S(2)}, u32[]{:S(2)}) collective-permute-start(bf16[16,4,1024]{2,1,0:T(4,128)(2,1)S(1)} %all-to-all-done.4), channel_id=1, source_target_pairs={{0,16},{8,24},{16,0},{24,8},{1,17},{9,25},{17,1},{25,9},{2,18},{10... | collective-permute-start | bytes 393224 | tf_op jit(solution)/shard_map/ppermute | solution.py:38
  135.9 7.6 %collective-permute-start.9 = (bf16[16,4,1024]{2,1,0:T(4,128)(2,1)S(1)}, bf16[16,4,1024]{2,1,0:T(4,128)(2,1)S(1)}, u32[]{:S(2)}, u32[]{:S(2)}) collective-permute-start(bf16[16,4,1024]{2,1,0:T(4,128)(2,1)S(1)} %all-to-all-done.4), channel_id=1, source_target_pairs={{0,8},{8,16},{16,24},{24,0},{1,9},{9,17},{17,25},{25,1},{2,10},{10... | collective-permute-start | bytes 393224 | tf_op jit(solution)/shard_map/ppermute | solution.py:38
